TPU v7x, 32 devices: a whole 2x2x4 slice. The times are simulated.
32 devices in a mesh: section: 8 (over z, core), expert: 4 (over y, x).
Axes of the slice: x: 2, y: 2, z: 4, core: 2. Of those that a mesh axis runs over, the one named last changes fastest.
Arguments:
- residual: float32 [8, 512, 2048], P('section', 'expert')
- norm_gain: float32 [8, 2048], P('section'), may hold values from 0.1 to 1.9
- w_gate: bfloat16 [8, 4, 2048, 768], P('section', 'expert'), may hold values from -0.125 to 0.125
- w_up: bfloat16 [8, 4, 2048, 768], P('section', 'expert'), may hold values from -0.125 to 0.125
- w_down: bfloat16 [8, 4, 768, 2048], P('section', 'expert'), may hold values from -0.21875 to 0.21875
- route_ids: int32 [3, 8, 512, 2], P(None, 'section', 'expert'), may hold values from 0 to 3, as said below
- route_slots: int32 [3, 8, 512, 2], P(None, 'section', 'expert'), may hold values from 0 to 127, as said below
- combine_weights: float32 [3, 8, 512, 2], P(None, 'section', 'expert'), may hold values from 0.2 to 1
Outputs:
- residual_out: float32 [8, 512, 2048], P('section', 'expert')
Inputs may be any that keep to these rules, and one draw needn't show every extreme that they name: `route_ids`: each token names 2 different experts. Split the rows of one index of expert (128 tokens) into two halves of 64 tokens in order: in each half no expert is named more than 128 // 2 times, and at every step and section one expert is named exactly 128 // 2 times in every half of every index of expert. `route_slots`: the slot of (token t, choice k) is the number of earlier (token, choice) pairs, tokens in order then choices, in the same half of the same index of expert that name the same expert, plus 128 // 2 in the second half; so a slot of one source and expert is used at most once.
All inputs are finite; a program needn't handle non-finite values.
Results may differ from a plain program's by a relative error of at most 0.0033.
Values may be sent and summed in bfloat16 or wider, within the bound.
No kernel may reach another device: no remote copies, remote signals or barrier semaphores. Data moves between devices by JAX's collectives and lax.ppermute only.
A program may use at most 64 MiB of HBM per device.

v0:
```python
import jax
import jax.numpy as jnp
from jax import lax
from jax.sharding import PartitionSpec as P

TOP = 2
STEPS = 3


def shifted(x, axis, by):
    count = lax.axis_size(axis)
    return lax.ppermute(x, axis, [(i, (i + by) % count) for i in range(count)])


def expert_ffn(rows_in, gate_mat, up_mat, down_mat):
    gate_part = jnp.dot(rows_in, gate_mat, preferred_element_type=jnp.float32)
    upward = jnp.dot(rows_in, up_mat, preferred_element_type=jnp.float32)
    hidden = (jax.nn.silu(gate_part) * upward).astype(jnp.bfloat16)
    return jnp.dot(hidden, down_mat, preferred_element_type=jnp.float32).astype(jnp.bfloat16)


def rms_normed(current, gain_row):
    inv_rms = lax.rsqrt(jnp.mean(current * current, axis=-1, keepdims=True) + 1e-06)
    return (current * inv_rms * gain_row).astype(jnp.bfloat16)


def layer_block(
    token_rows, gain_row, chosen, slot_rows, weights_in, experts, cap_part, offset, dispatcher
):
    normed = rms_normed(token_rows, gain_row)
    flat_place = chosen * cap_part + (slot_rows - offset)
    place_iota = jnp.arange(experts * cap_part, dtype=jnp.int32)
    tables = [
        (flat_place[:, k : k + 1] == place_iota[None, :]).astype(jnp.bfloat16) for k in range(TOP)
    ]
    occupied = tables[0]
    k = 1
    occupied = occupied + tables[k]
    send = lax.dot_general(
        occupied, normed, (((0,), (0,)), ((), ())), preferred_element_type=jnp.float32
    )
    send = send.astype(jnp.bfloat16).reshape(experts, cap_part, normed.shape[1])
    returned = dispatcher(send).reshape(experts * cap_part, normed.shape[1])
    combined = jnp.zeros(token_rows.shape, jnp.float32)
    for k in range(TOP):
        picked = jnp.dot(tables[k], returned, preferred_element_type=jnp.float32)
        combined = combined + weights_in[:, k : k + 1] * picked
    return token_rows + combined


def per_device(residual, norm_gain, w_gate, w_up, w_down, route_ids, route_slots, combine_weights):
    experts = lax.axis_size("expert")
    tok_rows = residual.shape[1]
    capacity = 4 * tok_rows // experts
    gain_row = norm_gain[0]
    gate_mat = w_gate[0, 0]
    up_mat = w_up[0, 0]
    down_mat = w_down[0, 0]

    def run_expert(received):
        count = received.shape[0] * received.shape[1]
        result = expert_ffn(received.reshape(count, received.shape[2]), gate_mat, up_mat, down_mat)
        return result.reshape(received.shape)

    def whole_fn(received):
        return lax.all_to_all(
            run_expert(received), "expert", split_axis=0, concat_axis=0, tiled=True
        )

    def dispatch_whole(send):
        return whole_fn(lax.all_to_all(send, "expert", split_axis=0, concat_axis=0, tiled=True))

    current = residual[0]
    for step_index in range(STEPS):
        current = layer_block(
            current,
            gain_row,
            route_ids[step_index, 0],
            route_slots[step_index, 0],
            combine_weights[step_index, 0],
            experts,
            capacity,
            0,
            dispatch_whole,
        )
        current = shifted(current, "section", 1)
    return current[None]


def solution(mesh):
    in_specs = (
        P("section", "expert", None),
        P("section", None),
        P("section", "expert", None, None),
        P("section", "expert", None, None),
        P("section", "expert", None, None),
        P(None, "section", "expert", None),
        P(None, "section", "expert", None),
        P(None, "section", "expert", None),
    )
    out_specs = P("section", "expert", None)
    return jax.shard_map(
        per_device, mesh=mesh, in_specs=in_specs, out_specs=out_specs, check_vma=False
    )
```

profile of v0, /device:TPU:0, one launch (start us, length us, event | category | flops | bytes accessed | tf_op | source)
XLA Modules:
  0.0 272.0 jit_solution(13276970950537671804)
XLA Ops:
  0.0 1.5 fusion.39
  2.3 2.1 convolution_convert_fusion.2
  4.4 30.6 %all_to_all.30 = bf16[4,128,2048]{2,1,0:T(8,128)(2,1)S(1)} all-to-all(bf16[4,128,2048]{2,1,0:T(8,128)(2,1)S(1)} %bitcast.112), channel_id=1, replica_groups=mesh['section'=8,'expert'=4] {'expert'}, dimensions={0} | all-to-all | bytes 4194304 | tf_op jit(solution)/shard_map/all_to_all | solution.py:71
  35.0 1.3 copy-done.6
  36.3 3.0 %fusion.16 = f32[512,768]{1,0:T(8,128)} fusion(bf16[512,2048]{1,0:T(8,128)(2,1)S(1)} %bitcast.118, bf16[1,1,2048,768]{3,2,1,0:T(8,128)(2,1)S(1)} %copy-done.11), kind=kOutput, calls=%fused_computation.16 | convolution fusion | flops 1610612736 | bytes 6815744 | tf_op jit(solution)/shard_map/dot_general | solution.py:16
  39.3 8.3 %fusion.18 = bf16[512,2048]{1,0:T(8,128)(2,1)} fusion(bf16[1,1,768,2048]{3,2,1,0:T(8,128)(2,1)S(1)} %copy-done, f32[512,768]{1,0:T(8,128)} %fusion.16, bf16[512,2048]{1,0:T(8,128)(2,1)} %bitcast.119, bf16[1,1,2048,768]{3,2,1,0:T(8,128)(2,1)} %param.11), kind=kOutput, calls=%fused_computation.21 | convolution fusion | flops 3224633344 | bytes 12058624 | tf_op jit(solution)/shard_map/dot_general | solution.py:19
  47.5 4.6 %all-to-all-start.1 = ((bf16[4,128,2048]{2,1,0:T(8,128)(2,1)}), bf16[4,128,2048]{2,1,0:T(8,128)(2,1)}, u32[]{:S(2)}, u32[]{:S(2)}) async-start(bf16[4,128,2048]{2,1,0:T(8,128)(2,1)} %bitcast.115), calls=%async_computation.1 | async-start | bytes 4194304 | tf_op jit(solution)/shard_map/all_to_all | solution.py:66
  52.2 23.6 %all-to-all-done.1 = bf16[4,128,2048]{2,1,0:T(8,128)(2,1)} async-done(((bf16[4,128,2048]{2,1,0:T(8,128)(2,1)}), bf16[4,128,2048]{2,1,0:T(8,128)(2,1)}, u32[]{:S(2)}, u32[]{:S(2)}) %all-to-all-start.1) | async-done | bytes 2097184 | tf_op jit(solution)/shard_map/all_to_all | solution.py:66
  75.8 2.2 convolution_multiply_fusion.5
  78.0 2.1 fusion.32
  80.2 16.0 %collective-permute-done = f32[128,2048]{1,0:T(8,128)S(1)} collective-permute-done((f32[128,2048]{1,0:T(8,128)S(1)}, f32[128,2048]{1,0:T(8,128)S(1)}, u32[]{:S(2)}, u32[]{:S(2)}) %collective-permute-start) | collective-permute-done | bytes 1048608 | tf_op jit(solution)/shard_map/ppermute | solution.py:12
  96.3 0.8 convolution_convert_fusion.1
  97.2 26.0 %all_to_all.31 = bf16[4,128,2048]{2,1,0:T(8,128)(2,1)S(1)} all-to-all(bf16[4,128,2048]{2,1,0:T(8,128)(2,1)S(1)} %bitcast.113), channel_id=1, replica_groups=mesh['section'=8,'expert'=4] {'expert'}, dimensions={0} | all-to-all | bytes 4194304 | tf_op jit(solution)/shard_map/all_to_all | solution.py:71
  123.2 1.3 copy-done.7
  124.5 3.0 %fusion.14 = f32[512,768]{1,0:T(8,128)} fusion(bf16[512,2048]{1,0:T(8,128)(2,1)S(1)} %bitcast.120, bf16[1,1,2048,768]{3,2,1,0:T(8,128)(2,1)S(1)} %copy-done.12), kind=kOutput, calls=%fused_computation.14 | convolution fusion | flops 1610612736 | bytes 6815744 | tf_op jit(solution)/shard_map/dot_general | solution.py:16
  127.5 8.3 %fusion.21 = bf16[512,2048]{1,0:T(8,128)(2,1)} fusion(bf16[1,1,768,2048]{3,2,1,0:T(8,128)(2,1)S(1)} %copy-done, f32[512,768]{1,0:T(8,128)} %fusion.14, bf16[512,2048]{1,0:T(8,128)(2,1)} %bitcast.121, bf16[1,1,2048,768]{3,2,1,0:T(8,128)(2,1)} %param.11), kind=kOutput, calls=%fused_computation.22 | convolution fusion | flops 3224633344 | bytes 12058624 | tf_op jit(solution)/shard_map/dot_general | solution.py:19
  135.7 4.4 %all-to-all-start.3 = ((bf16[4,128,2048]{2,1,0:T(8,128)(2,1)}), bf16[4,128,2048]{2,1,0:T(8,128)(2,1)}, u32[]{:S(2)}, u32[]{:S(2)}) async-start(bf16[4,128,2048]{2,1,0:T(8,128)(2,1)} %bitcast.117), calls=%async_computation.3 | async-start | bytes 4194304 | tf_op jit(solution)/shard_map/all_to_all | solution.py:66
  140.2 21.4 %all-to-all-done.3 = bf16[4,128,2048]{2,1,0:T(8,128)(2,1)} async-done(((bf16[4,128,2048]{2,1,0:T(8,128)(2,1)}), bf16[4,128,2048]{2,1,0:T(8,128)(2,1)}, u32[]{:S(2)}, u32[]{:S(2)}) %all-to-all-start.3) | async-done | bytes 2097184 | tf_op jit(solution)/shard_map/all_to_all | solution.py:66
  161.6 2.2 convolution_multiply_fusion.3
  163.8 2.1 fusion.30
  166.0 16.0 %collective-permute-done.1 = f32[128,2048]{1,0:T(8,128)S(1)} collective-permute-done((f32[128,2048]{1,0:T(8,128)S(1)}, f32[128,2048]{1,0:T(8,128)S(1)}, u32[]{:S(2)}, u32[]{:S(2)}) %collective-permute-start.1) | collective-permute-done | bytes 1048608 | tf_op jit(solution)/shard_map/ppermute | solution.py:12
  182.2 0.8 convolution_convert_fusion
  183.0 27.6 %all_to_all.32 = bf16[4,128,2048]{2,1,0:T(8,128)(2,1)S(1)} all-to-all(bf16[4,128,2048]{2,1,0:T(8,128)(2,1)S(1)} %bitcast.114), channel_id=1, replica_groups=mesh['section'=8,'expert'=4] {'expert'}, dimensions={0} | all-to-all | bytes 4194304 | tf_op jit(solution)/shard_map/all_to_all | solution.py:71
  210.6 1.3 copy-done.8
  211.9 3.0 %fusion.12 = f32[512,768]{1,0:T(8,128)} fusion(bf16[512,2048]{1,0:T(8,128)(2,1)S(1)} %bitcast.122, bf16[1,1,2048,768]{3,2,1,0:T(8,128)(2,1)S(1)} %copy-done.13), kind=kOutput, calls=%fused_computation.12 | convolution fusion | flops 1610612736 | bytes 6815744 | tf_op jit(solution)/shard_map/dot_general | solution.py:16
  214.9 8.3 %fusion.24 = bf16[512,2048]{1,0:T(8,128)(2,1)} fusion(bf16[1,1,768,2048]{3,2,1,0:T(8,128)(2,1)S(1)} %copy-done, f32[512,768]{1,0:T(8,128)} %fusion.12, bf16[512,2048]{1,0:T(8,128)(2,1)} %bitcast.123, bf16[1,1,2048,768]{3,2,1,0:T(8,128)(2,1)} %param.11), kind=kOutput, calls=%fused_computation.23 | convolution fusion | flops 3224633344 | bytes 12058624 | tf_op jit(solution)/shard_map/dot_general | solution.py:19
  223.2 4.4 %all-to-all-start.5 = ((bf16[4,128,2048]{2,1,0:T(8,128)(2,1)}), bf16[4,128,2048]{2,1,0:T(8,128)(2,1)}, u32[]{:S(2)}, u32[]{:S(2)}) async-start(bf16[4,128,2048]{2,1,0:T(8,128)(2,1)} %bitcast.116), calls=%async_computation.5 | async-start | bytes 4194304 | tf_op jit(solution)/shard_map/all_to_all | solution.py:66
  227.6 23.0 %all-to-all-done.5 = bf16[4,128,2048]{2,1,0:T(8,128)(2,1)} async-done(((bf16[4,128,2048]{2,1,0:T(8,128)(2,1)}), bf16[4,128,2048]{2,1,0:T(8,128)(2,1)}, u32[]{:S(2)}, u32[]{:S(2)}) %all-to-all-start.5) | async-done | bytes 2097184 | tf_op jit(solution)/shard_map/all_to_all | solution.py:66
  250.6 2.2 convolution_multiply_fusion.1
  252.8 2.1 fusion.28
  255.0 16.0 %collective-permute-done.2 = f32[128,2048]{1,0:T(8,128)S(1)} collective-permute-done((f32[128,2048]{1,0:T(8,128)S(1)}, f32[128,2048]{1,0:T(8,128)S(1)}, u32[]{:S(2)}, u32[]{:S(2)}) %collective-permute-start.2) | collective-permute-done | bytes 1048608 | tf_op jit(solution)/shard_map/ppermute | solution.py:12
  271.0 1.0 copy.10
  (41 shorter events, 1.4 us)
Async XLA Ops:
  0.0 39.3 %copy-start = (bf16[1,1,768,2048]{3,2,1,0:T(8,128)(2,1)S(1)}, bf16[1,1,768,2048]{3,2,1,0:T(8,128)(2,1)}, u32[]{:S(2)}) copy-start(bf16[1,1,768,2048]{3,2,1,0:T(8,128)(2,1)} %param.12) | copy-start | bytes 9437188
  4.4 31.9 %copy-start.11 = (bf16[1,1,2048,768]{3,2,1,0:T(8,128)(2,1)S(1)}, bf16[1,1,2048,768]{3,2,1,0:T(8,128)(2,1)}, u32[]{:S(2)}) copy-start(bf16[1,1,2048,768]{3,2,1,0:T(8,128)(2,1)} %param.10) | copy-start | bytes 9437188
  35.0 1.3 copy-start.6
  47.5 4.6 %copy-start.10 = (f32[3,1,128,2]{2,3,1,0:T(2,128)S(1)}, f32[3,1,128,2]{2,3,1,0:T(2,128)}, u32[]{:S(2)}) copy-start(f32[3,1,128,2]{2,3,1,0:T(2,128)} %param.15) | copy-start | bytes 9220
  47.5 28.2 %all-to-all-start.1 = ((bf16[4,128,2048]{2,1,0:T(8,128)(2,1)}), bf16[4,128,2048]{2,1,0:T(8,128)(2,1)}, u32[]{:S(2)}, u32[]{:S(2)}) async-start(bf16[4,128,2048]{2,1,0:T(8,128)(2,1)} %bitcast.115), calls=%async_computation.1 | async-start | bytes 4194304 | tf_op jit(solution)/shard_map/all_to_all | solution.py:66
  75.8 2.2 copy-start.1
  78.0 18.4 %copy-start.9 = (f32[1,2048]{1,0:T(1,128)S(1)}, f32[1,2048]{1,0:T(1,128)}, u32[]{:S(2)}) copy-start(f32[1,2048]{1,0:T(1,128)} %param.9) | copy-start | bytes 24580
  80.1 16.1 %collective-permute-start = (f32[128,2048]{1,0:T(8,128)S(1)}, f32[128,2048]{1,0:T(8,128)S(1)}, u32[]{:S(2)}, u32[]{:S(2)}) collective-permute-start(f32[128,2048]{1,0:T(8,128)S(1)} %fusion.32), channel_id=1, source_target_pairs={{0,4},{4,8},{8,12},{12,16},{16,20},{20,24},{24,28},{28,0},{1,5},{5... | collective-permute-start | bytes 3145736 | tf_op jit(solution)/shard_map/ppermute | solution.py:12
  96.2 1.0 copy-start.4
  97.2 27.3 %copy-start.12 = (bf16[1,1,2048,768]{3,2,1,0:T(8,128)(2,1)S(1)}, bf16[1,1,2048,768]{3,2,1,0:T(8,128)(2,1)}, u32[]{:S(2)}) copy-start(bf16[1,1,2048,768]{3,2,1,0:T(8,128)(2,1)} %param.10) | copy-start | bytes 9437188
  123.2 1.3 copy-start.7
  135.7 25.9 %all-to-all-start.3 = ((bf16[4,128,2048]{2,1,0:T(8,128)(2,1)}), bf16[4,128,2048]{2,1,0:T(8,128)(2,1)}, u32[]{:S(2)}, u32[]{:S(2)}) async-start(bf16[4,128,2048]{2,1,0:T(8,128)(2,1)} %bitcast.117), calls=%async_computation.3 | async-start | bytes 4194304 | tf_op jit(solution)/shard_map/all_to_all | solution.py:66
  161.6 2.2 copy-start.5
  165.9 16.1 %collective-permute-start.1 = (f32[128,2048]{1,0:T(8,128)S(1)}, f32[128,2048]{1,0:T(8,128)S(1)}, u32[]{:S(2)}, u32[]{:S(2)}) collective-permute-start(f32[128,2048]{1,0:T(8,128)S(1)} %fusion.30), channel_id=1, source_target_pairs={{0,4},{4,8},{8,12},{12,16},{16,20},{20,24},{24,28},{28,0},{1,5},{5... | collective-permute-start | bytes 3145736 | tf_op jit(solution)/shard_map/ppermute | solution.py:12
  182.0 1.0 copy-start.2
  183.0 28.9 %copy-start.13 = (bf16[1,1,2048,768]{3,2,1,0:T(8,128)(2,1)S(1)}, bf16[1,1,2048,768]{3,2,1,0:T(8,128)(2,1)}, u32[]{:S(2)}) copy-start(bf16[1,1,2048,768]{3,2,1,0:T(8,128)(2,1)} %param.10) | copy-start | bytes 9437188
  210.6 1.3 copy-start.8
  223.2 27.5 %all-to-all-start.5 = ((bf16[4,128,2048]{2,1,0:T(8,128)(2,1)}), bf16[4,128,2048]{2,1,0:T(8,128)(2,1)}, u32[]{:S(2)}, u32[]{:S(2)}) async-start(bf16[4,128,2048]{2,1,0:T(8,128)(2,1)} %bitcast.116), calls=%async_computation.5 | async-start | bytes 4194304 | tf_op jit(solution)/shard_map/all_to_all | solution.py:66
  250.6 2.2 copy-start.3
  254.9 16.1 %collective-permute-start.2 = (f32[128,2048]{1,0:T(8,128)S(1)}, f32[128,2048]{1,0:T(8,128)S(1)}, u32[]{:S(2)}, u32[]{:S(2)}) collective-permute-start(f32[128,2048]{1,0:T(8,128)S(1)} %fusion.28), channel_id=1, source_target_pairs={{0,4},{4,8},{8,12},{12,16},{16,20},{20,24},{24,28},{28,0},{1,5},{5... | collective-permute-start | bytes 3145736 | tf_op jit(solution)/shard_map/ppermute | solution.py:12
where the time goes:
time: 273 us; the launch traced here: 272 us
  waiting for transfers between devices  116 us (42%)
  blocking collectives  84.1 us (31%)
  matrix products  50.3 us (18%)
  starting transfers between devices  13.6 us (5%)
  local copies, waits for them, and re-layouts  4.95 us (2%)
    all_to_all x3, blocking collectives, dispatch_whole(): lax.all_to_all(send, 'expert', split_axis=0, concat_axis=0, tiled=True)  84.1 us
    all_to_all x3, waiting for transfers between devices, whole_fn(): lax.all_to_all(run_expert(received), 'expert', split_axis=0, concat_axis=...  68.1 us
    ppermute x3, waiting for transfers between devices, shifted(): return lax.ppermute(x, axis, [(i, (i + by) % count) for i in range(count)])  48 us
    dot_general x3, matrix products, expert_ffn(): jnp.dot(hidden, down_mat, preferred_element_type=jnp.float32)  24.8 us
    all_to_all x3, starting transfers between devices, whole_fn(): lax.all_to_all(run_expert(received), 'expert', split_axis=0, concat_axis=...  13.4 us
    dot_general x6, matrix products, layer_block(): picked = jnp.dot(tables[k], returned, preferred_element_type=jnp.float32)  12.8 us
    dot_general x3, matrix products, expert_ffn(): gate_part = jnp.dot(rows_in, gate_mat, preferred_element_type=jnp.float32)  8.96 us
  transfers between devices with their start and end apart: 6, of which 6 were waited for; matrix products, arithmetic and copies ran while one was open for 0% of the time, Pallas kernels for 0%

commit v1 on v0

v1 whole, which is shorter than its diff:
```python
import jax
import jax.numpy as jnp
from jax import lax
from jax.experimental import pallas as pl
from jax.experimental.pallas import tpu as pltpu
from jax.sharding import PartitionSpec as P

TOP = 2
STEPS = 3
CHUNKS = 2
SHIFT = 2
LIMIT = 20 * 1024 * 1024


def shifted(x, axis, by):
    count = lax.axis_size(axis)
    return lax.ppermute(x, axis, [(i, (i + by) % count) for i in range(count)])


def rms_normed(current, gain_row):
    inv_rms = lax.rsqrt(jnp.mean(current * current, axis=-1, keepdims=True) + 1e-06)
    return (current * inv_rms * gain_row).astype(jnp.bfloat16)


def expert_ffn(rows_in, gate_mat, up_mat, down_mat):
    gate_part = jnp.dot(rows_in, gate_mat, preferred_element_type=jnp.float32)
    upward = jnp.dot(rows_in, up_mat, preferred_element_type=jnp.float32)
    hidden = (jax.nn.silu(gate_part) * upward).astype(jnp.bfloat16)
    return jnp.dot(hidden, down_mat, preferred_element_type=jnp.float32).astype(jnp.bfloat16)


def layer_by_slots(token_rows, gain_row, chosen, slot_rows, weights_in, experts, cap, mats):
    normed = rms_normed(token_rows, gain_row)
    flat_place = chosen * cap + slot_rows
    place_iota = jnp.arange(experts * cap, dtype=jnp.int32)
    tables = [
        (flat_place[:, k : k + 1] == place_iota[None, :]).astype(jnp.bfloat16) for k in range(TOP)
    ]
    occupied = tables[0] + tables[1]
    send = lax.dot_general(
        occupied, normed, (((0,), (0,)), ((), ())), preferred_element_type=jnp.float32
    )
    send = send.astype(jnp.bfloat16).reshape(experts, cap, normed.shape[1])
    received = lax.all_to_all(send, "expert", split_axis=0, concat_axis=0, tiled=True)
    result = expert_ffn(received.reshape(experts * cap, normed.shape[1]), *mats)
    returned = lax.all_to_all(
        result.reshape(send.shape), "expert", split_axis=0, concat_axis=0, tiled=True
    ).reshape(experts * cap, normed.shape[1])
    combined = jnp.zeros(token_rows.shape, jnp.float32)
    for k in range(TOP):
        picked = jnp.dot(tables[k], returned, preferred_element_type=jnp.float32)
        combined = combined + weights_in[:, k : k + 1] * picked
    return token_rows + combined


def run_by_slots(residual, norm_gain, mats, route_ids, route_slots, combine_weights):
    experts = lax.axis_size("expert")
    cap = 4 * residual.shape[1] // experts
    current = residual[0]
    for step in range(STEPS):
        current = layer_by_slots(
            current,
            norm_gain[0],
            route_ids[step, 0],
            route_slots[step, 0],
            combine_weights[step, 0],
            experts,
            cap,
            mats,
        )
        current = shifted(current, "section", 1)
    return current[None]


def across(x, bits):
    return lax.ppermute(x, "expert", [(e, e ^ bits) for e in range(4)])


def onward(x, bits):
    sections = lax.axis_size("section")
    pairs = [
        (s * 4 + e, ((s + 1) % sections) * 4 + (e ^ bits)) for s in range(sections) for e in range(4)
    ]
    return lax.ppermute(x, ("section", "expert"), pairs)


def norm_kernel(x_ref, gain_ref, normed_ref):
    x = x_ref[...]
    inv_rms = lax.rsqrt(jnp.mean(x * x, axis=-1, keepdims=True) + 1e-06)
    normed_ref[...] = (x * inv_rms * gain_ref[...]).astype(jnp.bfloat16)


def norm_rows(x, gain):
    return pl.pallas_call(
        norm_kernel,
        out_shape=jax.ShapeDtypeStruct(x.shape, jnp.bfloat16),
        compiler_params=pltpu.CompilerParams(vmem_limit_bytes=LIMIT),
        cost_estimate=pl.CostEstimate(flops=5 * x.size, bytes_accessed=6 * x.size, transcendentals=0),
    )(x, gain)


def total_kernel(x_ref, own_ref, a_ref, b_ref, gain_ref, new_ref, normed_ref):
    f32 = jnp.float32
    x = x_ref[...] + (own_ref[...].astype(f32) + a_ref[...].astype(f32) + b_ref[...].astype(f32))
    new_ref[...] = x
    inv_rms = lax.rsqrt(jnp.mean(x * x, axis=-1, keepdims=True) + 1e-06)
    normed_ref[...] = (x * inv_rms * gain_ref[...]).astype(jnp.bfloat16)


def total_rows(x, own, a, b, gain):
    return pl.pallas_call(
        total_kernel,
        out_shape=(
            jax.ShapeDtypeStruct(x.shape, jnp.float32),
            jax.ShapeDtypeStruct(x.shape, jnp.bfloat16),
        ),
        compiler_params=pltpu.CompilerParams(vmem_limit_bytes=LIMIT),
        cost_estimate=pl.CostEstimate(flops=8 * x.size, bytes_accessed=16 * x.size, transcendentals=0),
    )(x, own, a, b, gain)


def ffn_kernel(own, rx, ry, rd, weight, gate, up, down, o_own, o_x, o_y, o_d):
    f32 = jnp.float32
    n = own.shape[0]
    rows = jnp.concatenate([own[...], rx[...], ry[...], rd[...]], axis=0)
    gate_part = jnp.dot(rows, gate[...], preferred_element_type=f32)
    upward = jnp.dot(rows, up[...], preferred_element_type=f32)
    silu = gate_part / (1.0 + jnp.exp(-gate_part))
    hidden = (silu * upward * weight[...]).astype(jnp.bfloat16)
    out = jnp.dot(hidden, down[...], preferred_element_type=f32).astype(jnp.bfloat16)
    for j, ref in enumerate((o_own, o_x, o_y, o_d)):
        ref[...] = out[j * n : (j + 1) * n]


def weighted_ffn(pieces, weight, gate_mat, up_mat, down_mat):
    n, width = pieces[0].shape
    macs = 4 * n * gate_mat.size * 3
    return pl.pallas_call(
        ffn_kernel,
        out_shape=[jax.ShapeDtypeStruct((n, width), jnp.bfloat16)] * 4,
        compiler_params=pltpu.CompilerParams(vmem_limit_bytes=LIMIT),
        cost_estimate=pl.CostEstimate(
            flops=2 * macs, bytes_accessed=16 * n * width, transcendentals=4 * n * gate_mat.shape[1]
        ),
    )(*pieces, weight, gate_mat, up_mat, down_mat)


def run_by_rows(residual, norm_gain, mats, route_ids, combine_weights):
    me = lax.axis_index("expert")
    rows = residual.shape[1] // CHUNKS
    row_weights = []
    for bits in range(4):
        named = route_ids[:, 0] == (me ^ bits)
        weight = jnp.sum(jnp.where(named, combine_weights[:, 0], 0.0), axis=-1)
        row_weights.append(across(weight, bits) if bits else weight)
    row_weights = jnp.stack(row_weights, axis=1)
    gain = norm_gain
    next_gain = lax.ppermute(norm_gain, "section", [((i + 1) % 8, i) for i in range(8)]) if SHIFT == 2 else gain
    xs = [residual[0, c * rows : (c + 1) * rows] for c in range(CHUNKS)]
    firsts = []
    for c in range(CHUNKS):
        own = norm_rows(xs[c], gain)
        firsts.append((own, across(own, 1), across(own, 2)))
    for step in range(STEPS):
        for c in range(CHUNKS):
            one, two = (1, 2) if c % 2 == 0 else (2, 1)
            own, rx, ry = firsts[c]
            rd = across(rx, 2) if c % 2 == 0 else across(ry, 1)
            weight = row_weights[step, :, c * rows : (c + 1) * rows].reshape(4 * rows, 1)
            o_own, o_x, o_y, o_d = weighted_ffn((own, rx, ry, rd), weight, *mats)
            if c % 2 == 0:
                got_x = across(o_x, 1)
                got_y = across(o_y + across(o_d, 1), 2)
            else:
                got_y = across(o_y, 2)
                got_x = across(o_x + across(o_d, 2), 1)
            new, normed = total_rows(xs[c], o_own, got_x, got_y, next_gain)
            if step < STEPS - 1:
                if SHIFT == 2:
                    firsts[c] = (onward(normed, 0), onward(normed, 1), onward(normed, 2))
                    xs[c] = onward(new, 0)
                else:
                    xs[c] = onward(new, 0)
                    own = norm_rows(xs[c], gain)
                    firsts[c] = (own, across(own, 1), across(own, 2))
            else:
                xs[c] = onward(new, 0)
    return jnp.concatenate(xs, axis=0)[None]


def per_device(residual, norm_gain, w_gate, w_up, w_down, route_ids, route_slots, combine_weights):
    mats = (w_gate[0, 0], w_up[0, 0], w_down[0, 0])
    if lax.axis_size("expert") == 4:
        return run_by_rows(residual, norm_gain, mats, route_ids, combine_weights)
    return run_by_slots(residual, norm_gain, mats, route_ids, route_slots, combine_weights)


def solution(mesh):
    in_specs = (
        P("section", "expert", None),
        P("section", None),
        P("section", "expert", None, None),
        P("section", "expert", None, None),
        P("section", "expert", None, None),
        P(None, "section", "expert", None),
        P(None, "section", "expert", None),
        P(None, "section", "expert", None),
    )
    out_specs = P("section", "expert", None)
    return jax.shard_map(
        per_device, mesh=mesh, in_specs=in_specs, out_specs=out_specs, check_vma=False
    )
```

time: 273 us -> 184 us (0.67)
  blocking collectives: 84.1 us -> 0 us
  matrix products: 50.3 us -> 0 us
  waiting for transfers between devices: 116 us -> 72.4 us
  starting transfers between devices: 13.6 us -> 50.5 us
  Pallas kernels: 0 us -> 30.5 us
  local copies, waits for them, and re-layouts: 4.95 us -> 26.6 us
    all_to_all x3 -> x0, blocking collectives: 84.1 us -> none  [dispatch_whole(): lax.all_to_all(send, 'expert', split_axis=0, concat_axis=0, tiled=True)]
    all_to_all x3 -> x0, waiting for transfers between devices: 68.1 us -> none  [whole_fn(): lax.all_to_all(run_expert(received), 'expert', split_axis=0, concat_axis=...]
    ppermute x3 -> x50, starting transfers between devices: 0.17 us -> 50.5 us  [the longest x31 36.7 us: across(): return lax.ppermute(x, 'expert', [(e, e ^ bits) for e in range(4)])]
    dot_general x15 -> x0, matrix products: 50.3 us -> none  [the longest x3 24.8 us: expert_ffn(): jnp.dot(hidden, down_mat, preferred_element_type=jnp.float32)]
    pallas_call x0 -> x14, Pallas kernels: none -> 30.5 us  [the longest x6 23.8 us: weighted_ffn(): pl.pallas_call(ffn_kernel, out_shape=[jax.ShapeDtypeStruct((n, width), jn...]
    ppermute x3 -> x50, waiting for transfers between devices: 48 us -> 72.4 us  [the longest x31 41.6 us: across(): return lax.ppermute(x, 'expert', [(e, e ^ bits) for e in range(4)])]
    unnamed x29 -> x72, local copies, waits for them, and re-layouts: 4.92 us -> 23.7 us
    all_to_all x3 -> x0, starting transfers between devices: 13.4 us -> none  [whole_fn(): lax.all_to_all(run_expert(received), 'expert', split_axis=0, concat_axis=...]
  transfers between devices with their start and end apart: 6 -> 50, of which waited for: 6 -> 26; matrix products, arithmetic and copies ran while one was open for 0% -> 2% of each run, Pallas kernels for 0% -> 16%
where the time goes in v1:
time: 184 us
  waiting for transfers between devices  72.4 us (39%)
  starting transfers between devices  50.5 us (27%)
  Pallas kernels  30.5 us (17%)
  local copies, waits for them, and re-layouts  26.6 us (14%)
  other arithmetic  3.14 us (2%)
    ppermute x31, waiting for transfers between devices, across(): return lax.ppermute(x, 'expert', [(e, e ^ bits) for e in range(4)])  41.6 us
    ppermute x31, starting transfers between devices, across(): return lax.ppermute(x, 'expert', [(e, e ^ bits) for e in range(4)])  36.7 us
    ppermute x18, waiting for transfers between devices, onward(): return lax.ppermute(x, ('section', 'expert'), pairs)  29.5 us
    pallas_call x6, Pallas kernels, weighted_ffn(): pl.pallas_call(ffn_kernel, out_shape=[jax.ShapeDtypeStruct((n, width), jn...  23.8 us
    unnamed x72, local copies, waits for them, and re-layouts  23.7 us
    ppermute x18, starting transfers between devices, onward(): return lax.ppermute(x, ('section', 'expert'), pairs)  13.7 us
    pallas_call x6, Pallas kernels, total_rows(): pl.pallas_call(total_kernel, out_shape=(jax.ShapeDtypeStruct(x.shape, jnp...  5.68 us
  transfers between devices with their start and end apart: 50, of which 26 were waited for; matrix products, arithmetic and copies ran while one was open for 2% of the time, Pallas kernels for 16%

profile of v1, /device:TPU:0, one launch (start us, length us, event | category | flops | bytes accessed | tf_op | source)
XLA Modules:
  0.0 183.5 jit_solution(15455235910127436383)
XLA Ops:
  3.9 3.0 %collective-permute-start.28 = (bf16[64,2048]{1,0:T(8,128)(2,1)}, bf16[64,2048]{1,0:T(8,128)(2,1)}, u32[]{:S(2)}, u32[]{:S(2)}) collective-permute-start(bf16[64,2048]{1,0:T(8,128)(2,1)} %shard_map.80.own), channel_id=1, source_target_pairs={{0,2},{1,3},{2,0},{3,1},{4,6},{5,7},{6,4},{7,5},{8,10},{9,11},{10,... | collective-permute-start | bytes 786440 | tf_op jit(solution)/shard_map/ppermute | solution.py:76
  9.3 2.0 %collective-permute-start.4 = (f32[3,128]{1,0:T(4,128)S(1)}, f32[3,128]{1,0:T(4,128)S(1)}, u32[]{:S(2)}, u32[]{:S(2)}) collective-permute-start(f32[3,128]{1,0:T(4,128)S(1)} %get-tuple-element.76), channel_id=1, source_target_pairs={{0,2},{1,3},{2,0},{3,1},{4,6},{5,7},{6,4},{7,5},{8,10},{9,11},{10,... | collective-permute-start | bytes 4616 | tf_op jit(solution)/shard_map/ppermute | solution.py:76
  19.6 4.5 %collective-permute-done.27.rx = bf16[64,2048]{1,0:T(8,128)(2,1)} collective-permute-done((bf16[64,2048]{1,0:T(8,128)(2,1)}, bf16[64,2048]{1,0:T(8,128)(2,1)}, u32[]{:S(2)}, u32[]{:S(2)}) %collective-permute-start.27) | collective-permute-done | bytes 262176 | tf_op jit(solution)/shard_map/ppermute | solution.py:76
  24.2 3.2 %collective-permute-done.29.rd = bf16[64,2048]{1,0:T(8,128)(2,1)} collective-permute-done((bf16[64,2048]{1,0:T(8,128)(2,1)}, bf16[64,2048]{1,0:T(8,128)(2,1)}, u32[]{:S(2)}, u32[]{:S(2)}) %collective-permute-start.29) | collective-permute-done | bytes 262176 | tf_op jit(solution)/shard_map/ppermute | solution.py:76
  27.4 1.9 %copy-done.1 = bf16[1,1,2048,768]{3,2,1,0:T(8,128)(2,1)S(1)} copy-done((bf16[1,1,2048,768]{3,2,1,0:T(8,128)(2,1)S(1)}, bf16[1,1,2048,768]{3,2,1,0:T(8,128)(2,1)}, u32[]{:S(2)}) %copy-start.1) | copy-done | bytes 3145752
  31.2 4.6 %shard_map.81 = (bf16[64,2048]{1,0:T(8,128)(2,1)S(1)}, bf16[64,2048]{1,0:T(8,128)(2,1)S(1)}, bf16[64,2048]{1,0:T(8,128)(2,1)S(1)}, bf16[64,2048]{1,0:T(8,128)(2,1)}) custom-call(bf16[64,2048]{1,0:T(8,128)(2,1)} %shard_map.80.own, bf16[64,2048]{1,0:T(8,128)(2,1)} %collective-permute-done.27.rx, bf16[64,2048]{1,0:T(8,128)(2,1)} %collective-permute-done.28.ry, ...), custom_call_target="tpu_custom_call" | custom-call | flops 2415919104 | bytes 2097152 | tf_op jit(solution)/shard_map/pallas_call | solution.py:138
  43.3 3.9 %shard_map.74 = (bf16[64,2048]{1,0:T(8,128)(2,1)S(1)}, bf16[64,2048]{1,0:T(8,128)(2,1)S(1)}, bf16[64,2048]{1,0:T(8,128)(2,1)S(1)}, bf16[64,2048]{1,0:T(8,128)(2,1)S(1)}) custom-call(bf16[64,2048]{1,0:T(8,128)(2,1)S(1)} %shard_map.73.own, bf16[64,2048]{1,0:T(8,128)(2,1)} %collective-permute-done.rx, bf16[64,2048]{1,0:T(8,128)(2,1)} %collective-permute-done.1.ry, ...), custom_call_target="tpu_custom_call" | custom-call | flops 2415919104 | bytes 2097152 | tf_op jit(solution)/shard_map/pallas_call | solution.py:138
  52.4 4.1 %collective-permute-done.7 = bf16[64,2048]{1,0:T(8,128)(2,1)S(1)} collective-permute-done((bf16[64,2048]{1,0:T(8,128)(2,1)S(1)}, bf16[64,2048]{1,0:T(8,128)(2,1)S(1)}, u32[]{:S(2)}, u32[]{:S(2)}) %collective-permute-start.7) | collective-permute-done | bytes 262176 | tf_op jit(solution)/shard_map/ppermute | solution.py:76
  58.5 2.6 %collective-permute-done.31.a_ref = bf16[64,2048]{1,0:T(8,128)(2,1)S(1)} collective-permute-done((bf16[64,2048]{1,0:T(8,128)(2,1)S(1)}, bf16[64,2048]{1,0:T(8,128)(2,1)S(1)}, u32[]{:S(2)}, u32[]{:S(2)}) %collective-permute-start.31) | collective-permute-done | bytes 262176 | tf_op jit(solution)/shard_map/ppermute | solution.py:76
  68.9 1.9 %collective-permute-done.36.ry = bf16[64,2048]{1,0:T(8,128)(2,1)} collective-permute-done((bf16[64,2048]{1,0:T(8,128)(2,1)}, bf16[64,2048]{1,0:T(8,128)(2,1)}, u32[]{:S(2)}, u32[]{:S(2)}) %collective-permute-start.36) | collective-permute-done | bytes 262176 | tf_op jit(solution)/shard_map/ppermute | solution.py:84
  74.0 2.5 %collective-permute-done.12.rx = bf16[64,2048]{1,0:T(8,128)(2,1)} collective-permute-done((bf16[64,2048]{1,0:T(8,128)(2,1)}, bf16[64,2048]{1,0:T(8,128)(2,1)}, u32[]{:S(2)}, u32[]{:S(2)}) %collective-permute-start.12) | collective-permute-done | bytes 262176 | tf_op jit(solution)/shard_map/ppermute | solution.py:84
  78.3 4.3 %collective-permute-done.35.rx = bf16[64,2048]{1,0:T(8,128)(2,1)} collective-permute-done((bf16[64,2048]{1,0:T(8,128)(2,1)}, bf16[64,2048]{1,0:T(8,128)(2,1)}, u32[]{:S(2)}, u32[]{:S(2)}) %collective-permute-start.35) | collective-permute-done | bytes 262176 | tf_op jit(solution)/shard_map/ppermute | solution.py:84
  83.8 2.7 %collective-permute-done.37.rd = bf16[64,2048]{1,0:T(8,128)(2,1)} collective-permute-done((bf16[64,2048]{1,0:T(8,128)(2,1)}, bf16[64,2048]{1,0:T(8,128)(2,1)}, u32[]{:S(2)}, u32[]{:S(2)}) %collective-permute-start.37) | collective-permute-done | bytes 262176 | tf_op jit(solution)/shard_map/ppermute | solution.py:76
  86.5 1.9 %copy-done.3 = bf16[1,1,2048,768]{3,2,1,0:T(8,128)(2,1)S(1)} copy-done((bf16[1,1,2048,768]{3,2,1,0:T(8,128)(2,1)S(1)}, bf16[1,1,2048,768]{3,2,1,0:T(8,128)(2,1)}, u32[]{:S(2)}) %copy-start.3) | copy-done | bytes 3145752
  91.2 3.8 %shard_map.83 = (bf16[64,2048]{1,0:T(8,128)(2,1)S(1)}, bf16[64,2048]{1,0:T(8,128)(2,1)S(1)}, bf16[64,2048]{1,0:T(8,128)(2,1)S(1)}, bf16[64,2048]{1,0:T(8,128)(2,1)S(1)}) custom-call(bf16[64,2048]{1,0:T(8,128)(2,1)S(1)} %copy-done.20, bf16[64,2048]{1,0:T(8,128)(2,1)} %collective-permute-done.35.rx, bf16[64,2048]{1,0:T(8,128)(2,1)} %collective-permute-done.36.ry, ...), custom_call_target="tpu_custom_call" | custom-call | flops 2415919104 | bytes 2097152 | tf_op jit(solution)/shard_map/pallas_call | solution.py:138
  95.9 3.9 %shard_map.76 = (bf16[64,2048]{1,0:T(8,128)(2,1)S(1)}, bf16[64,2048]{1,0:T(8,128)(2,1)S(1)}, bf16[64,2048]{1,0:T(8,128)(2,1)S(1)}, bf16[64,2048]{1,0:T(8,128)(2,1)S(1)}) custom-call(bf16[64,2048]{1,0:T(8,128)(2,1)} %collective-permute-done.11.own, bf16[64,2048]{1,0:T(8,128)(2,1)} %collective-permute-done.12.rx, bf16[64,2048]{1,0:T(8,128)(2,1)} %collective-permute-done.13.ry, ...), custom_call_target="tpu_custom_call" | custom-call | flops 2415919104 | bytes 2097152 | tf_op jit(solution)/shard_map/pallas_call | solution.py:138
  103.2 3.4 %collective-permute-done.16 = bf16[64,2048]{1,0:T(8,128)(2,1)S(1)} collective-permute-done((bf16[64,2048]{1,0:T(8,128)(2,1)S(1)}, bf16[64,2048]{1,0:T(8,128)(2,1)S(1)}, u32[]{:S(2)}, u32[]{:S(2)}) %collective-permute-start.16) | collective-permute-done | bytes 262176 | tf_op jit(solution)/shard_map/ppermute | solution.py:76
  109.8 2.4 %collective-permute-done.39.a_ref = bf16[64,2048]{1,0:T(8,128)(2,1)S(1)} collective-permute-done((bf16[64,2048]{1,0:T(8,128)(2,1)S(1)}, bf16[64,2048]{1,0:T(8,128)(2,1)S(1)}, u32[]{:S(2)}, u32[]{:S(2)}) %collective-permute-start.39) | collective-permute-done | bytes 262176 | tf_op jit(solution)/shard_map/ppermute | solution.py:76
  115.0 2.8 %collective-permute-done.15.a_ref = bf16[64,2048]{1,0:T(8,128)(2,1)S(1)} collective-permute-done((bf16[64,2048]{1,0:T(8,128)(2,1)S(1)}, bf16[64,2048]{1,0:T(8,128)(2,1)S(1)}, u32[]{:S(2)}, u32[]{:S(2)}) %collective-permute-start.15) | collective-permute-done | bytes 262176 | tf_op jit(solution)/shard_map/ppermute | solution.py:76
  120.0 1.9 %collective-permute-start.43 = (bf16[64,2048]{1,0:T(8,128)(2,1)}, bf16[64,2048]{1,0:T(8,128)(2,1)}, u32[]{:S(2)}, u32[]{:S(2)}) collective-permute-start(bf16[64,2048]{1,0:T(8,128)(2,1)} %get-tuple-element.67), channel_id=1, source_target_pairs={{0,5},{1,4},{2,7},{3,6},{4,9},{5,8},{6,11},{7,10},{8,13},{9,12},{1... | collective-permute-start | bytes 786440 | tf_op jit(solution)/shard_map/ppermute | solution.py:84
  126.0 2.6 %collective-permute-done.20.rx = bf16[64,2048]{1,0:T(8,128)(2,1)} collective-permute-done((bf16[64,2048]{1,0:T(8,128)(2,1)}, bf16[64,2048]{1,0:T(8,128)(2,1)}, u32[]{:S(2)}, u32[]{:S(2)}) %collective-permute-start.20) | collective-permute-done | bytes 262176 | tf_op jit(solution)/shard_map/ppermute | solution.py:84
  129.6 5.9 %collective-permute-done.43.rx = bf16[64,2048]{1,0:T(8,128)(2,1)} collective-permute-done((bf16[64,2048]{1,0:T(8,128)(2,1)}, bf16[64,2048]{1,0:T(8,128)(2,1)}, u32[]{:S(2)}, u32[]{:S(2)}) %collective-permute-start.43) | collective-permute-done | bytes 262176 | tf_op jit(solution)/shard_map/ppermute | solution.py:84
  135.5 1.9 %collective-permute-start.41 = (f32[64,2048]{1,0:T(8,128)}, f32[64,2048]{1,0:T(8,128)S(1)}, u32[]{:S(2)}, u32[]{:S(2)}) collective-permute-start(f32[64,2048]{1,0:T(8,128)} %copy-done.27), channel_id=1, source_target_pairs={{0,4},{1,5},{2,6},{3,7},{4,8},{5,9},{6,10},{7,11},{8,12},{9,13},{1... | collective-permute-start | bytes 1572872 | tf_op jit(solution)/shard_map/ppermute | solution.py:84
  137.4 2.7 %collective-permute-done.45.rd = bf16[64,2048]{1,0:T(8,128)(2,1)} collective-permute-done((bf16[64,2048]{1,0:T(8,128)(2,1)}, bf16[64,2048]{1,0:T(8,128)(2,1)}, u32[]{:S(2)}, u32[]{:S(2)}) %collective-permute-start.45) | collective-permute-done | bytes 262176 | tf_op jit(solution)/shard_map/ppermute | solution.py:76
  140.1 1.9 %copy-done.4 = bf16[1,1,2048,768]{3,2,1,0:T(8,128)(2,1)S(1)} copy-done((bf16[1,1,2048,768]{3,2,1,0:T(8,128)(2,1)S(1)}, bf16[1,1,2048,768]{3,2,1,0:T(8,128)(2,1)}, u32[]{:S(2)}) %copy-start.4) | copy-done | bytes 3145752
  144.8 3.8 %shard_map.85 = (bf16[64,2048]{1,0:T(8,128)(2,1)S(1)}, bf16[64,2048]{1,0:T(8,128)(2,1)S(1)}, bf16[64,2048]{1,0:T(8,128)(2,1)S(1)}, bf16[64,2048]{1,0:T(8,128)(2,1)S(1)}) custom-call(bf16[64,2048]{1,0:T(8,128)(2,1)S(1)} %copy-done.18, bf16[64,2048]{1,0:T(8,128)(2,1)} %collective-permute-done.43.rx, bf16[64,2048]{1,0:T(8,128)(2,1)} %collective-permute-done.44.ry, ...), custom_call_target="tpu_custom_call" | custom-call | flops 2415919104 | bytes 2097152 | tf_op jit(solution)/shard_map/pallas_call | solution.py:138
  149.4 3.9 %shard_map.78 = (bf16[64,2048]{1,0:T(8,128)(2,1)S(1)}, bf16[64,2048]{1,0:T(8,128)(2,1)S(1)}, bf16[64,2048]{1,0:T(8,128)(2,1)S(1)}, bf16[64,2048]{1,0:T(8,128)(2,1)S(1)}) custom-call(bf16[64,2048]{1,0:T(8,128)(2,1)} %collective-permute-done.19.own, bf16[64,2048]{1,0:T(8,128)(2,1)} %collective-permute-done.20.rx, bf16[64,2048]{1,0:T(8,128)(2,1)} %collective-permute-done.21.ry, ...), custom_call_target="tpu_custom_call" | custom-call | flops 2415919104 | bytes 2097152 | tf_op jit(solution)/shard_map/pallas_call | solution.py:138
  156.8 3.1 %collective-permute-done.24 = bf16[64,2048]{1,0:T(8,128)(2,1)S(1)} collective-permute-done((bf16[64,2048]{1,0:T(8,128)(2,1)S(1)}, bf16[64,2048]{1,0:T(8,128)(2,1)S(1)}, u32[]{:S(2)}, u32[]{:S(2)}) %collective-permute-start.24) | collective-permute-done | bytes 262176 | tf_op jit(solution)/shard_map/ppermute | solution.py:76
  162.6 2.9 %collective-permute-done.47.a_ref = bf16[64,2048]{1,0:T(8,128)(2,1)S(1)} collective-permute-done((bf16[64,2048]{1,0:T(8,128)(2,1)S(1)}, bf16[64,2048]{1,0:T(8,128)(2,1)S(1)}, u32[]{:S(2)}, u32[]{:S(2)}) %collective-permute-start.47) | collective-permute-done | bytes 262176 | tf_op jit(solution)/shard_map/ppermute | solution.py:76
  166.5 4.5 %collective-permute-done.23.a_ref = bf16[64,2048]{1,0:T(8,128)(2,1)S(1)} collective-permute-done((bf16[64,2048]{1,0:T(8,128)(2,1)S(1)}, bf16[64,2048]{1,0:T(8,128)(2,1)S(1)}, u32[]{:S(2)}, u32[]{:S(2)}) %collective-permute-start.23) | collective-permute-done | bytes 262176 | tf_op jit(solution)/shard_map/ppermute | solution.py:76
  171.9 5.0 %collective-permute-done.49 = f32[64,2048]{1,0:T(8,128)S(1)} collective-permute-done((f32[64,2048]{1,0:T(8,128)S(1)}, f32[64,2048]{1,0:T(8,128)S(1)}, u32[]{:S(2)}, u32[]{:S(2)}) %collective-permute-start.49) | collective-permute-done | bytes 524320 | tf_op jit(solution)/shard_map/ppermute | solution.py:84
  176.9 5.6 %collective-permute-done.26 = f32[64,2048]{1,0:T(8,128)S(1)} collective-permute-done((f32[64,2048]{1,0:T(8,128)S(1)}, f32[64,2048]{1,0:T(8,128)S(1)}, u32[]{:S(2)}, u32[]{:S(2)}) %collective-permute-start.26) | collective-permute-done | bytes 524320 | tf_op jit(solution)/shard_map/ppermute | solution.py:84
  (175 shorter events, 78.2 us)
Async XLA Ops:
  3.9 14.0 %collective-permute-start.28 = (bf16[64,2048]{1,0:T(8,128)(2,1)}, bf16[64,2048]{1,0:T(8,128)(2,1)}, u32[]{:S(2)}, u32[]{:S(2)}) collective-permute-start(bf16[64,2048]{1,0:T(8,128)(2,1)} %shard_map.80.own), channel_id=1, source_target_pairs={{0,2},{1,3},{2,0},{3,1},{4,6},{5,7},{6,4},{7,5},{8,10},{9,11},{10,... | collective-permute-start | bytes 786440 | tf_op jit(solution)/shard_map/ppermute | solution.py:76
  7.0 11.5 %collective-permute-start = (bf16[64,2048]{1,0:T(8,128)(2,1)S(1)}, bf16[64,2048]{1,0:T(8,128)(2,1)}, u32[]{:S(2)}, u32[]{:S(2)}) collective-permute-start(bf16[64,2048]{1,0:T(8,128)(2,1)S(1)} %shard_map.73.own), channel_id=1, source_target_pairs={{0,1},{1,0},{2,3},{3,2},{4,5},{5,4},{6,7},{7,6},{8,9},{9,8},{10,11... | collective-permute-start | bytes 786440 | tf_op jit(solution)/shard_map/ppermute | solution.py:76
  16.3 23.1 %collective-permute-start.1 = (bf16[64,2048]{1,0:T(8,128)(2,1)S(1)}, bf16[64,2048]{1,0:T(8,128)(2,1)}, u32[]{:S(2)}, u32[]{:S(2)}) collective-permute-start(bf16[64,2048]{1,0:T(8,128)(2,1)S(1)} %shard_map.73.own), channel_id=1, source_target_pairs={{0,2},{1,3},{2,0},{3,1},{4,6},{5,7},{6,4},{7,5},{8,10},{9,11},{10,... | collective-permute-start | bytes 786440 | tf_op jit(solution)/shard_map/ppermute | solution.py:76
  18.5 21.0 %collective-permute-start.2 = (bf16[64,2048]{1,0:T(8,128)(2,1)}, bf16[64,2048]{1,0:T(8,128)(2,1)}, u32[]{:S(2)}, u32[]{:S(2)}) collective-permute-start(bf16[64,2048]{1,0:T(8,128)(2,1)} %collective-permute-done.rx), channel_id=1, source_target_pairs={{0,2},{1,3},{2,0},{3,1},{4,6},{5,7},{6,4},{7,5},{8,10},{9,11},{10,... | collective-permute-start | bytes 786440 | tf_op jit(solution)/shard_map/ppermute | solution.py:76
  37.9 11.4 %collective-permute-start.30 = (bf16[64,2048]{1,0:T(8,128)(2,1)}, bf16[64,2048]{1,0:T(8,128)(2,1)}, u32[]{:S(2)}, u32[]{:S(2)}) collective-permute-start(bf16[64,2048]{1,0:T(8,128)(2,1)} %get-tuple-element.58), channel_id=1, source_target_pairs={{0,2},{1,3},{2,0},{3,1},{4,6},{5,7},{6,4},{7,5},{8,10},{9,11},{10,... | collective-permute-start | bytes 786440 | tf_op jit(solution)/shard_map/ppermute | solution.py:76
  50.3 10.7 %collective-permute-start.31 = (bf16[64,2048]{1,0:T(8,128)(2,1)S(1)}, bf16[64,2048]{1,0:T(8,128)(2,1)S(1)}, u32[]{:S(2)}, u32[]{:S(2)}) collective-permute-start(bf16[64,2048]{1,0:T(8,128)(2,1)S(1)} %add.21), channel_id=1, source_target_pairs={{0,1},{1,0},{2,3},{3,2},{4,5},{5,4},{6,7},{7,6},{8,9},{9,8},{10,11... | collective-permute-start | bytes 786440 | tf_op jit(solution)/shard_map/ppermute | solution.py:76
  51.0 13.4 %collective-permute-start.6 = (bf16[64,2048]{1,0:T(8,128)(2,1)S(1)}, bf16[64,2048]{1,0:T(8,128)(2,1)S(1)}, u32[]{:S(2)}, u32[]{:S(2)}) collective-permute-start(bf16[64,2048]{1,0:T(8,128)(2,1)S(1)} %get-tuple-element.40), channel_id=1, source_target_pairs={{0,1},{1,0},{2,3},{3,2},{4,5},{5,4},{6,7},{7,6},{8,9},{9,8},{10,11... | collective-permute-start | bytes 786440 | tf_op jit(solution)/shard_map/ppermute | solution.py:76
  62.6 10.7 %collective-permute-start.34 = (bf16[64,2048]{1,0:T(8,128)(2,1)}, bf16[64,2048]{1,0:T(8,128)(2,1)S(1)}, u32[]{:S(2)}, u32[]{:S(2)}) collective-permute-start(bf16[64,2048]{1,0:T(8,128)(2,1)} %get-tuple-element.61), channel_id=1, source_target_pairs={{0,4},{1,5},{2,6},{3,7},{4,8},{5,9},{6,10},{7,11},{8,12},{9,13},{1... | collective-permute-start | bytes 786440 | tf_op jit(solution)/shard_map/ppermute | solution.py:84
  66.1 10.4 %collective-permute-start.12 = (bf16[64,2048]{1,0:T(8,128)(2,1)}, bf16[64,2048]{1,0:T(8,128)(2,1)}, u32[]{:S(2)}, u32[]{:S(2)}) collective-permute-start(bf16[64,2048]{1,0:T(8,128)(2,1)} %get-tuple-element.44), channel_id=1, source_target_pairs={{0,5},{1,4},{2,7},{3,6},{4,9},{5,8},{6,11},{7,10},{8,13},{9,12},{1... | collective-permute-start | bytes 786440 | tf_op jit(solution)/shard_map/ppermute | solution.py:84
  67.1 15.4 %collective-permute-start.35 = (bf16[64,2048]{1,0:T(8,128)(2,1)}, bf16[64,2048]{1,0:T(8,128)(2,1)}, u32[]{:S(2)}, u32[]{:S(2)}) collective-permute-start(bf16[64,2048]{1,0:T(8,128)(2,1)} %get-tuple-element.61), channel_id=1, source_target_pairs={{0,5},{1,4},{2,7},{3,6},{4,9},{5,8},{6,11},{7,10},{8,13},{9,12},{1... | collective-permute-start | bytes 786440 | tf_op jit(solution)/shard_map/ppermute | solution.py:84
  70.8 15.7 %collective-permute-start.37 = (bf16[64,2048]{1,0:T(8,128)(2,1)}, bf16[64,2048]{1,0:T(8,128)(2,1)}, u32[]{:S(2)}, u32[]{:S(2)}) collective-permute-start(bf16[64,2048]{1,0:T(8,128)(2,1)} %collective-permute-done.36.ry), channel_id=1, source_target_pairs={{0,1},{1,0},{2,3},{3,2},{4,5},{5,4},{6,7},{7,6},{8,9},{9,8},{10,11... | collective-permute-start | bytes 786440 | tf_op jit(solution)/shard_map/ppermute | solution.py:76
  72.3 23.6 %collective-permute-start.11 = (bf16[64,2048]{1,0:T(8,128)(2,1)}, bf16[64,2048]{1,0:T(8,128)(2,1)}, u32[]{:S(2)}, u32[]{:S(2)}) collective-permute-start(bf16[64,2048]{1,0:T(8,128)(2,1)} %get-tuple-element.44), channel_id=1, source_target_pairs={{0,4},{1,5},{2,6},{3,7},{4,8},{5,9},{6,10},{7,11},{8,12},{9,13},{1... | collective-permute-start | bytes 786440 | tf_op jit(solution)/shard_map/ppermute | solution.py:84
  74.0 21.9 %collective-permute-start.13 = (bf16[64,2048]{1,0:T(8,128)(2,1)}, bf16[64,2048]{1,0:T(8,128)(2,1)}, u32[]{:S(2)}, u32[]{:S(2)}) collective-permute-start(bf16[64,2048]{1,0:T(8,128)(2,1)} %get-tuple-element.44), channel_id=1, source_target_pairs={{0,6},{1,7},{2,4},{3,5},{4,10},{5,11},{6,8},{7,9},{8,14},{9,15},{1... | collective-permute-start | bytes 786440 | tf_op jit(solution)/shard_map/ppermute | solution.py:84
  76.5 19.3 %collective-permute-start.14 = (bf16[64,2048]{1,0:T(8,128)(2,1)}, bf16[64,2048]{1,0:T(8,128)(2,1)}, u32[]{:S(2)}, u32[]{:S(2)}) collective-permute-start(bf16[64,2048]{1,0:T(8,128)(2,1)} %collective-permute-done.12.rx), channel_id=1, source_target_pairs={{0,2},{1,3},{2,0},{3,1},{4,6},{5,7},{6,4},{7,5},{8,10},{9,11},{10,... | collective-permute-start | bytes 786440 | tf_op jit(solution)/shard_map/ppermute | solution.py:76
  82.6 25.6 %collective-permute-start.33 = (f32[64,2048]{1,0:T(8,128)}, f32[64,2048]{1,0:T(8,128)S(1)}, u32[]{:S(2)}, u32[]{:S(2)}) collective-permute-start(f32[64,2048]{1,0:T(8,128)} %copy-done.28), channel_id=1, source_target_pairs={{0,4},{1,5},{2,6},{3,7},{4,8},{5,9},{6,10},{7,11},{8,12},{9,13},{1... | collective-permute-start | bytes 1572872 | tf_op jit(solution)/shard_map/ppermute | solution.py:84
  101.3 13.7 %collective-permute-start.10 = (f32[64,2048]{1,0:T(8,128)S(1)}, f32[64,2048]{1,0:T(8,128)S(1)}, u32[]{:S(2)}, u32[]{:S(2)}) collective-permute-start(f32[64,2048]{1,0:T(8,128)S(1)} %copy-done.24), channel_id=1, source_target_pairs={{0,4},{1,5},{2,6},{3,7},{4,8},{5,9},{6,10},{7,11},{8,12},{9,13},{1... | collective-permute-start | bytes 1572872 | tf_op jit(solution)/shard_map/ppermute | solution.py:84
  102.5 9.7 %collective-permute-start.39 = (bf16[64,2048]{1,0:T(8,128)(2,1)S(1)}, bf16[64,2048]{1,0:T(8,128)(2,1)S(1)}, u32[]{:S(2)}, u32[]{:S(2)}) collective-permute-start(bf16[64,2048]{1,0:T(8,128)(2,1)S(1)} %add.22), channel_id=1, source_target_pairs={{0,1},{1,0},{2,3},{3,2},{4,5},{5,4},{6,7},{7,6},{8,9},{9,8},{10,11... | collective-permute-start | bytes 786440 | tf_op jit(solution)/shard_map/ppermute | solution.py:76
  106.6 11.2 %collective-permute-start.15 = (bf16[64,2048]{1,0:T(8,128)(2,1)S(1)}, bf16[64,2048]{1,0:T(8,128)(2,1)S(1)}, u32[]{:S(2)}, u32[]{:S(2)}) collective-permute-start(bf16[64,2048]{1,0:T(8,128)(2,1)S(1)} %get-tuple-element.46), channel_id=1, source_target_pairs={{0,1},{1,0},{2,3},{3,2},{4,5},{5,4},{6,7},{7,6},{8,9},{9,8},{10,11... | collective-permute-start | bytes 786440 | tf_op jit(solution)/shard_map/ppermute | solution.py:76
  108.1 9.8 %collective-permute-start.17 = (bf16[64,2048]{1,0:T(8,128)(2,1)S(1)}, bf16[64,2048]{1,0:T(8,128)(2,1)S(1)}, u32[]{:S(2)}, u32[]{:S(2)}) collective-permute-start(bf16[64,2048]{1,0:T(8,128)(2,1)S(1)} %add.19), channel_id=1, source_target_pairs={{0,2},{1,3},{2,0},{3,1},{4,6},{5,7},{6,4},{7,5},{8,10},{9,11},{10,... | collective-permute-start | bytes 786440 | tf_op jit(solution)/shard_map/ppermute | solution.py:76
  113.8 10.2 %collective-permute-start.42 = (bf16[64,2048]{1,0:T(8,128)(2,1)}, bf16[64,2048]{1,0:T(8,128)(2,1)S(1)}, u32[]{:S(2)}, u32[]{:S(2)}) collective-permute-start(bf16[64,2048]{1,0:T(8,128)(2,1)} %get-tuple-element.67), channel_id=1, source_target_pairs={{0,4},{1,5},{2,6},{3,7},{4,8},{5,9},{6,10},{7,11},{8,12},{9,13},{1... | collective-permute-start | bytes 786440 | tf_op jit(solution)/shard_map/ppermute | solution.py:84
  120.0 15.4 %collective-permute-start.43 = (bf16[64,2048]{1,0:T(8,128)(2,1)}, bf16[64,2048]{1,0:T(8,128)(2,1)}, u32[]{:S(2)}, u32[]{:S(2)}) collective-permute-start(bf16[64,2048]{1,0:T(8,128)(2,1)} %get-tuple-element.67), channel_id=1, source_target_pairs={{0,5},{1,4},{2,7},{3,6},{4,9},{5,8},{6,11},{7,10},{8,13},{9,12},{1... | collective-permute-start | bytes 786440 | tf_op jit(solution)/shard_map/ppermute | solution.py:84
  122.1 18.0 %collective-permute-start.45 = (bf16[64,2048]{1,0:T(8,128)(2,1)}, bf16[64,2048]{1,0:T(8,128)(2,1)}, u32[]{:S(2)}, u32[]{:S(2)}) collective-permute-start(bf16[64,2048]{1,0:T(8,128)(2,1)} %collective-permute-done.44.ry), channel_id=1, source_target_pairs={{0,1},{1,0},{2,3},{3,2},{4,5},{5,4},{6,7},{7,6},{8,9},{9,8},{10,11... | collective-permute-start | bytes 786440 | tf_op jit(solution)/shard_map/ppermute | solution.py:76
  123.5 25.9 %collective-permute-start.19 = (bf16[64,2048]{1,0:T(8,128)(2,1)}, bf16[64,2048]{1,0:T(8,128)(2,1)}, u32[]{:S(2)}, u32[]{:S(2)}) collective-permute-start(bf16[64,2048]{1,0:T(8,128)(2,1)} %get-tuple-element.50), channel_id=1, source_target_pairs={{0,4},{1,5},{2,6},{3,7},{4,8},{5,9},{6,10},{7,11},{8,12},{9,13},{1... | collective-permute-start | bytes 786440 | tf_op jit(solution)/shard_map/ppermute | solution.py:84
  124.7 24.7 %collective-permute-start.21 = (bf16[64,2048]{1,0:T(8,128)(2,1)}, bf16[64,2048]{1,0:T(8,128)(2,1)}, u32[]{:S(2)}, u32[]{:S(2)}) collective-permute-start(bf16[64,2048]{1,0:T(8,128)(2,1)} %get-tuple-element.50), channel_id=1, source_target_pairs={{0,6},{1,7},{2,4},{3,5},{4,10},{5,11},{6,8},{7,9},{8,14},{9,15},{1... | collective-permute-start | bytes 786440 | tf_op jit(solution)/shard_map/ppermute | solution.py:84
  128.6 20.8 %collective-permute-start.22 = (bf16[64,2048]{1,0:T(8,128)(2,1)}, bf16[64,2048]{1,0:T(8,128)(2,1)}, u32[]{:S(2)}, u32[]{:S(2)}) collective-permute-start(bf16[64,2048]{1,0:T(8,128)(2,1)} %collective-permute-done.20.rx), channel_id=1, source_target_pairs={{0,2},{1,3},{2,0},{3,1},{4,6},{5,7},{6,4},{7,5},{8,10},{9,11},{10,... | collective-permute-start | bytes 786440 | tf_op jit(solution)/shard_map/ppermute | solution.py:76
  135.5 25.1 %collective-permute-start.41 = (f32[64,2048]{1,0:T(8,128)}, f32[64,2048]{1,0:T(8,128)S(1)}, u32[]{:S(2)}, u32[]{:S(2)}) collective-permute-start(f32[64,2048]{1,0:T(8,128)} %copy-done.27), channel_id=1, source_target_pairs={{0,4},{1,5},{2,6},{3,7},{4,8},{5,9},{6,10},{7,11},{8,12},{9,13},{1... | collective-permute-start | bytes 1572872 | tf_op jit(solution)/shard_map/ppermute | solution.py:84
  154.1 12.4 %collective-permute-start.18 = (f32[64,2048]{1,0:T(8,128)S(1)}, f32[64,2048]{1,0:T(8,128)S(1)}, u32[]{:S(2)}, u32[]{:S(2)}) collective-permute-start(f32[64,2048]{1,0:T(8,128)S(1)} %copy-done.26), channel_id=1, source_target_pairs={{0,4},{1,5},{2,6},{3,7},{4,8},{5,9},{6,10},{7,11},{8,12},{9,13},{1... | collective-permute-start | bytes 1572872 | tf_op jit(solution)/shard_map/ppermute | solution.py:84
  155.4 10.1 %collective-permute-start.47 = (bf16[64,2048]{1,0:T(8,128)(2,1)S(1)}, bf16[64,2048]{1,0:T(8,128)(2,1)S(1)}, u32[]{:S(2)}, u32[]{:S(2)}) collective-permute-start(bf16[64,2048]{1,0:T(8,128)(2,1)S(1)} %add.23), channel_id=1, source_target_pairs={{0,1},{1,0},{2,3},{3,2},{4,5},{5,4},{6,7},{7,6},{8,9},{9,8},{10,11... | collective-permute-start | bytes 786440 | tf_op jit(solution)/shard_map/ppermute | solution.py:76
  159.9 11.1 %collective-permute-start.23 = (bf16[64,2048]{1,0:T(8,128)(2,1)S(1)}, bf16[64,2048]{1,0:T(8,128)(2,1)S(1)}, u32[]{:S(2)}, u32[]{:S(2)}) collective-permute-start(bf16[64,2048]{1,0:T(8,128)(2,1)S(1)} %get-tuple-element.52), channel_id=1, source_target_pairs={{0,1},{1,0},{2,3},{3,2},{4,5},{5,4},{6,7},{7,6},{8,9},{9,8},{10,11... | collective-permute-start | bytes 786440 | tf_op jit(solution)/shard_map/ppermute | solution.py:76
  160.5 10.4 %collective-permute-start.25 = (bf16[64,2048]{1,0:T(8,128)(2,1)S(1)}, bf16[64,2048]{1,0:T(8,128)(2,1)S(1)}, u32[]{:S(2)}, u32[]{:S(2)}) collective-permute-start(bf16[64,2048]{1,0:T(8,128)(2,1)S(1)} %add.20), channel_id=1, source_target_pairs={{0,2},{1,3},{2,0},{3,1},{4,6},{5,7},{6,4},{7,5},{8,10},{9,11},{10,... | collective-permute-start | bytes 786440 | tf_op jit(solution)/shard_map/ppermute | solution.py:76
  166.5 10.4 %collective-permute-start.49 = (f32[64,2048]{1,0:T(8,128)S(1)}, f32[64,2048]{1,0:T(8,128)S(1)}, u32[]{:S(2)}, u32[]{:S(2)}) collective-permute-start(f32[64,2048]{1,0:T(8,128)S(1)} %get-tuple-element.72), channel_id=1, source_target_pairs={{0,4},{1,5},{2,6},{3,7},{4,8},{5,9},{6,10},{7,11},{8,12},{9,13},{1... | collective-permute-start | bytes 1572872 | tf_op jit(solution)/shard_map/ppermute | solution.py:84
  171.9 10.6 %collective-permute-start.26 = (f32[64,2048]{1,0:T(8,128)S(1)}, f32[64,2048]{1,0:T(8,128)S(1)}, u32[]{:S(2)}, u32[]{:S(2)}) collective-permute-start(f32[64,2048]{1,0:T(8,128)S(1)} %get-tuple-element.55), channel_id=1, source_target_pairs={{0,4},{1,5},{2,6},{3,7},{4,8},{5,9},{6,10},{7,11},{8,12},{9,13},{1... | collective-permute-start | bytes 1572872 | tf_op jit(solution)/shard_map/ppermute | solution.py:84
  (54 other events, 448.9 us)

commit v2 on v1

v2 whole, which is shorter than its diff:
```python
import functools

import jax
import jax.numpy as jnp
from jax import lax
from jax.experimental import pallas as pl
from jax.experimental.pallas import tpu as pltpu
from jax.sharding import PartitionSpec as P

TOP = 2
STEPS = 3
SIZES = (64, 64)
MODE = ("rows", "rows")
LAST = ("whole", "whole")
CARRY = (False, False)
LIMIT = 16 * 1024 * 1024


def order(k):
    for step in range(STEPS):
        for what in range(4):
            for c in range(k):
                yield what, step + what // 3, c


def shifted(x, axis, by):
    count = lax.axis_size(axis)
    return lax.ppermute(x, axis, [(i, (i + by) % count) for i in range(count)])


def rms_normed(current, gain_row):
    inv_rms = lax.rsqrt(jnp.mean(current * current, axis=-1, keepdims=True) + 1e-06)
    return (current * inv_rms * gain_row).astype(jnp.bfloat16)


def expert_ffn(rows_in, gate_mat, up_mat, down_mat):
    gate_part = jnp.dot(rows_in, gate_mat, preferred_element_type=jnp.float32)
    upward = jnp.dot(rows_in, up_mat, preferred_element_type=jnp.float32)
    hidden = (jax.nn.silu(gate_part) * upward).astype(jnp.bfloat16)
    return jnp.dot(hidden, down_mat, preferred_element_type=jnp.float32).astype(jnp.bfloat16)


def layer_by_slots(token_rows, gain_row, chosen, slot_rows, weights_in, experts, cap, mats):
    normed = rms_normed(token_rows, gain_row)
    flat_place = chosen * cap + slot_rows
    place_iota = jnp.arange(experts * cap, dtype=jnp.int32)
    tables = [
        (flat_place[:, k : k + 1] == place_iota[None, :]).astype(jnp.bfloat16) for k in range(TOP)
    ]
    occupied = tables[0] + tables[1]
    send = lax.dot_general(
        occupied, normed, (((0,), (0,)), ((), ())), preferred_element_type=jnp.float32
    )
    send = send.astype(jnp.bfloat16).reshape(experts, cap, normed.shape[1])
    received = lax.all_to_all(send, "expert", split_axis=0, concat_axis=0, tiled=True)
    result = expert_ffn(received.reshape(experts * cap, normed.shape[1]), *mats)
    returned = lax.all_to_all(
        result.reshape(send.shape), "expert", split_axis=0, concat_axis=0, tiled=True
    ).reshape(experts * cap, normed.shape[1])
    combined = jnp.zeros(token_rows.shape, jnp.float32)
    for k in range(TOP):
        picked = jnp.dot(tables[k], returned, preferred_element_type=jnp.float32)
        combined = combined + weights_in[:, k : k + 1] * picked
    return token_rows + combined


def run_by_slots(residual, norm_gain, mats, route_ids, route_slots, combine_weights):
    experts = lax.axis_size("expert")
    cap = 4 * residual.shape[1] // experts
    current = residual[0]
    for step in range(STEPS):
        current = layer_by_slots(
            current,
            norm_gain[0],
            route_ids[step, 0],
            route_slots[step, 0],
            combine_weights[step, 0],
            experts,
            cap,
            mats,
        )
        current = shifted(current, "section", 1)
    return current[None]


def across(x, bits):
    return lax.ppermute(x, "expert", [(e, e ^ bits) for e in range(4)])


def onward(x, bits, by=1):
    sections = lax.axis_size("section")
    pairs = [
        (s * 4 + e, ((s + by) % sections) * 4 + (e ^ bits)) for s in range(sections) for e in range(4)
    ]
    return lax.ppermute(x, ("section", "expert"), pairs)


def normed_of(x, gain):
    inv_rms = lax.rsqrt(jnp.mean(x * x, axis=-1, keepdims=True) + 1e-06)
    return (x * inv_rms * gain).astype(jnp.bfloat16)


VMEM_SPEC = pl.BlockSpec(memory_space=pltpu.VMEM)
SMEM_SPEC = pl.BlockSpec(memory_space=pltpu.SMEM)
ANY_SPEC = pl.BlockSpec(memory_space=pl.ANY)
MARK = jax.ShapeDtypeStruct((8, 128), jnp.float32)


def call(kernel, outs, ins, specs, flops, moved, exps=0, scratch=()):
    return pl.pallas_call(
        kernel,
        in_specs=specs,
        out_shape=outs,
        scratch_shapes=scratch,
        compiler_params=pltpu.CompilerParams(vmem_limit_bytes=LIMIT),
        cost_estimate=pl.CostEstimate(flops=flops, bytes_accessed=moved, transcendentals=exps),
    )(*ins)


def far(x):
    return pltpu.with_memory_space_constraint(x, pltpu.HBM)


def bf16_rows(n, width):
    return jax.ShapeDtypeStruct((n, width), jnp.bfloat16)


def f32_rows(n, width):
    return jax.ShapeDtypeStruct((n, width), jnp.float32)


def start_kernel(me_ref, x_far, gain_far, ids_far, combine_far, *refs):
    x_refs, refs = refs[: len(SIZES)], refs[len(SIZES) :]
    normed_refs, refs = refs[: len(SIZES)], refs[len(SIZES) :]
    weight_refs, (mark, gain, ids, combine, sems) = refs[:4], refs[4:]
    copies = []
    at = 0
    for c, n in enumerate(SIZES):
        rows = x_far.at[0, pl.ds(at, n)]
        copies.append(pltpu.make_async_copy(rows, x_refs[c], sems.at[c]))
        at += n
    others = ((gain_far, gain), (ids_far, ids), (combine_far, combine))
    for j, (src, dst) in enumerate(others):
        copies.append(pltpu.make_async_copy(src, dst, sems.at[len(SIZES) + j]))
    for copy in copies:
        copy.start()
    mark[...] = jnp.zeros_like(mark)
    for copy in copies:
        copy.wait()
    for c in range(len(SIZES)):
        normed_refs[c][...] = normed_of(x_refs[c][...], gain[...])
    me = me_ref[0]
    for bits, out in enumerate(weight_refs):
        for step in range(STEPS):
            named = ids[step] == (me ^ bits)
            out[step : step + 1] = jnp.sum(
                jnp.where(named, combine[step], 0.0), axis=0, keepdims=True
            )


def start_rows(me, x, gain, ids, combine):
    width = x.shape[-1]
    outs = [f32_rows(n, width) for n in SIZES] + [bf16_rows(n, width) for n in SIZES]
    outs += [jax.ShapeDtypeStruct((STEPS, ids.shape[-1]), jnp.float32)] * 4 + [MARK]
    scratch = [
        pltpu.VMEM(gain.shape, jnp.float32),
        pltpu.VMEM(ids.shape, jnp.int32),
        pltpu.VMEM(combine.shape, jnp.float32),
        pltpu.SemaphoreType.DMA((len(SIZES) + 3,)),
    ]
    ins = (me, *(far(v) for v in (x, gain, ids, combine)))
    specs = [SMEM_SPEC] + [ANY_SPEC] * 4
    return call(start_kernel, outs, ins, specs, 5 * x.size, 6 * x.size, scratch=scratch)


def load_kernel(*refs):
    sems = refs[-1]
    mats, outs = refs[:3], refs[-4:-1]
    copies = [pltpu.make_async_copy(m, o, sems.at[j]) for j, (m, o) in enumerate(zip(mats, outs))]
    for copy in copies:
        copy.start()
    for copy in copies:
        copy.wait()


def load_mats(mats, before):
    outs = [pltpu.VMEM(m.shape, m.dtype) for m in mats]
    ins = (*(far(m) for m in mats), *before)
    size = sum(2 * m.size for m in mats)
    scratch = [pltpu.SemaphoreType.DMA((3,))]
    return call(load_kernel, outs, ins, [ANY_SPEC] * len(ins), 0, 2 * size, scratch=scratch)


def add_kernel(a_ref, b_ref, before, out_ref, mark):
    del before
    f32 = jnp.float32
    out_ref[...] = (a_ref[...].astype(f32) + b_ref[...].astype(f32)).astype(jnp.bfloat16)
    mark[...] = jnp.zeros_like(mark)


def add_rows(a, b, before):
    specs = [VMEM_SPEC] * 2 + [ANY_SPEC]
    outs = (bf16_rows(*a.shape), MARK)
    return call(add_kernel, outs, (a, b, before), specs, a.size, 6 * a.size)


def summed(x_ref, own_ref, a_ref, b_ref):
    f32 = jnp.float32
    return x_ref[...] + (own_ref[...].astype(f32) + a_ref[...].astype(f32) + b_ref[...].astype(f32))


def total_kernel(x_ref, own_ref, a_ref, b_ref, gain_ref, before, new_ref, normed_ref, mark):
    del before
    x = summed(x_ref, own_ref, a_ref, b_ref)
    new_ref[...] = x
    normed_ref[...] = normed_of(x, gain_ref[...])
    mark[...] = jnp.zeros_like(mark)


def total_rows(x, sums, gain, before):
    n, width = x.shape
    outs = [f32_rows(n, width), bf16_rows(n, width), MARK]
    specs = [VMEM_SPEC] * 5 + [ANY_SPEC]
    return call(total_kernel, outs, (x, *sums, gain, before), specs, 8 * n * width, 16 * n * width)


def add_total_kernel(x_ref, own_ref, a_ref, b_ref, before, new_ref, mark):
    del before
    new_ref[...] = summed(x_ref, own_ref, a_ref, b_ref)
    mark[...] = jnp.zeros_like(mark)


def add_total(x, sums, before):
    outs = [f32_rows(*x.shape), MARK]
    specs = [VMEM_SPEC] * 4 + [ANY_SPEC]
    return call(add_total_kernel, outs, (x, *sums, before), specs, 3 * x.size, 16 * x.size)


def renorm_kernel(x_ref, gain_ref, before, normed_ref, mark):
    del before
    normed_ref[...] = normed_of(x_ref[...], gain_ref[...])
    mark[...] = jnp.zeros_like(mark)


def renorm(x, gain, before):
    outs = [bf16_rows(*x.shape), MARK]
    return call(renorm_kernel, outs, (x, gain, before), [VMEM_SPEC] * 2 + [ANY_SPEC], 5 * x.size, 6 * x.size)


def final_kernel(counts, *refs):
    out = refs[-1]
    at = i = 0
    for n, count in zip(SIZES, counts):
        out[0, at : at + n] = refs[i][...] if count == 1 else summed(*refs[i : i + 4])
        at += n
        i += count


def final_rows(groups, shape):
    out = jax.ShapeDtypeStruct(shape, jnp.float32)
    size = shape[1] * shape[2]
    ins = [v for group in groups for v in group]
    kernel = functools.partial(final_kernel, tuple(len(group) for group in groups))
    return call(kernel, out, ins, [VMEM_SPEC] * len(ins), 3 * size, 14 * size)


def ffn_kernel(step, first, keep, own, rx, ry, rd, w0, w1, w2, w3, gate, up, down, before, *rest):
    del before
    f32 = jnp.float32
    n = own.shape[0]
    token = lax.broadcasted_iota(jnp.int32, (n, w0.shape[1]), 1)
    here = token == first + lax.broadcasted_iota(jnp.int32, (n, w0.shape[1]), 0)
    weight = [
        jnp.sum(jnp.where(here, w[step : step + 1], 0.0), axis=1, keepdims=True)
        for w in (w0, w1, w2, w3)
    ]
    weight = jnp.concatenate(weight, axis=0)
    rows = jnp.concatenate([own[...], rx[...], ry[...], rd[...]], axis=0)
    gate_part = jnp.dot(rows, gate[...], preferred_element_type=f32)
    upward = jnp.dot(rows, up[...], preferred_element_type=f32)
    silu = gate_part / (1.0 + jnp.exp(-gate_part))
    hidden = (silu * upward * weight).astype(jnp.bfloat16)
    out = jnp.dot(hidden, down[...], preferred_element_type=f32).astype(jnp.bfloat16)
    outs = rest[1:] if keep else rest
    for j in range(4):
        outs[j][...] = out[j * n : (j + 1) * n]
    outs[4][...] = jnp.zeros_like(outs[4])
    if keep:
        outs[5][...] = rest[0][...]


def weighted_ffn(step, first, pieces, weights, mats, before, carried=None):
    n, width = pieces[0].shape
    wide = mats[0].shape[1]
    macs = 4 * n * mats[0].size * 3
    keep = carried is not None
    kernel = functools.partial(ffn_kernel, step, first, keep)
    outs = [bf16_rows(n, width)] * 4 + [MARK]
    ins = (*pieces, *weights, *mats, before)
    specs = [VMEM_SPEC] * 11 + [ANY_SPEC]
    if keep:
        outs.append(f32_rows(n, width))
        ins += (carried,)
        specs.append(VMEM_SPEC)
    return call(kernel, outs, ins, specs, 2 * macs, 16 * n * width, 4 * n * wide)


def run_by_rows(residual, norm_gain, mats, route_ids, combine_weights):
    me = lax.axis_index("expert").reshape(1)
    sections = lax.axis_size("section")
    chunks = range(len(SIZES))
    starts = [sum(SIZES[:c]) for c in chunks]
    ids, combine = (jnp.transpose(v[:, 0], (0, 2, 1)) for v in (route_ids, combine_weights))
    outs = start_rows(me, residual, norm_gain, ids, combine)
    k = len(SIZES)
    xs, owns, weights, mark = list(outs[:k]), outs[k : 2 * k], outs[2 * k : 2 * k + 4], outs[-1]
    firsts = [(own, across(own, 1), across(own, 2)) for own in owns]
    weights = [weights[0], *(across(weights[bits], bits) for bits in (1, 2, 3))]
    next_gain = lax.ppermute(norm_gain, "section", [((i + 1) % sections, i) for i in range(sections)])
    mats = load_mats(mats, (mark,))
    state = {"mark": mark}
    sums = {}

    def way(step, c):
        return LAST[c] if step == STEPS - 1 else MODE[c]

    for c in chunks:
        if way(0, c) == "sums":
            xs[c] = onward(xs[c], 0)

    def apply_experts(step, c):
        own, rx, ry = firsts[c]
        rd = across(rx, 2) if c % 2 == 0 else across(ry, 1)
        carried = xs[c] if step and CARRY[c] else None
        outs = weighted_ffn(step, starts[c], (own, rx, ry, rd), weights, mats, state["mark"], carried)
        o_own, o_x, o_y, o_d, state["mark"] = outs[:5]
        if carried is not None:
            xs[c] = onward(outs[5], 0, hops(step, c))
        mine, other, bits = (o_y, o_x, 1) if c % 2 == 0 else (o_x, o_y, 2)
        part = across(o_d, bits)
        if way(step, c) == "sums":
            sums[c] = (onward(o_own, 0), onward(other, bits), mine, part)
        else:
            sums[c] = (o_own, across(other, bits), mine, part)

    def hops(step, c):
        before, now = way(step - 1, c), way(step, c)
        return (before != "sums") + (now == "sums")

    def pass_sum(step, c):
        own, got, mine, part = sums[c]
        both, state["mark"] = add_rows(mine, part, state["mark"])
        go = onward if way(step, c) == "sums" else across
        sums[c] = (own, got, go(both, 2 if c % 2 == 0 else 1))

    def move_on(step, c):
        mode = way(step, c)
        if step == STEPS - 1:
            if mode == "sums":
                return
            new, state["mark"] = add_total(xs[c], sums[c], state["mark"])
            sums[c] = ()
            xs[c] = onward(new, 0)
            return
        if mode == "whole":
            new, state["mark"] = add_total(xs[c], sums[c], state["mark"])
            xs[c] = onward(new, 0)
            return
        gain = norm_gain if mode == "sums" else next_gain
        xs[c], normed, state["mark"] = total_rows(xs[c], sums[c], gain, state["mark"])
        if mode == "rows":
            firsts[c] = tuple(onward(normed, bits) for bits in (0, 1, 2))
        else:
            firsts[c] = (normed, across(normed, 1), across(normed, 2))
        if not CARRY[c] and hops(step + 1, c):
            xs[c] = onward(xs[c], 0, hops(step + 1, c))

    def begin(step, c):
        if step < STEPS and way(step - 1, c) == "whole":
            own, state["mark"] = renorm(xs[c], norm_gain, state["mark"])
            firsts[c] = (own, across(own, 1), across(own, 2))

    for what, step, c in order(k):
        (apply_experts, pass_sum, move_on, begin)[what](step, c)
    return final_rows([(xs[c], *sums[c]) for c in chunks], residual.shape)


def per_device(residual, norm_gain, w_gate, w_up, w_down, route_ids, route_slots, combine_weights):
    mats = (w_gate[0, 0], w_up[0, 0], w_down[0, 0])
    if lax.axis_size("expert") == 4:
        return run_by_rows(residual, norm_gain, mats, route_ids, combine_weights)
    return run_by_slots(residual, norm_gain, mats, route_ids, route_slots, combine_weights)


def solution(mesh):
    in_specs = (
        P("section", "expert", None),
        P("section", None),
        P("section", "expert", None, None),
        P("section", "expert", None, None),
        P("section", "expert", None, None),
        P(None, "section", "expert", None),
        P(None, "section", "expert", None),
        P(None, "section", "expert", None),
    )
    out_specs = P("section", "expert", None)
    return jax.shard_map(
        per_device, mesh=mesh, in_specs=in_specs, out_specs=out_specs, check_vma=False
    )
```

time: 184 us -> 162 us (0.88)
  local copies, waits for them, and re-layouts: 26.6 us -> 0.01 us
  waiting for transfers between devices: 72.4 us -> 88.2 us
  Pallas kernels: 30.5 us -> 24.4 us
  other arithmetic: 3.14 us -> 0 us
    unnamed x72 -> x2, local copies, waits for them, and re-layouts: 23.7 us -> 0.01 us
    ppermute x31, waiting for transfers between devices: 41.6 us -> 56.1 us  [across(): return lax.ppermute(x, 'expert', [(e, e ^ bits) for e in range(4)])]
    pallas_call x14 -> x21, Pallas kernels: 30.5 us -> 24.4 us  [call(): pl.pallas_call(kernel, in_specs=specs, out_shape=outs, scratch_shapes=scr...]
    ppermute x31, starting transfers between devices: 36.7 us -> 33.1 us  [across(): return lax.ppermute(x, 'expert', [(e, e ^ bits) for e in range(4)])]
    ppermute x18, starting transfers between devices: 13.7 us -> 16.3 us  [onward(): return lax.ppermute(x, ('section', 'expert'), pairs)]
  transfers between devices with their start and end apart: 50 -> 50, of which waited for: 26 -> 29; matrix products, arithmetic and copies ran while one was open for 2% -> 0% of each run, Pallas kernels for 16% -> 13%
where the time goes in v2:
time: 162 us
  waiting for transfers between devices  88.2 us (54%)
  starting transfers between devices  49.4 us (30%)
  Pallas kernels  24.4 us (15%)
    ppermute x31, waiting for transfers between devices, across(): return lax.ppermute(x, 'expert', [(e, e ^ bits) for e in range(4)])  56.1 us
    ppermute x31, starting transfers between devices, across(): return lax.ppermute(x, 'expert', [(e, e ^ bits) for e in range(4)])  33.1 us
    ppermute x18, waiting for transfers between devices, onward(): return lax.ppermute(x, ('section', 'expert'), pairs)  30.7 us
    pallas_call x21, Pallas kernels, call(): pl.pallas_call(kernel, in_specs=specs, out_shape=outs, scratch_shapes=scr...  24.4 us
    ppermute x18, starting transfers between devices, onward(): return lax.ppermute(x, ('section', 'expert'), pairs)  16.3 us
  transfers between devices with their start and end apart: 50, of which 29 were waited for; matrix products, arithmetic and copies ran while one was open for 0% of the time, Pallas kernels for 13%

profile of v2, /device:TPU:0, one launch (start us, length us, event | category | flops | bytes accessed | tf_op | source)
XLA Modules:
  0.0 162.3 jit_solution(1816229652952884267)
XLA Ops:
  1.5 3.0 %collective-permute-start = (bf16[64,2048]{1,0:T(8,128)(2,1)S(1)}, bf16[64,2048]{1,0:T(8,128)(2,1)S(1)}, u32[]{:S(2)}, u32[]{:S(2)}) collective-permute-start(bf16[64,2048]{1,0:T(8,128)(2,1)S(1)} %get-tuple-element.75.own), channel_id=1, source_target_pairs={{0,1},{1,0},{2,3},{3,2},{4,5},{5,4},{6,7},{7,6},{8,9},{9,8},{10,11... | collective-permute-start | bytes 786440 | tf_op jit(solution)/shard_map/ppermute | solution.py:87
  6.5 4.3 %collective-permute-done.rx = bf16[64,2048]{1,0:T(8,128)(2,1)S(1)} collective-permute-done((bf16[64,2048]{1,0:T(8,128)(2,1)S(1)}, bf16[64,2048]{1,0:T(8,128)(2,1)S(1)}, u32[]{:S(2)}, u32[]{:S(2)}) %collective-permute-start) | collective-permute-done | bytes 262176 | tf_op jit(solution)/shard_map/ppermute | solution.py:87
  16.1 9.0 %collective-permute-done.3.w1 = f32[3,128]{1,0:T(4,128)S(1)} collective-permute-done((f32[3,128]{1,0:T(4,128)S(1)}, f32[3,128]{1,0:T(4,128)S(1)}, u32[]{:S(2)}, u32[]{:S(2)}) %collective-permute-start.3) | collective-permute-done | bytes 1568 | tf_op jit(solution)/shard_map/ppermute | solution.py:87
  25.7 3.0 %collective-permute-done.4.w2 = f32[3,128]{1,0:T(4,128)S(1)} collective-permute-done((f32[3,128]{1,0:T(4,128)S(1)}, f32[3,128]{1,0:T(4,128)S(1)}, u32[]{:S(2)}, u32[]{:S(2)}) %collective-permute-start.4) | collective-permute-done | bytes 1568 | tf_op jit(solution)/shard_map/ppermute | solution.py:87
  30.1 3.8 %shard_map.74 = (bf16[2048,768]{1,0:T(8,128)(2,1)S(1)}, bf16[2048,768]{1,0:T(8,128)(2,1)S(1)}, bf16[768,2048]{1,0:T(8,128)(2,1)S(1)}) custom-call(bf16[2048,768]{1,0:T(8,128)(2,1)} %bitcast.10, bf16[2048,768]{1,0:T(8,128)(2,1)} %bitcast.11, bf16[768,2048]{1,0:T(8,128)(2,1)} %bitcast.12, f32[8,128]{1,0:T(8,128)S(1)} %get-tuple-element.80.refs_3_.before), custom_call_target="tpu_custom_call" | custom-call | bytes 18874368 | tf_op jit(solution)/shard_map/pallas_call | solution.py:110
  33.9 2.6 %shard_map.75 = (bf16[64,2048]{1,0:T(8,128)(2,1)S(1)}, bf16[64,2048]{1,0:T(8,128)(2,1)S(1)}, bf16[64,2048]{1,0:T(8,128)(2,1)S(1)}, bf16[64,2048]{1,0:T(8,128)(2,1)S(1)}, f32[8,128]{1,0:T(8,128)S(1)}) custom-call(bf16[64,2048]{1,0:T(8,128)(2,1)S(1)} %get-tuple-element.75.own, bf16[64,2048]{1,0:T(8,128)(2,1)S(1)} %collective-permute-done.rx, ...), custom_call_target="tpu_custom_call" | custom-call | flops 2415919104 | bytes 2097152 | tf_op jit(solution)/shard_map/pallas_call | solution.py:110
  37.4 2.7 %shard_map.76 = (bf16[64,2048]{1,0:T(8,128)(2,1)S(1)}, bf16[64,2048]{1,0:T(8,128)(2,1)S(1)}, bf16[64,2048]{1,0:T(8,128)(2,1)S(1)}, bf16[64,2048]{1,0:T(8,128)(2,1)S(1)}, f32[8,128]{1,0:T(8,128)S(1)}) custom-call(bf16[64,2048]{1,0:T(8,128)(2,1)S(1)} %get-tuple-element.88.own, bf16[64,2048]{1,0:T(8,128)(2,1)S(1)} %collective-permute-done.8.rx, ...), custom_call_target="tpu_custom_call" | custom-call | flops 2415919104 | bytes 2097152 | tf_op jit(solution)/shard_map/pallas_call | solution.py:110
  43.0 2.8 %collective-permute-done.7.b_ref = bf16[64,2048]{1,0:T(8,128)(2,1)S(1)} collective-permute-done((bf16[64,2048]{1,0:T(8,128)(2,1)S(1)}, bf16[64,2048]{1,0:T(8,128)(2,1)S(1)}, u32[]{:S(2)}, u32[]{:S(2)}) %collective-permute-start.7) | collective-permute-done | bytes 262176 | tf_op jit(solution)/shard_map/ppermute | solution.py:87
  57.0 2.0 %collective-permute-start.17 = (bf16[64,2048]{1,0:T(8,128)(2,1)S(1)}, bf16[64,2048]{1,0:T(8,128)(2,1)S(1)}, u32[]{:S(2)}, u32[]{:S(2)}) collective-permute-start(bf16[64,2048]{1,0:T(8,128)(2,1)S(1)} %get-tuple-element.97), channel_id=1, source_target_pairs={{0,6},{1,7},{2,4},{3,5},{4,10},{5,11},{6,8},{7,9},{8,14},{9,15},{1... | collective-permute-start | bytes 786440 | tf_op jit(solution)/shard_map/ppermute | solution.py:95
  59.0 3.0 %collective-permute-done.16.rx = bf16[64,2048]{1,0:T(8,128)(2,1)S(1)} collective-permute-done((bf16[64,2048]{1,0:T(8,128)(2,1)S(1)}, bf16[64,2048]{1,0:T(8,128)(2,1)S(1)}, u32[]{:S(2)}, u32[]{:S(2)}) %collective-permute-start.16) | collective-permute-done | bytes 262176 | tf_op jit(solution)/shard_map/ppermute | solution.py:95
  65.4 6.7 %collective-permute-done.17.ry = bf16[64,2048]{1,0:T(8,128)(2,1)S(1)} collective-permute-done((bf16[64,2048]{1,0:T(8,128)(2,1)S(1)}, bf16[64,2048]{1,0:T(8,128)(2,1)S(1)}, u32[]{:S(2)}, u32[]{:S(2)}) %collective-permute-start.17) | collective-permute-done | bytes 262176 | tf_op jit(solution)/shard_map/ppermute | solution.py:95
  72.1 2.2 %collective-permute-start.14 = (f32[64,2048]{1,0:T(8,128)S(1)}, f32[64,2048]{1,0:T(8,128)S(1)}, u32[]{:S(2)}, u32[]{:S(2)}) collective-permute-start(f32[64,2048]{1,0:T(8,128)S(1)} %get-tuple-element.96), channel_id=1, source_target_pairs={{0,4},{1,5},{2,6},{3,7},{4,8},{5,9},{6,10},{7,11},{8,12},{9,13},{1... | collective-permute-start | bytes 1572872 | tf_op jit(solution)/shard_map/ppermute | solution.py:95
  75.9 2.7 %shard_map.81 = (bf16[64,2048]{1,0:T(8,128)(2,1)S(1)}, bf16[64,2048]{1,0:T(8,128)(2,1)S(1)}, bf16[64,2048]{1,0:T(8,128)(2,1)S(1)}, bf16[64,2048]{1,0:T(8,128)(2,1)S(1)}, f32[8,128]{1,0:T(8,128)S(1)}) custom-call(bf16[64,2048]{1,0:T(8,128)(2,1)S(1)} %collective-permute-done.15.own, bf16[64,2048]{1,0:T(8,128)(2,1)S(1)} %collective-permute-done.16.rx, ...), custom_call_target="tpu_custom_call" | custom-call | flops 2415919104 | bytes 2097152 | tf_op jit(solution)/shard_map/pallas_call | solution.py:110
  81.3 2.7 %shard_map.82 = (bf16[64,2048]{1,0:T(8,128)(2,1)S(1)}, bf16[64,2048]{1,0:T(8,128)(2,1)S(1)}, bf16[64,2048]{1,0:T(8,128)(2,1)S(1)}, bf16[64,2048]{1,0:T(8,128)(2,1)S(1)}, f32[8,128]{1,0:T(8,128)S(1)}) custom-call(bf16[64,2048]{1,0:T(8,128)(2,1)S(1)} %collective-permute-done.23.own, bf16[64,2048]{1,0:T(8,128)(2,1)S(1)} %collective-permute-done.24.rx, ...), custom_call_target="tpu_custom_call" | custom-call | flops 2415919104 | bytes 2097152 | tf_op jit(solution)/shard_map/pallas_call | solution.py:110
  87.1 6.2 %collective-permute-done.28.b_ref = bf16[64,2048]{1,0:T(8,128)(2,1)S(1)} collective-permute-done((bf16[64,2048]{1,0:T(8,128)(2,1)S(1)}, bf16[64,2048]{1,0:T(8,128)(2,1)S(1)}, u32[]{:S(2)}, u32[]{:S(2)}) %collective-permute-start.28) | collective-permute-done | bytes 262176 | tf_op jit(solution)/shard_map/ppermute | solution.py:87
  93.3 2.1 %collective-permute-start.36 = (bf16[64,2048]{1,0:T(8,128)(2,1)S(1)}, bf16[64,2048]{1,0:T(8,128)(2,1)S(1)}, u32[]{:S(2)}, u32[]{:S(2)}) collective-permute-start(bf16[64,2048]{1,0:T(8,128)(2,1)S(1)} %get-tuple-element.121), channel_id=1, source_target_pairs={{0,1},{1,0},{2,3},{3,2},{4,5},{5,4},{6,7},{7,6},{8,9},{9,8},{10,11... | collective-permute-start | bytes 786440 | tf_op jit(solution)/shard_map/ppermute | solution.py:87
  95.5 3.4 %collective-permute-done.27.b_ref = bf16[64,2048]{1,0:T(8,128)(2,1)S(1)} collective-permute-done((bf16[64,2048]{1,0:T(8,128)(2,1)S(1)}, bf16[64,2048]{1,0:T(8,128)(2,1)S(1)}, u32[]{:S(2)}, u32[]{:S(2)}) %collective-permute-start.27) | collective-permute-done | bytes 262176 | tf_op jit(solution)/shard_map/ppermute | solution.py:87
  99.2 3.9 %collective-permute-done.35.a_ref = bf16[64,2048]{1,0:T(8,128)(2,1)S(1)} collective-permute-done((bf16[64,2048]{1,0:T(8,128)(2,1)S(1)}, bf16[64,2048]{1,0:T(8,128)(2,1)S(1)}, u32[]{:S(2)}, u32[]{:S(2)}) %collective-permute-start.35) | collective-permute-done | bytes 262176 | tf_op jit(solution)/shard_map/ppermute | solution.py:87
  103.4 3.2 %collective-permute-start.32 = (bf16[64,2048]{1,0:T(8,128)(2,1)S(1)}, bf16[64,2048]{1,0:T(8,128)(2,1)S(1)}, u32[]{:S(2)}, u32[]{:S(2)}) collective-permute-start(bf16[64,2048]{1,0:T(8,128)(2,1)S(1)} %get-tuple-element.117), channel_id=1, source_target_pairs={{0,6},{1,7},{2,4},{3,5},{4,10},{5,11},{6,8},{7,9},{8,14},{9,15},{1... | collective-permute-start | bytes 786440 | tf_op jit(solution)/shard_map/ppermute | solution.py:95
  107.7 2.0 %collective-permute-start.40 = (bf16[64,2048]{1,0:T(8,128)(2,1)S(1)}, bf16[64,2048]{1,0:T(8,128)(2,1)S(1)}, u32[]{:S(2)}, u32[]{:S(2)}) collective-permute-start(bf16[64,2048]{1,0:T(8,128)(2,1)S(1)} %get-tuple-element.128), channel_id=1, source_target_pairs={{0,5},{1,4},{2,7},{3,6},{4,9},{5,8},{6,11},{7,10},{8,13},{9,12},{1... | collective-permute-start | bytes 786440 | tf_op jit(solution)/shard_map/ppermute | solution.py:95
  109.7 2.3 %collective-permute-done.41.ry = bf16[64,2048]{1,0:T(8,128)(2,1)S(1)} collective-permute-done((bf16[64,2048]{1,0:T(8,128)(2,1)S(1)}, bf16[64,2048]{1,0:T(8,128)(2,1)S(1)}, u32[]{:S(2)}, u32[]{:S(2)}) %collective-permute-start.41) | collective-permute-done | bytes 262176 | tf_op jit(solution)/shard_map/ppermute | solution.py:95
  112.0 6.5 %collective-permute-done.32.ry = bf16[64,2048]{1,0:T(8,128)(2,1)S(1)} collective-permute-done((bf16[64,2048]{1,0:T(8,128)(2,1)S(1)}, bf16[64,2048]{1,0:T(8,128)(2,1)S(1)}, u32[]{:S(2)}, u32[]{:S(2)}) %collective-permute-start.32) | collective-permute-done | bytes 262176 | tf_op jit(solution)/shard_map/ppermute | solution.py:95
  118.8 1.9 %collective-permute-start.29 = (f32[64,2048]{1,0:T(8,128)S(1)}, f32[64,2048]{1,0:T(8,128)S(1)}, u32[]{:S(2)}, u32[]{:S(2)}) collective-permute-start(f32[64,2048]{1,0:T(8,128)S(1)} %get-tuple-element.116), channel_id=1, source_target_pairs={{0,4},{1,5},{2,6},{3,7},{4,8},{5,9},{6,10},{7,11},{8,12},{9,13},{1... | collective-permute-start | bytes 1572872 | tf_op jit(solution)/shard_map/ppermute | solution.py:95
  120.8 2.0 %collective-permute-done.33.rd = bf16[64,2048]{1,0:T(8,128)(2,1)S(1)} collective-permute-done((bf16[64,2048]{1,0:T(8,128)(2,1)S(1)}, bf16[64,2048]{1,0:T(8,128)(2,1)S(1)}, u32[]{:S(2)}, u32[]{:S(2)}) %collective-permute-start.33) | collective-permute-done | bytes 262176 | tf_op jit(solution)/shard_map/ppermute | solution.py:87
  122.8 2.7 %shard_map.87 = (bf16[64,2048]{1,0:T(8,128)(2,1)S(1)}, bf16[64,2048]{1,0:T(8,128)(2,1)S(1)}, bf16[64,2048]{1,0:T(8,128)(2,1)S(1)}, bf16[64,2048]{1,0:T(8,128)(2,1)S(1)}, f32[8,128]{1,0:T(8,128)S(1)}) custom-call(bf16[64,2048]{1,0:T(8,128)(2,1)S(1)} %collective-permute-done.30.own, bf16[64,2048]{1,0:T(8,128)(2,1)S(1)} %collective-permute-done.31.rx, ...), custom_call_target="tpu_custom_call" | custom-call | flops 2415919104 | bytes 2097152 | tf_op jit(solution)/shard_map/pallas_call | solution.py:110
  127.6 2.7 %shard_map.88 = (bf16[64,2048]{1,0:T(8,128)(2,1)S(1)}, bf16[64,2048]{1,0:T(8,128)(2,1)S(1)}, bf16[64,2048]{1,0:T(8,128)(2,1)S(1)}, bf16[64,2048]{1,0:T(8,128)(2,1)S(1)}, f32[8,128]{1,0:T(8,128)S(1)}) custom-call(bf16[64,2048]{1,0:T(8,128)(2,1)S(1)} %collective-permute-done.39.own, bf16[64,2048]{1,0:T(8,128)(2,1)S(1)} %collective-permute-done.40.rx, ...), custom_call_target="tpu_custom_call" | custom-call | flops 2415919104 | bytes 2097152 | tf_op jit(solution)/shard_map/pallas_call | solution.py:110
  134.0 5.5 %collective-permute-done.44.b_ref = bf16[64,2048]{1,0:T(8,128)(2,1)S(1)} collective-permute-done((bf16[64,2048]{1,0:T(8,128)(2,1)S(1)}, bf16[64,2048]{1,0:T(8,128)(2,1)S(1)}, u32[]{:S(2)}, u32[]{:S(2)}) %collective-permute-start.44) | collective-permute-done | bytes 262176 | tf_op jit(solution)/shard_map/ppermute | solution.py:87
  139.6 2.4 %collective-permute-start.48 = (bf16[64,2048]{1,0:T(8,128)(2,1)S(1)}, bf16[64,2048]{1,0:T(8,128)(2,1)S(1)}, u32[]{:S(2)}, u32[]{:S(2)}) collective-permute-start(bf16[64,2048]{1,0:T(8,128)(2,1)S(1)} %get-tuple-element.140), channel_id=1, source_target_pairs={{0,1},{1,0},{2,3},{3,2},{4,5},{5,4},{6,7},{7,6},{8,9},{9,8},{10,11... | collective-permute-start | bytes 786440 | tf_op jit(solution)/shard_map/ppermute | solution.py:87
  142.0 3.1 %collective-permute-done.43.b_ref = bf16[64,2048]{1,0:T(8,128)(2,1)S(1)} collective-permute-done((bf16[64,2048]{1,0:T(8,128)(2,1)S(1)}, bf16[64,2048]{1,0:T(8,128)(2,1)S(1)}, u32[]{:S(2)}, u32[]{:S(2)}) %collective-permute-start.43) | collective-permute-done | bytes 262176 | tf_op jit(solution)/shard_map/ppermute | solution.py:87
  145.3 4.7 %collective-permute-done.47.a_ref = bf16[64,2048]{1,0:T(8,128)(2,1)S(1)} collective-permute-done((bf16[64,2048]{1,0:T(8,128)(2,1)S(1)}, bf16[64,2048]{1,0:T(8,128)(2,1)S(1)}, u32[]{:S(2)}, u32[]{:S(2)}) %collective-permute-start.47) | collective-permute-done | bytes 262176 | tf_op jit(solution)/shard_map/ppermute | solution.py:87
  150.7 5.0 %collective-permute-done.45.refs_0_ = f32[64,2048]{1,0:T(8,128)S(1)} collective-permute-done((f32[64,2048]{1,0:T(8,128)S(1)}, f32[64,2048]{1,0:T(8,128)S(1)}, u32[]{:S(2)}, u32[]{:S(2)}) %collective-permute-start.45) | collective-permute-done | bytes 524320 | tf_op jit(solution)/shard_map/ppermute | solution.py:95
  155.6 5.6 %collective-permute-done.49.refs_1_ = f32[64,2048]{1,0:T(8,128)S(1)} collective-permute-done((f32[64,2048]{1,0:T(8,128)S(1)}, f32[64,2048]{1,0:T(8,128)S(1)}, u32[]{:S(2)}, u32[]{:S(2)}) %collective-permute-start.49) | collective-permute-done | bytes 524320 | tf_op jit(solution)/shard_map/ppermute | solution.py:95
  (91 shorter events, 46.4 us)
Async XLA Ops:
  1.5 9.3 %collective-permute-start = (bf16[64,2048]{1,0:T(8,128)(2,1)S(1)}, bf16[64,2048]{1,0:T(8,128)(2,1)S(1)}, u32[]{:S(2)}, u32[]{:S(2)}) collective-permute-start(bf16[64,2048]{1,0:T(8,128)(2,1)S(1)} %get-tuple-element.75.own), channel_id=1, source_target_pairs={{0,1},{1,0},{2,3},{3,2},{4,5},{5,4},{6,7},{7,6},{8,9},{9,8},{10,11... | collective-permute-start | bytes 786440 | tf_op jit(solution)/shard_map/ppermute | solution.py:87
  4.5 9.6 %collective-permute-start.9 = (bf16[64,2048]{1,0:T(8,128)(2,1)S(1)}, bf16[64,2048]{1,0:T(8,128)(2,1)S(1)}, u32[]{:S(2)}, u32[]{:S(2)}) collective-permute-start(bf16[64,2048]{1,0:T(8,128)(2,1)S(1)} %get-tuple-element.88.own), channel_id=1, source_target_pairs={{0,2},{1,3},{2,0},{3,1},{4,6},{5,7},{6,4},{7,5},{8,10},{9,11},{10,... | collective-permute-start | bytes 786440 | tf_op jit(solution)/shard_map/ppermute | solution.py:87
  6.0 27.9 %collective-permute-start.1 = (bf16[64,2048]{1,0:T(8,128)(2,1)S(1)}, bf16[64,2048]{1,0:T(8,128)(2,1)S(1)}, u32[]{:S(2)}, u32[]{:S(2)}) collective-permute-start(bf16[64,2048]{1,0:T(8,128)(2,1)S(1)} %get-tuple-element.75.own), channel_id=1, source_target_pairs={{0,2},{1,3},{2,0},{3,1},{4,6},{5,7},{6,4},{7,5},{8,10},{9,11},{10,... | collective-permute-start | bytes 786440 | tf_op jit(solution)/shard_map/ppermute | solution.py:87
  10.8 23.2 %collective-permute-start.2 = (bf16[64,2048]{1,0:T(8,128)(2,1)S(1)}, bf16[64,2048]{1,0:T(8,128)(2,1)S(1)}, u32[]{:S(2)}, u32[]{:S(2)}) collective-permute-start(bf16[64,2048]{1,0:T(8,128)(2,1)S(1)} %collective-permute-done.rx), channel_id=1, source_target_pairs={{0,2},{1,3},{2,0},{3,1},{4,6},{5,7},{6,4},{7,5},{8,10},{9,11},{10,... | collective-permute-start | bytes 786440 | tf_op jit(solution)/shard_map/ppermute | solution.py:87
  12.6 24.9 %collective-permute-start.8 = (bf16[64,2048]{1,0:T(8,128)(2,1)S(1)}, bf16[64,2048]{1,0:T(8,128)(2,1)S(1)}, u32[]{:S(2)}, u32[]{:S(2)}) collective-permute-start(bf16[64,2048]{1,0:T(8,128)(2,1)S(1)} %get-tuple-element.88.own), channel_id=1, source_target_pairs={{0,1},{1,0},{2,3},{3,2},{4,5},{5,4},{6,7},{7,6},{8,9},{9,8},{10,11... | collective-permute-start | bytes 786440 | tf_op jit(solution)/shard_map/ppermute | solution.py:87
  14.0 23.4 %collective-permute-start.10 = (bf16[64,2048]{1,0:T(8,128)(2,1)S(1)}, bf16[64,2048]{1,0:T(8,128)(2,1)S(1)}, u32[]{:S(2)}, u32[]{:S(2)}) collective-permute-start(bf16[64,2048]{1,0:T(8,128)(2,1)S(1)} %collective-permute-done.9.ry), channel_id=1, source_target_pairs={{0,1},{1,0},{2,3},{3,2},{4,5},{5,4},{6,7},{7,6},{8,9},{9,8},{10,11... | collective-permute-start | bytes 786440 | tf_op jit(solution)/shard_map/ppermute | solution.py:87
  14.6 10.5 %collective-permute-start.3 = (f32[3,128]{1,0:T(4,128)S(1)}, f32[3,128]{1,0:T(4,128)S(1)}, u32[]{:S(2)}, u32[]{:S(2)}) collective-permute-start(f32[3,128]{1,0:T(4,128)S(1)} %get-tuple-element.77), channel_id=1, source_target_pairs={{0,1},{1,0},{2,3},{3,2},{4,5},{5,4},{6,7},{7,6},{8,9},{9,8},{10,11... | collective-permute-start | bytes 4616 | tf_op jit(solution)/shard_map/ppermute | solution.py:87
  41.5 10.7 %collective-permute-start.6 = (bf16[64,2048]{1,0:T(8,128)(2,1)S(1)}, bf16[64,2048]{1,0:T(8,128)(2,1)S(1)}, u32[]{:S(2)}, u32[]{:S(2)}) collective-permute-start(bf16[64,2048]{1,0:T(8,128)(2,1)S(1)} %get-tuple-element.85), channel_id=1, source_target_pairs={{0,1},{1,0},{2,3},{3,2},{4,5},{5,4},{6,7},{7,6},{8,9},{9,8},{10,11... | collective-permute-start | bytes 786440 | tf_op jit(solution)/shard_map/ppermute | solution.py:87
  57.0 15.1 %collective-permute-start.17 = (bf16[64,2048]{1,0:T(8,128)(2,1)S(1)}, bf16[64,2048]{1,0:T(8,128)(2,1)S(1)}, u32[]{:S(2)}, u32[]{:S(2)}) collective-permute-start(bf16[64,2048]{1,0:T(8,128)(2,1)S(1)} %get-tuple-element.97), channel_id=1, source_target_pairs={{0,6},{1,7},{2,4},{3,5},{4,10},{5,11},{6,8},{7,9},{8,14},{9,15},{1... | collective-permute-start | bytes 786440 | tf_op jit(solution)/shard_map/ppermute | solution.py:95
  59.0 13.1 %collective-permute-start.15 = (bf16[64,2048]{1,0:T(8,128)(2,1)S(1)}, bf16[64,2048]{1,0:T(8,128)(2,1)S(1)}, u32[]{:S(2)}, u32[]{:S(2)}) collective-permute-start(bf16[64,2048]{1,0:T(8,128)(2,1)S(1)} %get-tuple-element.97), channel_id=1, source_target_pairs={{0,4},{1,5},{2,6},{3,7},{4,8},{5,9},{6,10},{7,11},{8,12},{9,13},{1... | collective-permute-start | bytes 786440 | tf_op jit(solution)/shard_map/ppermute | solution.py:95
  61.9 14.0 %collective-permute-start.18 = (bf16[64,2048]{1,0:T(8,128)(2,1)S(1)}, bf16[64,2048]{1,0:T(8,128)(2,1)S(1)}, u32[]{:S(2)}, u32[]{:S(2)}) collective-permute-start(bf16[64,2048]{1,0:T(8,128)(2,1)S(1)} %collective-permute-done.16.rx), channel_id=1, source_target_pairs={{0,2},{1,3},{2,0},{3,1},{4,6},{5,7},{6,4},{7,5},{8,10},{9,11},{10,... | collective-permute-start | bytes 786440 | tf_op jit(solution)/shard_map/ppermute | solution.py:87
  63.1 17.1 %collective-permute-start.24 = (bf16[64,2048]{1,0:T(8,128)(2,1)S(1)}, bf16[64,2048]{1,0:T(8,128)(2,1)S(1)}, u32[]{:S(2)}, u32[]{:S(2)}) collective-permute-start(bf16[64,2048]{1,0:T(8,128)(2,1)S(1)} %get-tuple-element.108), channel_id=1, source_target_pairs={{0,5},{1,4},{2,7},{3,6},{4,9},{5,8},{6,11},{7,10},{8,13},{9,12},{1... | collective-permute-start | bytes 786440 | tf_op jit(solution)/shard_map/ppermute | solution.py:95
  65.4 14.8 %collective-permute-start.23 = (bf16[64,2048]{1,0:T(8,128)(2,1)S(1)}, bf16[64,2048]{1,0:T(8,128)(2,1)S(1)}, u32[]{:S(2)}, u32[]{:S(2)}) collective-permute-start(bf16[64,2048]{1,0:T(8,128)(2,1)S(1)} %get-tuple-element.108), channel_id=1, source_target_pairs={{0,4},{1,5},{2,6},{3,7},{4,8},{5,9},{6,10},{7,11},{8,12},{9,13},{1... | collective-permute-start | bytes 786440 | tf_op jit(solution)/shard_map/ppermute | solution.py:95
  72.1 21.2 %collective-permute-start.14 = (f32[64,2048]{1,0:T(8,128)S(1)}, f32[64,2048]{1,0:T(8,128)S(1)}, u32[]{:S(2)}, u32[]{:S(2)}) collective-permute-start(f32[64,2048]{1,0:T(8,128)S(1)} %get-tuple-element.96), channel_id=1, source_target_pairs={{0,4},{1,5},{2,6},{3,7},{4,8},{5,9},{6,10},{7,11},{8,12},{9,13},{1... | collective-permute-start | bytes 1572872 | tf_op jit(solution)/shard_map/ppermute | solution.py:95
  84.0 15.1 %collective-permute-start.34 = (f32[64,2048]{1,0:T(8,128)S(1)}, f32[64,2048]{1,0:T(8,128)S(1)}, u32[]{:S(2)}, u32[]{:S(2)}) collective-permute-start(f32[64,2048]{1,0:T(8,128)S(1)} %get-tuple-element.118), channel_id=1, source_target_pairs={{0,4},{1,5},{2,6},{3,7},{4,8},{5,9},{6,10},{7,11},{8,12},{9,13},{1... | collective-permute-start | bytes 1572872 | tf_op jit(solution)/shard_map/ppermute | solution.py:95
  84.3 11.2 %collective-permute-start.21 = (bf16[64,2048]{1,0:T(8,128)(2,1)S(1)}, bf16[64,2048]{1,0:T(8,128)(2,1)S(1)}, u32[]{:S(2)}, u32[]{:S(2)}) collective-permute-start(bf16[64,2048]{1,0:T(8,128)(2,1)S(1)} %get-tuple-element.105), channel_id=1, source_target_pairs={{0,1},{1,0},{2,3},{3,2},{4,5},{5,4},{6,7},{7,6},{8,9},{9,8},{10,11... | collective-permute-start | bytes 786440 | tf_op jit(solution)/shard_map/ppermute | solution.py:87
  86.7 12.1 %collective-permute-start.27 = (bf16[64,2048]{1,0:T(8,128)(2,1)S(1)}, bf16[64,2048]{1,0:T(8,128)(2,1)S(1)}, u32[]{:S(2)}, u32[]{:S(2)}) collective-permute-start(bf16[64,2048]{1,0:T(8,128)(2,1)S(1)} %get-tuple-element.111), channel_id=1, source_target_pairs={{0,2},{1,3},{2,0},{3,1},{4,6},{5,7},{6,4},{7,5},{8,10},{9,11},{10,... | collective-permute-start | bytes 786440 | tf_op jit(solution)/shard_map/ppermute | solution.py:87
  93.2 9.9 %collective-permute-start.35 = (bf16[64,2048]{1,0:T(8,128)(2,1)S(1)}, bf16[64,2048]{1,0:T(8,128)(2,1)S(1)}, u32[]{:S(2)}, u32[]{:S(2)}) collective-permute-start(bf16[64,2048]{1,0:T(8,128)(2,1)S(1)} %get-tuple-element.120), channel_id=1, source_target_pairs={{0,2},{1,3},{2,0},{3,1},{4,6},{5,7},{6,4},{7,5},{8,10},{9,11},{10,... | collective-permute-start | bytes 786440 | tf_op jit(solution)/shard_map/ppermute | solution.py:87
  93.3 9.8 %collective-permute-start.36 = (bf16[64,2048]{1,0:T(8,128)(2,1)S(1)}, bf16[64,2048]{1,0:T(8,128)(2,1)S(1)}, u32[]{:S(2)}, u32[]{:S(2)}) collective-permute-start(bf16[64,2048]{1,0:T(8,128)(2,1)S(1)} %get-tuple-element.121), channel_id=1, source_target_pairs={{0,1},{1,0},{2,3},{3,2},{4,5},{5,4},{6,7},{7,6},{8,9},{9,8},{10,11... | collective-permute-start | bytes 786440 | tf_op jit(solution)/shard_map/ppermute | solution.py:87
  103.4 15.1 %collective-permute-start.32 = (bf16[64,2048]{1,0:T(8,128)(2,1)S(1)}, bf16[64,2048]{1,0:T(8,128)(2,1)S(1)}, u32[]{:S(2)}, u32[]{:S(2)}) collective-permute-start(bf16[64,2048]{1,0:T(8,128)(2,1)S(1)} %get-tuple-element.117), channel_id=1, source_target_pairs={{0,6},{1,7},{2,4},{3,5},{4,10},{5,11},{6,8},{7,9},{8,14},{9,15},{1... | collective-permute-start | bytes 786440 | tf_op jit(solution)/shard_map/ppermute | solution.py:95
  106.6 12.2 %collective-permute-start.30 = (bf16[64,2048]{1,0:T(8,128)(2,1)S(1)}, bf16[64,2048]{1,0:T(8,128)(2,1)S(1)}, u32[]{:S(2)}, u32[]{:S(2)}) collective-permute-start(bf16[64,2048]{1,0:T(8,128)(2,1)S(1)} %get-tuple-element.117), channel_id=1, source_target_pairs={{0,4},{1,5},{2,6},{3,7},{4,8},{5,9},{6,10},{7,11},{8,12},{9,13},{1... | collective-permute-start | bytes 786440 | tf_op jit(solution)/shard_map/ppermute | solution.py:95
  107.7 15.1 %collective-permute-start.33 = (bf16[64,2048]{1,0:T(8,128)(2,1)S(1)}, bf16[64,2048]{1,0:T(8,128)(2,1)S(1)}, u32[]{:S(2)}, u32[]{:S(2)}) collective-permute-start(bf16[64,2048]{1,0:T(8,128)(2,1)S(1)} %collective-permute-done.31.rx), channel_id=1, source_target_pairs={{0,2},{1,3},{2,0},{3,1},{4,6},{5,7},{6,4},{7,5},{8,10},{9,11},{10,... | collective-permute-start | bytes 786440 | tf_op jit(solution)/shard_map/ppermute | solution.py:87
  107.7 19.1 %collective-permute-start.40 = (bf16[64,2048]{1,0:T(8,128)(2,1)S(1)}, bf16[64,2048]{1,0:T(8,128)(2,1)S(1)}, u32[]{:S(2)}, u32[]{:S(2)}) collective-permute-start(bf16[64,2048]{1,0:T(8,128)(2,1)S(1)} %get-tuple-element.128), channel_id=1, source_target_pairs={{0,5},{1,4},{2,7},{3,6},{4,9},{5,8},{6,11},{7,10},{8,13},{9,12},{1... | collective-permute-start | bytes 786440 | tf_op jit(solution)/shard_map/ppermute | solution.py:95
  112.0 14.8 %collective-permute-start.39 = (bf16[64,2048]{1,0:T(8,128)(2,1)S(1)}, bf16[64,2048]{1,0:T(8,128)(2,1)S(1)}, u32[]{:S(2)}, u32[]{:S(2)}) collective-permute-start(bf16[64,2048]{1,0:T(8,128)(2,1)S(1)} %get-tuple-element.128), channel_id=1, source_target_pairs={{0,4},{1,5},{2,6},{3,7},{4,8},{5,9},{6,10},{7,11},{8,12},{9,13},{1... | collective-permute-start | bytes 786440 | tf_op jit(solution)/shard_map/ppermute | solution.py:95
  118.8 20.7 %collective-permute-start.29 = (f32[64,2048]{1,0:T(8,128)S(1)}, f32[64,2048]{1,0:T(8,128)S(1)}, u32[]{:S(2)}, u32[]{:S(2)}) collective-permute-start(f32[64,2048]{1,0:T(8,128)S(1)} %get-tuple-element.116), channel_id=1, source_target_pairs={{0,4},{1,5},{2,6},{3,7},{4,8},{5,9},{6,10},{7,11},{8,12},{9,13},{1... | collective-permute-start | bytes 1572872 | tf_op jit(solution)/shard_map/ppermute | solution.py:95
  130.3 14.9 %collective-permute-start.46 = (f32[64,2048]{1,0:T(8,128)S(1)}, f32[64,2048]{1,0:T(8,128)S(1)}, u32[]{:S(2)}, u32[]{:S(2)}) collective-permute-start(f32[64,2048]{1,0:T(8,128)S(1)} %get-tuple-element.137), channel_id=1, source_target_pairs={{0,4},{1,5},{2,6},{3,7},{4,8},{5,9},{6,10},{7,11},{8,12},{9,13},{1... | collective-permute-start | bytes 1572872 | tf_op jit(solution)/shard_map/ppermute | solution.py:95
  130.8 11.2 %collective-permute-start.37 = (bf16[64,2048]{1,0:T(8,128)(2,1)S(1)}, bf16[64,2048]{1,0:T(8,128)(2,1)S(1)}, u32[]{:S(2)}, u32[]{:S(2)}) collective-permute-start(bf16[64,2048]{1,0:T(8,128)(2,1)S(1)} %get-tuple-element.125), channel_id=1, source_target_pairs={{0,1},{1,0},{2,3},{3,2},{4,5},{5,4},{6,7},{7,6},{8,9},{9,8},{10,11... | collective-permute-start | bytes 786440 | tf_op jit(solution)/shard_map/ppermute | solution.py:87
  133.4 11.7 %collective-permute-start.43 = (bf16[64,2048]{1,0:T(8,128)(2,1)S(1)}, bf16[64,2048]{1,0:T(8,128)(2,1)S(1)}, u32[]{:S(2)}, u32[]{:S(2)}) collective-permute-start(bf16[64,2048]{1,0:T(8,128)(2,1)S(1)} %get-tuple-element.131), channel_id=1, source_target_pairs={{0,2},{1,3},{2,0},{3,1},{4,6},{5,7},{6,4},{7,5},{8,10},{9,11},{10,... | collective-permute-start | bytes 786440 | tf_op jit(solution)/shard_map/ppermute | solution.py:87
  139.4 10.5 %collective-permute-start.47 = (bf16[64,2048]{1,0:T(8,128)(2,1)S(1)}, bf16[64,2048]{1,0:T(8,128)(2,1)S(1)}, u32[]{:S(2)}, u32[]{:S(2)}) collective-permute-start(bf16[64,2048]{1,0:T(8,128)(2,1)S(1)} %get-tuple-element.139), channel_id=1, source_target_pairs={{0,2},{1,3},{2,0},{3,1},{4,6},{5,7},{6,4},{7,5},{8,10},{9,11},{10,... | collective-permute-start | bytes 786440 | tf_op jit(solution)/shard_map/ppermute | solution.py:87
  139.6 10.4 %collective-permute-start.48 = (bf16[64,2048]{1,0:T(8,128)(2,1)S(1)}, bf16[64,2048]{1,0:T(8,128)(2,1)S(1)}, u32[]{:S(2)}, u32[]{:S(2)}) collective-permute-start(bf16[64,2048]{1,0:T(8,128)(2,1)S(1)} %get-tuple-element.140), channel_id=1, source_target_pairs={{0,1},{1,0},{2,3},{3,2},{4,5},{5,4},{6,7},{7,6},{8,9},{9,8},{10,11... | collective-permute-start | bytes 786440 | tf_op jit(solution)/shard_map/ppermute | solution.py:87
  145.2 10.5 %collective-permute-start.45 = (f32[64,2048]{1,0:T(8,128)S(1)}, f32[64,2048]{1,0:T(8,128)S(1)}, u32[]{:S(2)}, u32[]{:S(2)}) collective-permute-start(f32[64,2048]{1,0:T(8,128)S(1)} %get-tuple-element.136), channel_id=1, source_target_pairs={{0,4},{1,5},{2,6},{3,7},{4,8},{5,9},{6,10},{7,11},{8,12},{9,13},{1... | collective-permute-start | bytes 1572872 | tf_op jit(solution)/shard_map/ppermute | solution.py:95
  150.7 10.6 %collective-permute-start.49 = (f32[64,2048]{1,0:T(8,128)S(1)}, f32[64,2048]{1,0:T(8,128)S(1)}, u32[]{:S(2)}, u32[]{:S(2)}) collective-permute-start(f32[64,2048]{1,0:T(8,128)S(1)} %get-tuple-element.142), channel_id=1, source_target_pairs={{0,4},{1,5},{2,6},{3,7},{4,8},{5,9},{6,10},{7,11},{8,12},{9,13},{1... | collective-permute-start | bytes 1572872 | tf_op jit(solution)/shard_map/ppermute | solution.py:95
  (19 other events, 152.2 us)

commit v3 on v2

v3 whole, which is shorter than its diff:
```python
import functools

import jax
import jax.numpy as jnp
from jax import lax
from jax.experimental import pallas as pl
from jax.experimental.pallas import tpu as pltpu
from jax.sharding import PartitionSpec as P

TOP = 2
STEPS = 3
SIZES = (64, 64)
FIRST = (1, 2)
BACK = (1, 2)
MODE = ("rows", "sums")
LAST = ("rows", "sums")
LIMIT = 16 * 1024 * 1024


def order(k):
    for step in range(STEPS):
        for what in range(3):
            for c in range(k):
                yield what, step, c


def shifted(x, axis, by):
    count = lax.axis_size(axis)
    return lax.ppermute(x, axis, [(i, (i + by) % count) for i in range(count)])


def rms_normed(current, gain_row):
    inv_rms = lax.rsqrt(jnp.mean(current * current, axis=-1, keepdims=True) + 1e-06)
    return (current * inv_rms * gain_row).astype(jnp.bfloat16)


def expert_ffn(rows_in, gate_mat, up_mat, down_mat):
    gate_part = jnp.dot(rows_in, gate_mat, preferred_element_type=jnp.float32)
    upward = jnp.dot(rows_in, up_mat, preferred_element_type=jnp.float32)
    hidden = (jax.nn.silu(gate_part) * upward).astype(jnp.bfloat16)
    return jnp.dot(hidden, down_mat, preferred_element_type=jnp.float32).astype(jnp.bfloat16)


def layer_by_slots(token_rows, gain_row, chosen, slot_rows, weights_in, experts, cap, mats):
    normed = rms_normed(token_rows, gain_row)
    flat_place = chosen * cap + slot_rows
    place_iota = jnp.arange(experts * cap, dtype=jnp.int32)
    tables = [
        (flat_place[:, k : k + 1] == place_iota[None, :]).astype(jnp.bfloat16) for k in range(TOP)
    ]
    occupied = tables[0] + tables[1]
    send = lax.dot_general(
        occupied, normed, (((0,), (0,)), ((), ())), preferred_element_type=jnp.float32
    )
    send = send.astype(jnp.bfloat16).reshape(experts, cap, normed.shape[1])
    received = lax.all_to_all(send, "expert", split_axis=0, concat_axis=0, tiled=True)
    result = expert_ffn(received.reshape(experts * cap, normed.shape[1]), *mats)
    returned = lax.all_to_all(
        result.reshape(send.shape), "expert", split_axis=0, concat_axis=0, tiled=True
    ).reshape(experts * cap, normed.shape[1])
    combined = jnp.zeros(token_rows.shape, jnp.float32)
    for k in range(TOP):
        picked = jnp.dot(tables[k], returned, preferred_element_type=jnp.float32)
        combined = combined + weights_in[:, k : k + 1] * picked
    return token_rows + combined


def run_by_slots(residual, norm_gain, mats, route_ids, route_slots, combine_weights):
    experts = lax.axis_size("expert")
    cap = 4 * residual.shape[1] // experts
    current = residual[0]
    for step in range(STEPS):
        current = layer_by_slots(
            current,
            norm_gain[0],
            route_ids[step, 0],
            route_slots[step, 0],
            combine_weights[step, 0],
            experts,
            cap,
            mats,
        )
        current = shifted(current, "section", 1)
    return current[None]


def across(x, bits):
    return lax.ppermute(x, "expert", [(e, e ^ bits) for e in range(4)])


def onward(x, bits, by=1):
    sections = lax.axis_size("section")
    pairs = [
        (s * 4 + e, ((s + by) % sections) * 4 + (e ^ bits)) for s in range(sections) for e in range(4)
    ]
    return lax.ppermute(x, ("section", "expert"), pairs)


def normed_of(x, gain):
    inv_rms = lax.rsqrt(jnp.mean(x * x, axis=-1, keepdims=True) + 1e-06)
    return (x * inv_rms * gain).astype(jnp.bfloat16)


VMEM_SPEC = pl.BlockSpec(memory_space=pltpu.VMEM)
SMEM_SPEC = pl.BlockSpec(memory_space=pltpu.SMEM)
ANY_SPEC = pl.BlockSpec(memory_space=pl.ANY)
MARK = jax.ShapeDtypeStruct((8, 128), jnp.float32)


def call(kernel, outs, ins, specs, flops, moved, exps=0, scratch=(), after=()):
    ins, specs = (*after, *ins), [ANY_SPEC] * len(after) + list(specs)
    return pl.pallas_call(
        lambda *refs: kernel(*refs[len(after) :]),
        in_specs=specs,
        out_shape=outs,
        scratch_shapes=scratch,
        compiler_params=pltpu.CompilerParams(vmem_limit_bytes=LIMIT),
        cost_estimate=pl.CostEstimate(flops=flops, bytes_accessed=moved, transcendentals=exps),
    )(*ins)


def far(x):
    return pltpu.with_memory_space_constraint(x, pltpu.HBM)


def bf16_rows(n, width):
    return jax.ShapeDtypeStruct((n, width), jnp.bfloat16)


def f32_rows(n, width):
    return jax.ShapeDtypeStruct((n, width), jnp.float32)


def start_kernel(x_far, gain_far, ids_far, combine_far, *refs):
    x_refs, refs = refs[: len(SIZES)], refs[len(SIZES) :]
    normed_refs, (mark, gain, ids, combine, sems) = refs[: len(SIZES)], refs[len(SIZES) :]
    bf16, f32 = jnp.bfloat16, jnp.float32
    copies = []
    others = ((ids_far, ids), (combine_far, combine), (gain_far, gain))
    for j, (src, dst) in enumerate(others):
        copies.append(pltpu.make_async_copy(src, dst, sems.at[len(SIZES) + j]))
    at = 0
    for c, n in enumerate(SIZES):
        rows = x_far.at[0, pl.ds(at, n)]
        copies.append(pltpu.make_async_copy(rows, x_refs[c], sems.at[c]))
        at += n
    for copy in copies:
        copy.start()
    mark[...] = jnp.zeros_like(mark)
    copies[0].wait()
    copies[1].wait()
    lines = []
    for step in range(STEPS):
        for e in range(4):
            named = ids[step] == e
            lines.append(jnp.sum(jnp.where(named, combine[step], 0.0), axis=0, keepdims=True))
    tokens = ids.shape[-1]
    lines.append(jnp.zeros((32 - len(lines), tokens), f32))
    lines = jnp.concatenate(lines, axis=0)
    first = lines.astype(bf16).astype(f32)
    second = (lines - first).astype(bf16).astype(f32)
    third = lines - first - second
    blocks = [first, second, third, jnp.zeros((32, tokens), f32)]
    columns = jnp.concatenate(blocks, axis=0).T.astype(bf16)
    for copy in copies[2:]:
        copy.wait()
    at = 0
    for c, n in enumerate(SIZES):
        width = x_refs[c].shape[1]
        normed_refs[c][:, :width] = normed_of(x_refs[c][...], gain[...])
        normed_refs[c][:, width:] = columns[at : at + n]
        at += n


def start_rows(x, gain, ids, combine):
    width = x.shape[-1]
    outs = [f32_rows(n, width) for n in SIZES] + [bf16_rows(n, width + 128) for n in SIZES] + [MARK]
    scratch = [
        pltpu.VMEM(gain.shape, jnp.float32),
        pltpu.VMEM(ids.shape, jnp.int32),
        pltpu.VMEM(combine.shape, jnp.float32),
        pltpu.SemaphoreType.DMA((len(SIZES) + 3,)),
    ]
    ins = tuple(far(v) for v in (x, gain, ids, combine))
    return call(start_kernel, outs, ins, [ANY_SPEC] * 4, 5 * x.size, 6 * x.size, scratch=scratch)


def add_kernel(a_ref, b_ref, before, out_ref, mark):
    del before
    f32 = jnp.float32
    out_ref[...] = (a_ref[...].astype(f32) + b_ref[...].astype(f32)).astype(jnp.bfloat16)
    mark[...] = jnp.zeros_like(mark)


def add_rows(a, b, before, after):
    specs = [VMEM_SPEC] * 2 + [ANY_SPEC]
    outs = (bf16_rows(*a.shape), MARK)
    return call(add_kernel, outs, (a, b, before), specs, a.size, 6 * a.size, after=after)


def summed(x_ref, a_ref, b_ref):
    return x_ref[...] + (a_ref[...].astype(jnp.float32) + b_ref[...].astype(jnp.float32))


def total_kernel(x_ref, a_ref, b_ref, gain_ref, before, new_ref, normed_ref, mark):
    del before
    x = summed(x_ref, a_ref, b_ref)
    new_ref[...] = x
    normed_ref[...] = normed_of(x, gain_ref[...])
    mark[...] = jnp.zeros_like(mark)


def total_rows(sums, gain, before):
    n, width = sums[0].shape
    outs = [f32_rows(n, width), bf16_rows(n, width), MARK]
    specs = [VMEM_SPEC] * 4 + [ANY_SPEC]
    return call(total_kernel, outs, (*sums, gain, before), specs, 8 * n * width, 16 * n * width)


def last_total_kernel(x_ref, a_ref, b_ref, before, new_ref, mark):
    del before
    new_ref[...] = summed(x_ref, a_ref, b_ref)
    mark[...] = jnp.zeros_like(mark)


def last_total(sums, before):
    n, width = sums[0].shape
    specs = [VMEM_SPEC] * 3 + [ANY_SPEC]
    outs = [f32_rows(n, width), MARK]
    return call(last_total_kernel, outs, (*sums, before), specs, 3 * n * width, 12 * n * width)


def final_kernel(counts, *refs):
    out = refs[-1]
    at = i = 0
    for n, count in zip(SIZES, counts):
        out[0, at : at + n] = refs[i][...] if count == 1 else summed(*refs[i : i + 3])
        at += n
        i += count


def final_rows(groups, shape):
    out = jax.ShapeDtypeStruct(shape, jnp.float32)
    size = shape[1] * shape[2]
    ins = [v for group in groups for v in group]
    kernel = functools.partial(final_kernel, tuple(len(group) for group in groups))
    return call(kernel, out, ins, [VMEM_SPEC] * len(ins), 3 * size, 14 * size)


def experts_of(x, rows, weight, gate, up, down, waits, outs):
    f32 = jnp.float32
    waits[0]()
    gate_part = jnp.dot(rows, gate[...], preferred_element_type=f32)
    waits[1]()
    upward = jnp.dot(rows, up[...], preferred_element_type=f32)
    silu = gate_part / (1.0 + jnp.exp(-gate_part))
    hidden = (silu * upward * weight).astype(jnp.bfloat16)
    waits[2]()
    out = jnp.dot(hidden, down[...], preferred_element_type=f32)
    n = outs[0].shape[0]
    outs[0][...] = x[...] + out[:n]
    for j in range(1, 4):
        outs[j][...] = out[j * n : (j + 1) * n].astype(jnp.bfloat16)


def first_ffn_kernel(load, me_ref, x, own, rx, ry, rd, gate, up, down, *rest):
    outs, rest = rest[-6 - 4 * load :], rest[: -6 - 4 * load]
    weights, mark = outs[4], outs[5]
    waits = [lambda: None] * 3
    if load:
        mats, sems = outs[6:9], outs[9]
        copies = [
            pltpu.make_async_copy(src, dst, sems.at[j])
            for j, (src, dst) in enumerate(zip((gate, up, down), mats))
        ]
        for copy in copies:
            copy.start()
        waits = [copy.wait for copy in copies]
        gate, up, down = mats
    width = own.shape[1] - 128
    pieces = (own, rx, ry, rd)
    parts = jnp.concatenate([p[:, width:] for p in pieces], axis=0).astype(jnp.float32)
    column = lax.broadcasted_iota(jnp.int32, parts.shape, 1)
    of_steps = []
    for step in range(STEPS):
        mine = (column & 31) == 4 * step + me_ref[0]
        of_steps.append(jnp.sum(jnp.where(mine, parts, 0.0), axis=1, keepdims=True))
        weights[:, step : step + 1] = of_steps[step]
    rows = jnp.concatenate([p[:, :width] for p in pieces], axis=0)
    experts_of(x, rows, of_steps[0], gate, up, down, waits, outs[:4])
    mark[...] = jnp.zeros_like(mark)


def first_ffn(me, x, pieces, mats, load, before):
    n, width = pieces[0].shape
    width -= 128
    wide = mats[0].shape[1]
    macs = 4 * n * mats[0].size * 3
    outs = [f32_rows(n, width)] + [bf16_rows(n, width)] * 3 + [f32_rows(4 * n, 128), MARK]
    scratch = ()
    if load:
        outs += [pltpu.VMEM(m.shape, m.dtype) for m in mats]
        scratch = [pltpu.SemaphoreType.DMA((3,))]
        mats = [far(m) for m in mats]
    ins = (me, x, *pieces, *mats, *before)
    specs = [SMEM_SPEC] + [VMEM_SPEC] * 5 + [ANY_SPEC if load else VMEM_SPEC] * 3 + [ANY_SPEC] * len(before)
    kernel = functools.partial(first_ffn_kernel, load)
    return call(kernel, outs, ins, specs, 2 * macs, 16 * n * width, 4 * n * wide, scratch=scratch)


def ffn_kernel(step, x, own, rx, ry, rd, weights, gate, up, down, before, *outs):
    del before
    mine = own[...] if own.shape[0] == x.shape[0] else normed_of(x[...], own[...])
    rows = jnp.concatenate([mine, rx[...], ry[...], rd[...]], axis=0)
    experts_of(x, rows, weights[:, step : step + 1], gate, up, down, [lambda: None] * 3, outs)
    outs[4][...] = jnp.zeros_like(outs[4])


def weighted_ffn(step, x, pieces, weights, mats, before):
    n, width = x.shape
    wide = mats[0].shape[1]
    macs = 4 * n * mats[0].size * 3
    kernel = functools.partial(ffn_kernel, step)
    outs = [f32_rows(n, width)] + [bf16_rows(n, width)] * 3 + [MARK]
    ins = (x, *pieces, weights, *mats, before)
    specs = [VMEM_SPEC] * 9 + [ANY_SPEC]
    return call(kernel, outs, ins, specs, 2 * macs, 16 * n * width, 4 * n * wide)


def run_by_rows(residual, norm_gain, mats, route_ids, combine_weights):
    me = lax.axis_index("expert").reshape(1)
    k = len(SIZES)
    ids, combine = (jnp.transpose(v[:, 0], (0, 2, 1)) for v in (route_ids, combine_weights))
    outs = start_rows(residual, norm_gain, ids, combine)
    xs, owns, mark = list(outs[:k]), outs[k : 2 * k], outs[-1]
    firsts = [(own, across(own, 1), across(own, 2)) for own in owns]
    sections = lax.axis_size("section")
    next_gain = norm_gain
    if "rows" in MODE:
        next_gain = lax.ppermute(norm_gain, "section", [((i + 1) % sections, i) for i in range(sections)])
    weights = {}
    state = {"mark": mark, "mats": mats}
    sums = {}

    def way(step, c):
        return LAST[c] if step == STEPS - 1 else MODE[c]

    def apply_experts(step, c):
        own, rx, ry = firsts[c]
        rd = across(rx, 2) if FIRST[c] == 1 else across(ry, 1)
        pieces = (own, rx, ry, rd)
        if step:
            outs = weighted_ffn(step, xs[c], pieces, weights[c], state["mats"], state["mark"])
            kept, o_x, o_y, o_d, state["mark"] = outs
        else:
            outs = first_ffn(me, xs[c], pieces, state["mats"], not weights, (state["mark"], next_gain))
            kept, o_x, o_y, o_d, weights[c], state["mark"] = outs[:6]
            if len(outs) > 6:
                state["mats"] = outs[6:]
        if BACK[c] == 1:
            sums[c] = (kept, o_x, o_y, across(o_d, 1))
        else:
            sums[c] = (kept, o_y, o_x, across(o_d, 2))
        kept, other, mine, part = sums[c]
        if way(step, c) == "sums":
            sums[c] = (onward(kept, 0), onward(other, BACK[c]), mine, part)
        else:
            sums[c] = (kept, across(other, BACK[c]), mine, part)

    def pass_sum(step, c):
        kept, got, mine, part = sums[c]
        both, state["mark"] = add_rows(mine, part, state["mark"], ())
        go = onward if way(step, c) == "sums" else across
        sums[c] = (kept, got, go(both, 3 - BACK[c]))

    def move_on(step, c):
        if way(step, c) == "sums":
            if step < STEPS - 1:
                xs[c], normed, state["mark"] = total_rows(sums[c], norm_gain, state["mark"])
                firsts[c] = (normed, across(normed, 1), across(normed, 2))
            return
        if step < STEPS - 1:
            new, normed, state["mark"] = total_rows(sums[c], next_gain, state["mark"])
            firsts[c] = (norm_gain, onward(normed, 1), onward(normed, 2))
            xs[c] = onward(new, 0)
        else:
            new, state["mark"] = last_total(sums[c], state["mark"])
            sums[c] = (onward(new, 0),)

    for what, step, c in order(k):
        (apply_experts, pass_sum, move_on)[what](step, c)
    return final_rows([sums[c] for c in range(k)], residual.shape)


def per_device(residual, norm_gain, w_gate, w_up, w_down, route_ids, route_slots, combine_weights):
    mats = (w_gate[0, 0], w_up[0, 0], w_down[0, 0])
    if lax.axis_size("expert") == 4:
        return run_by_rows(residual, norm_gain, mats, route_ids, combine_weights)
    return run_by_slots(residual, norm_gain, mats, route_ids, route_slots, combine_weights)


def solution(mesh):
    in_specs = (
        P("section", "expert", None),
        P("section", None),
        P("section", "expert", None, None),
        P("section", "expert", None, None),
        P("section", "expert", None, None),
        P(None, "section", "expert", None),
        P(None, "section", "expert", None),
        P(None, "section", "expert", None),
    )
    out_specs = P("section", "expert", None)
    return jax.shard_map(
        per_device, mesh=mesh, in_specs=in_specs, out_specs=out_specs, check_vma=False
    )
```

time: 162 us -> 152 us (0.938)
  waiting for transfers between devices: 88.2 us -> 78.8 us
    ppermute x31 -> x26, waiting for transfers between devices: 56.1 us -> 42.1 us  [across(): return lax.ppermute(x, 'expert', [(e, e ^ bits) for e in range(4)])]
    ppermute x18 -> x16, waiting for transfers between devices: 30.7 us -> 35.2 us  [onward(): return lax.ppermute(x, ('section', 'expert'), pairs)]
    pallas_call x21 -> x19, Pallas kernels: 24.4 us -> 23.4 us  [call(): pl.pallas_call(lambda *refs: kernel(*refs[len(after):]), in_specs=specs,...]
    ppermute x18 -> x16, starting transfers between devices: 16.3 us -> 15.6 us  [onward(): return lax.ppermute(x, ('section', 'expert'), pairs)]
    ppermute x31 -> x26, starting transfers between devices: 33.1 us -> 32.6 us  [across(): return lax.ppermute(x, 'expert', [(e, e ^ bits) for e in range(4)])]
  transfers between devices with their start and end apart: 50 -> 43, of which waited for: 29 -> 24; matrix products, arithmetic and copies ran while one was open for 0% -> 0% of each run, Pallas kernels for 13% -> 14%
where the time goes in v3:
time: 152 us
  waiting for transfers between devices  78.8 us (52%)
  starting transfers between devices  49.6 us (33%)
  Pallas kernels  23.4 us (15%)
    ppermute x26, waiting for transfers between devices, across(): return lax.ppermute(x, 'expert', [(e, e ^ bits) for e in range(4)])  42.1 us
    ppermute x16, waiting for transfers between devices, onward(): return lax.ppermute(x, ('section', 'expert'), pairs)  35.2 us
    ppermute x26, starting transfers between devices, across(): return lax.ppermute(x, 'expert', [(e, e ^ bits) for e in range(4)])  32.6 us
    pallas_call x19, Pallas kernels, call(): pl.pallas_call(lambda *refs: kernel(*refs[len(after):]), in_specs=specs,...  23.4 us
    ppermute x16, starting transfers between devices, onward(): return lax.ppermute(x, ('section', 'expert'), pairs)  15.6 us
  transfers between devices with their start and end apart: 43, of which 24 were waited for; matrix products, arithmetic and copies ran while one was open for 0% of the time, Pallas kernels for 14%

profile of v3, /device:TPU:0, one launch (start us, length us, event | category | flops | bytes accessed | tf_op | source)
XLA Modules:
  0.0 152.0 jit_solution(1775858935662812577)
XLA Ops:
  1.5 3.0 %collective-permute-start = (bf16[64,2176]{1,0:T(8,128)(2,1)S(1)}, bf16[64,2176]{1,0:T(8,128)(2,1)S(1)}, u32[]{:S(2)}, u32[]{:S(2)}) collective-permute-start(bf16[64,2176]{1,0:T(8,128)(2,1)S(1)} %get-tuple-element.71.refs_2_), channel_id=1, source_target_pairs={{0,1},{1,0},{2,3},{3,2},{4,5},{5,4},{6,7},{7,6},{8,9},{9,8},{10,11... | collective-permute-start | bytes 835592 | tf_op jit(solution)/shard_map/ppermute | solution.py:88
  6.5 4.6 %collective-permute-done.refs_3_ = bf16[64,2176]{1,0:T(8,128)(2,1)S(1)} collective-permute-done((bf16[64,2176]{1,0:T(8,128)(2,1)S(1)}, bf16[64,2176]{1,0:T(8,128)(2,1)S(1)}, u32[]{:S(2)}, u32[]{:S(2)}) %collective-permute-start) | collective-permute-done | bytes 278560 | tf_op jit(solution)/shard_map/ppermute | solution.py:88
  11.2 1.8 %collective-permute-start.2 = (bf16[64,2176]{1,0:T(8,128)(2,1)S(1)}, bf16[64,2176]{1,0:T(8,128)(2,1)S(1)}, u32[]{:S(2)}, u32[]{:S(2)}) collective-permute-start(bf16[64,2176]{1,0:T(8,128)(2,1)S(1)} %collective-permute-done.refs_3_), channel_id=1, source_target_pairs={{0,2},{1,3},{2,0},{3,1},{4,6},{5,7},{6,4},{7,5},{8,10},{9,11},{10,... | collective-permute-start | bytes 835592 | tf_op jit(solution)/shard_map/ppermute | solution.py:88
  17.9 2.2 %collective-permute-done.1.refs_4_ = bf16[64,2176]{1,0:T(8,128)(2,1)S(1)} collective-permute-done((bf16[64,2176]{1,0:T(8,128)(2,1)S(1)}, bf16[64,2176]{1,0:T(8,128)(2,1)S(1)}, u32[]{:S(2)}, u32[]{:S(2)}) %collective-permute-start.1) | collective-permute-done | bytes 278560 | tf_op jit(solution)/shard_map/ppermute | solution.py:88
  20.1 4.5 %collective-permute-done.2.refs_5_ = bf16[64,2176]{1,0:T(8,128)(2,1)S(1)} collective-permute-done((bf16[64,2176]{1,0:T(8,128)(2,1)S(1)}, bf16[64,2176]{1,0:T(8,128)(2,1)S(1)}, u32[]{:S(2)}, u32[]{:S(2)}) %collective-permute-start.2) | collective-permute-done | bytes 278560 | tf_op jit(solution)/shard_map/ppermute | solution.py:88
  24.6 5.4 %shard_map.74 = (f32[64,2048]{1,0:T(8,128)S(1)}, bf16[64,2048]{1,0:T(8,128)(2,1)S(1)}, bf16[64,2048]{1,0:T(8,128)(2,1)S(1)}, bf16[64,2048]{1,0:T(8,128)(2,1)S(1)...) custom-call(s32[1]{0:T(128)} %bitcast.refs_0_, ...), custom_call_target="tpu_custom_call" | custom-call | flops 2415919104 | bytes 2097152 | tf_op jit(solution)/shard_map/pallas_call | solution.py:112
  30.4 2.7 %shard_map.75 = (f32[64,2048]{1,0:T(8,128)S(1)}, bf16[64,2048]{1,0:T(8,128)(2,1)S(1)}, bf16[64,2048]{1,0:T(8,128)(2,1)S(1)}, bf16[64,2048]{1,0:T(8,128)(2,1)S(1)...) custom-call(s32[1]{0:T(128)} %bitcast.refs_0_, f32[64,2048]{1,0:T(8,128)S(1)} %get-tuple-element.77.refs_1_, ...), custom_call_target="tpu_custom_call" | custom-call | flops 2415919104 | bytes 2097152 | tf_op jit(solution)/shard_map/pallas_call | solution.py:112
  36.4 1.8 %collective-permute-done.5.refs_1_ = bf16[64,2048]{1,0:T(8,128)(2,1)S(1)} collective-permute-done((bf16[64,2048]{1,0:T(8,128)(2,1)S(1)}, bf16[64,2048]{1,0:T(8,128)(2,1)S(1)}, u32[]{:S(2)}, u32[]{:S(2)}) %collective-permute-start.5) | collective-permute-done | bytes 262176 | tf_op jit(solution)/shard_map/ppermute | solution.py:88
  38.3 2.5 %collective-permute-start.9 = (bf16[64,2048]{1,0:T(8,128)(2,1)S(1)}, bf16[64,2048]{1,0:T(8,128)(2,1)S(1)}, u32[]{:S(2)}, u32[]{:S(2)}) collective-permute-start(bf16[64,2048]{1,0:T(8,128)(2,1)S(1)} %get-tuple-element.84), channel_id=1, source_target_pairs={{0,2},{1,3},{2,0},{3,1},{4,6},{5,7},{6,4},{7,5},{8,10},{9,11},{10,... | collective-permute-start | bytes 786440 | tf_op jit(solution)/shard_map/ppermute | solution.py:88
  42.5 3.9 %collective-permute-done.9.refs_2_ = bf16[64,2048]{1,0:T(8,128)(2,1)S(1)} collective-permute-done((bf16[64,2048]{1,0:T(8,128)(2,1)S(1)}, bf16[64,2048]{1,0:T(8,128)(2,1)S(1)}, u32[]{:S(2)}, u32[]{:S(2)}) %collective-permute-start.9) | collective-permute-done | bytes 262176 | tf_op jit(solution)/shard_map/ppermute | solution.py:88
  46.7 4.7 %collective-permute-start.12 = (bf16[64,2048]{1,0:T(8,128)(2,1)S(1)}, bf16[64,2048]{1,0:T(8,128)(2,1)S(1)}, u32[]{:S(2)}, u32[]{:S(2)}) collective-permute-start(bf16[64,2048]{1,0:T(8,128)(2,1)S(1)} %get-tuple-element.90), channel_id=1, source_target_pairs={{0,5},{1,4},{2,7},{3,6},{4,9},{5,8},{6,11},{7,10},{8,13},{9,12},{1... | collective-permute-start | bytes 786440 | tf_op jit(solution)/shard_map/ppermute | solution.py:96
  53.8 7.4 %collective-permute-done.12.refs_2_ = bf16[64,2048]{1,0:T(8,128)(2,1)S(1)} collective-permute-done((bf16[64,2048]{1,0:T(8,128)(2,1)S(1)}, bf16[64,2048]{1,0:T(8,128)(2,1)S(1)}, u32[]{:S(2)}, u32[]{:S(2)}) %collective-permute-start.12) | collective-permute-done | bytes 262176 | tf_op jit(solution)/shard_map/ppermute | solution.py:96
  63.5 3.2 %collective-permute-done.13.refs_3_ = bf16[64,2048]{1,0:T(8,128)(2,1)S(1)} collective-permute-done((bf16[64,2048]{1,0:T(8,128)(2,1)S(1)}, bf16[64,2048]{1,0:T(8,128)(2,1)S(1)}, u32[]{:S(2)}, u32[]{:S(2)}) %collective-permute-start.13) | collective-permute-done | bytes 262176 | tf_op jit(solution)/shard_map/ppermute | solution.py:96
  66.7 5.2 %collective-permute-done.14.refs_4_ = bf16[64,2048]{1,0:T(8,128)(2,1)S(1)} collective-permute-done((bf16[64,2048]{1,0:T(8,128)(2,1)S(1)}, bf16[64,2048]{1,0:T(8,128)(2,1)S(1)}, u32[]{:S(2)}, u32[]{:S(2)}) %collective-permute-start.14) | collective-permute-done | bytes 262176 | tf_op jit(solution)/shard_map/ppermute | solution.py:88
  71.9 2.8 %shard_map.80 = (f32[64,2048]{1,0:T(8,128)S(1)}, bf16[64,2048]{1,0:T(8,128)(2,1)S(1)}, bf16[64,2048]{1,0:T(8,128)(2,1)S(1)}, bf16[64,2048]{1,0:T(8,128)(2,1)S(1)}, f32[8,128]{1,0:T(8,128)S(1)}) custom-call(f32[64,2048]{1,0:T(8,128)S(1)} %collective-permute-done.11.refs_0_, f32[1,2048]{1,0:T(1,128)S(1)} %copy-done, ...), custom_call_target="tpu_custom_call" | custom-call | flops 2415919104 | bytes 2097152 | tf_op jit(solution)/shard_map/pallas_call | solution.py:112
  75.4 2.7 %shard_map.81 = (f32[64,2048]{1,0:T(8,128)S(1)}, bf16[64,2048]{1,0:T(8,128)(2,1)S(1)}, bf16[64,2048]{1,0:T(8,128)(2,1)S(1)}, bf16[64,2048]{1,0:T(8,128)(2,1)S(1)}, f32[8,128]{1,0:T(8,128)S(1)}) custom-call(f32[64,2048]{1,0:T(8,128)S(1)} %get-tuple-element.101.refs_0_, bf16[64,2048]{1,0:T(8,128)(2,1)S(1)} %get-tuple-element.102.refs_1_, ...), custom_call_target="tpu_custom_call" | custom-call | flops 2415919104 | bytes 2097152 | tf_op jit(solution)/shard_map/pallas_call | solution.py:112
  80.5 2.1 %collective-permute-done.19.refs_1_ = bf16[64,2048]{1,0:T(8,128)(2,1)S(1)} collective-permute-done((bf16[64,2048]{1,0:T(8,128)(2,1)S(1)}, bf16[64,2048]{1,0:T(8,128)(2,1)S(1)}, u32[]{:S(2)}, u32[]{:S(2)}) %collective-permute-start.19) | collective-permute-done | bytes 262176 | tf_op jit(solution)/shard_map/ppermute | solution.py:88
  84.6 2.2 %collective-permute-start.31 = (bf16[64,2048]{1,0:T(8,128)(2,1)S(1)}, bf16[64,2048]{1,0:T(8,128)(2,1)S(1)}, u32[]{:S(2)}, u32[]{:S(2)}) collective-permute-start(bf16[64,2048]{1,0:T(8,128)(2,1)S(1)} %get-tuple-element.115), channel_id=1, source_target_pairs={{0,5},{1,4},{2,7},{3,6},{4,9},{5,8},{6,11},{7,10},{8,13},{9,12},{1... | collective-permute-start | bytes 786440 | tf_op jit(solution)/shard_map/ppermute | solution.py:96
  86.7 3.5 %collective-permute-done.23.refs_2_ = bf16[64,2048]{1,0:T(8,128)(2,1)S(1)} collective-permute-done((bf16[64,2048]{1,0:T(8,128)(2,1)S(1)}, bf16[64,2048]{1,0:T(8,128)(2,1)S(1)}, u32[]{:S(2)}, u32[]{:S(2)}) %collective-permute-start.23) | collective-permute-done | bytes 262176 | tf_op jit(solution)/shard_map/ppermute | solution.py:88
  90.5 5.1 %collective-permute-start.25 = (f32[64,2048]{1,0:T(8,128)S(1)}, f32[64,2048]{1,0:T(8,128)S(1)}, u32[]{:S(2)}, u32[]{:S(2)}) collective-permute-start(f32[64,2048]{1,0:T(8,128)S(1)} %get-tuple-element.111), channel_id=1, source_target_pairs={{0,4},{1,5},{2,6},{3,7},{4,8},{5,9},{6,10},{7,11},{8,12},{9,13},{1... | collective-permute-start | bytes 1572872 | tf_op jit(solution)/shard_map/ppermute | solution.py:96
  98.1 2.0 %collective-permute-done.26.refs_2_ = bf16[64,2048]{1,0:T(8,128)(2,1)S(1)} collective-permute-done((bf16[64,2048]{1,0:T(8,128)(2,1)S(1)}, bf16[64,2048]{1,0:T(8,128)(2,1)S(1)}, u32[]{:S(2)}, u32[]{:S(2)}) %collective-permute-start.26) | collective-permute-done | bytes 262176 | tf_op jit(solution)/shard_map/ppermute | solution.py:96
  102.3 2.2 %collective-permute-done.35.refs_3_ = bf16[64,2048]{1,0:T(8,128)(2,1)S(1)} collective-permute-done((bf16[64,2048]{1,0:T(8,128)(2,1)S(1)}, bf16[64,2048]{1,0:T(8,128)(2,1)S(1)}, u32[]{:S(2)}, u32[]{:S(2)}) %collective-permute-start.35) | collective-permute-done | bytes 262176 | tf_op jit(solution)/shard_map/ppermute | solution.py:88
  106.2 5.6 %collective-permute-done.27.refs_3_ = bf16[64,2048]{1,0:T(8,128)(2,1)S(1)} collective-permute-done((bf16[64,2048]{1,0:T(8,128)(2,1)S(1)}, bf16[64,2048]{1,0:T(8,128)(2,1)S(1)}, u32[]{:S(2)}, u32[]{:S(2)}) %collective-permute-start.27) | collective-permute-done | bytes 262176 | tf_op jit(solution)/shard_map/ppermute | solution.py:96
  111.8 3.9 %collective-permute-done.28.refs_4_ = bf16[64,2048]{1,0:T(8,128)(2,1)S(1)} collective-permute-done((bf16[64,2048]{1,0:T(8,128)(2,1)S(1)}, bf16[64,2048]{1,0:T(8,128)(2,1)S(1)}, u32[]{:S(2)}, u32[]{:S(2)}) %collective-permute-start.28) | collective-permute-done | bytes 262176 | tf_op jit(solution)/shard_map/ppermute | solution.py:88
  115.7 2.8 %shard_map.86 = (f32[64,2048]{1,0:T(8,128)S(1)}, bf16[64,2048]{1,0:T(8,128)(2,1)S(1)}, bf16[64,2048]{1,0:T(8,128)(2,1)S(1)}, bf16[64,2048]{1,0:T(8,128)(2,1)S(1)}, f32[8,128]{1,0:T(8,128)S(1)}) custom-call(f32[64,2048]{1,0:T(8,128)S(1)} %collective-permute-done.25.refs_0_, f32[1,2048]{1,0:T(1,128)S(1)} %copy-done, ...), custom_call_target="tpu_custom_call" | custom-call | flops 2415919104 | bytes 2097152 | tf_op jit(solution)/shard_map/pallas_call | solution.py:112
  119.8 2.7 %shard_map.87 = (f32[64,2048]{1,0:T(8,128)S(1)}, bf16[64,2048]{1,0:T(8,128)(2,1)S(1)}, bf16[64,2048]{1,0:T(8,128)(2,1)S(1)}, bf16[64,2048]{1,0:T(8,128)(2,1)S(1)}, f32[8,128]{1,0:T(8,128)S(1)}) custom-call(f32[64,2048]{1,0:T(8,128)S(1)} %get-tuple-element.122.refs_0_, bf16[64,2048]{1,0:T(8,128)(2,1)S(1)} %get-tuple-element.123.refs_1_, ...), custom_call_target="tpu_custom_call" | custom-call | flops 2415919104 | bytes 2097152 | tf_op jit(solution)/shard_map/pallas_call | solution.py:112
  124.7 2.3 %collective-permute-done.33.refs_1_ = bf16[64,2048]{1,0:T(8,128)(2,1)S(1)} collective-permute-done((bf16[64,2048]{1,0:T(8,128)(2,1)S(1)}, bf16[64,2048]{1,0:T(8,128)(2,1)S(1)}, u32[]{:S(2)}, u32[]{:S(2)}) %collective-permute-start.33) | collective-permute-done | bytes 262176 | tf_op jit(solution)/shard_map/ppermute | solution.py:88
  127.0 1.8 %collective-permute-start.37 = (bf16[64,2048]{1,0:T(8,128)(2,1)S(1)}, bf16[64,2048]{1,0:T(8,128)(2,1)S(1)}, u32[]{:S(2)}, u32[]{:S(2)}) collective-permute-start(bf16[64,2048]{1,0:T(8,128)(2,1)S(1)} %get-tuple-element.126), channel_id=1, source_target_pairs={{0,2},{1,3},{2,0},{3,1},{4,6},{5,7},{6,4},{7,5},{8,10},{9,11},{10,... | collective-permute-start | bytes 786440 | tf_op jit(solution)/shard_map/ppermute | solution.py:88
  130.7 2.8 %collective-permute-done.37.refs_2_ = bf16[64,2048]{1,0:T(8,128)(2,1)S(1)} collective-permute-done((bf16[64,2048]{1,0:T(8,128)(2,1)S(1)}, bf16[64,2048]{1,0:T(8,128)(2,1)S(1)}, u32[]{:S(2)}, u32[]{:S(2)}) %collective-permute-start.37) | collective-permute-done | bytes 262176 | tf_op jit(solution)/shard_map/ppermute | solution.py:88
  134.1 2.2 %collective-permute-start.41 = (bf16[64,2048]{1,0:T(8,128)(2,1)S(1)}, bf16[64,2048]{1,0:T(8,128)(2,1)S(1)}, u32[]{:S(2)}, u32[]{:S(2)}) collective-permute-start(bf16[64,2048]{1,0:T(8,128)(2,1)S(1)} %get-tuple-element.133), channel_id=1, source_target_pairs={{0,6},{1,7},{2,4},{3,5},{4,10},{5,11},{6,8},{7,9},{8,14},{9,15},{1... | collective-permute-start | bytes 786440 | tf_op jit(solution)/shard_map/ppermute | solution.py:96
  136.6 11.9 %collective-permute-done.41.refs_2_ = bf16[64,2048]{1,0:T(8,128)(2,1)S(1)} collective-permute-done((bf16[64,2048]{1,0:T(8,128)(2,1)S(1)}, bf16[64,2048]{1,0:T(8,128)(2,1)S(1)}, u32[]{:S(2)}, u32[]{:S(2)}) %collective-permute-start.41) | collective-permute-done | bytes 262176 | tf_op jit(solution)/shard_map/ppermute | solution.py:96
  148.6 2.4 %collective-permute-done.42.refs_3_ = bf16[64,2048]{1,0:T(8,128)(2,1)S(1)} collective-permute-done((bf16[64,2048]{1,0:T(8,128)(2,1)S(1)}, bf16[64,2048]{1,0:T(8,128)(2,1)S(1)}, u32[]{:S(2)}, u32[]{:S(2)}) %collective-permute-start.42) | collective-permute-done | bytes 262176 | tf_op jit(solution)/shard_map/ppermute | solution.py:96
  (75 shorter events, 38.0 us)
Async XLA Ops:
  1.5 9.7 %collective-permute-start = (bf16[64,2176]{1,0:T(8,128)(2,1)S(1)}, bf16[64,2176]{1,0:T(8,128)(2,1)S(1)}, u32[]{:S(2)}, u32[]{:S(2)}) collective-permute-start(bf16[64,2176]{1,0:T(8,128)(2,1)S(1)} %get-tuple-element.71.refs_2_), channel_id=1, source_target_pairs={{0,1},{1,0},{2,3},{3,2},{4,5},{5,4},{6,7},{7,6},{8,9},{9,8},{10,11... | collective-permute-start | bytes 835592 | tf_op jit(solution)/shard_map/ppermute | solution.py:88
  4.5 9.9 %collective-permute-start.7 = (bf16[64,2176]{1,0:T(8,128)(2,1)S(1)}, bf16[64,2176]{1,0:T(8,128)(2,1)S(1)}, u32[]{:S(2)}, u32[]{:S(2)}) collective-permute-start(bf16[64,2176]{1,0:T(8,128)(2,1)S(1)} %get-tuple-element.78.refs_2_), channel_id=1, source_target_pairs={{0,2},{1,3},{2,0},{3,1},{4,6},{5,7},{6,4},{7,5},{8,10},{9,11},{10,... | collective-permute-start | bytes 835592 | tf_op jit(solution)/shard_map/ppermute | solution.py:88
  6.0 14.0 %collective-permute-start.1 = (bf16[64,2176]{1,0:T(8,128)(2,1)S(1)}, bf16[64,2176]{1,0:T(8,128)(2,1)S(1)}, u32[]{:S(2)}, u32[]{:S(2)}) collective-permute-start(bf16[64,2176]{1,0:T(8,128)(2,1)S(1)} %get-tuple-element.71.refs_2_), channel_id=1, source_target_pairs={{0,2},{1,3},{2,0},{3,1},{4,6},{5,7},{6,4},{7,5},{8,10},{9,11},{10,... | collective-permute-start | bytes 835592 | tf_op jit(solution)/shard_map/ppermute | solution.py:88
  11.2 13.4 %collective-permute-start.2 = (bf16[64,2176]{1,0:T(8,128)(2,1)S(1)}, bf16[64,2176]{1,0:T(8,128)(2,1)S(1)}, u32[]{:S(2)}, u32[]{:S(2)}) collective-permute-start(bf16[64,2176]{1,0:T(8,128)(2,1)S(1)} %collective-permute-done.refs_3_), channel_id=1, source_target_pairs={{0,2},{1,3},{2,0},{3,1},{4,6},{5,7},{6,4},{7,5},{8,10},{9,11},{10,... | collective-permute-start | bytes 835592 | tf_op jit(solution)/shard_map/ppermute | solution.py:88
  12.9 17.5 %collective-permute-start.6 = (bf16[64,2176]{1,0:T(8,128)(2,1)S(1)}, bf16[64,2176]{1,0:T(8,128)(2,1)S(1)}, u32[]{:S(2)}, u32[]{:S(2)}) collective-permute-start(bf16[64,2176]{1,0:T(8,128)(2,1)S(1)} %get-tuple-element.78.refs_2_), channel_id=1, source_target_pairs={{0,1},{1,0},{2,3},{3,2},{4,5},{5,4},{6,7},{7,6},{8,9},{9,8},{10,11... | collective-permute-start | bytes 835592 | tf_op jit(solution)/shard_map/ppermute | solution.py:88
  14.4 16.0 %collective-permute-start.8 = (bf16[64,2176]{1,0:T(8,128)(2,1)S(1)}, bf16[64,2176]{1,0:T(8,128)(2,1)S(1)}, u32[]{:S(2)}, u32[]{:S(2)}) collective-permute-start(bf16[64,2176]{1,0:T(8,128)(2,1)S(1)} %collective-permute-done.7.refs_4_), channel_id=1, source_target_pairs={{0,1},{1,0},{2,3},{3,2},{4,5},{5,4},{6,7},{7,6},{8,9},{9,8},{10,11... | collective-permute-start | bytes 835592 | tf_op jit(solution)/shard_map/ppermute | solution.py:88
  30.0 8.2 %collective-permute-start.5 = (bf16[64,2048]{1,0:T(8,128)(2,1)S(1)}, bf16[64,2048]{1,0:T(8,128)(2,1)S(1)}, u32[]{:S(2)}, u32[]{:S(2)}) collective-permute-start(bf16[64,2048]{1,0:T(8,128)(2,1)S(1)} %get-tuple-element.76), channel_id=1, source_target_pairs={{0,1},{1,0},{2,3},{3,2},{4,5},{5,4},{6,7},{7,6},{8,9},{9,8},{10,11... | collective-permute-start | bytes 786440 | tf_op jit(solution)/shard_map/ppermute | solution.py:88
  36.4 16.0 %collective-permute-start.15 = (f32[64,2048]{1,0:T(8,128)S(1)}, f32[64,2048]{1,0:T(8,128)S(1)}, u32[]{:S(2)}, u32[]{:S(2)}) collective-permute-start(f32[64,2048]{1,0:T(8,128)S(1)} %get-tuple-element.92), channel_id=1, source_target_pairs={{0,4},{1,5},{2,6},{3,7},{4,8},{5,9},{6,10},{7,11},{8,12},{9,13},{1... | collective-permute-start | bytes 1572872 | tf_op jit(solution)/shard_map/ppermute | solution.py:96
  38.3 8.1 %collective-permute-start.9 = (bf16[64,2048]{1,0:T(8,128)(2,1)S(1)}, bf16[64,2048]{1,0:T(8,128)(2,1)S(1)}, u32[]{:S(2)}, u32[]{:S(2)}) collective-permute-start(bf16[64,2048]{1,0:T(8,128)(2,1)S(1)} %get-tuple-element.84), channel_id=1, source_target_pairs={{0,2},{1,3},{2,0},{3,1},{4,6},{5,7},{6,4},{7,5},{8,10},{9,11},{10,... | collective-permute-start | bytes 786440 | tf_op jit(solution)/shard_map/ppermute | solution.py:88
  40.8 10.6 %collective-permute-start.16 = (bf16[64,2048]{1,0:T(8,128)(2,1)S(1)}, bf16[64,2048]{1,0:T(8,128)(2,1)S(1)}, u32[]{:S(2)}, u32[]{:S(2)}) collective-permute-start(bf16[64,2048]{1,0:T(8,128)(2,1)S(1)} %get-tuple-element.93), channel_id=1, source_target_pairs={{0,6},{1,7},{2,4},{3,5},{4,10},{5,11},{6,8},{7,9},{8,14},{9,15},{1... | collective-permute-start | bytes 786440 | tf_op jit(solution)/shard_map/ppermute | solution.py:96
  40.9 11.5 %collective-permute-start.17 = (bf16[64,2048]{1,0:T(8,128)(2,1)S(1)}, bf16[64,2048]{1,0:T(8,128)(2,1)S(1)}, u32[]{:S(2)}, u32[]{:S(2)}) collective-permute-start(bf16[64,2048]{1,0:T(8,128)(2,1)S(1)} %get-tuple-element.94), channel_id=1, source_target_pairs={{0,5},{1,4},{2,7},{3,6},{4,9},{5,8},{6,11},{7,10},{8,13},{9,12},{1... | collective-permute-start | bytes 786440 | tf_op jit(solution)/shard_map/ppermute | solution.py:96
  46.6 20.1 %collective-permute-start.11 = (f32[64,2048]{1,0:T(8,128)S(1)}, f32[64,2048]{1,0:T(8,128)S(1)}, u32[]{:S(2)}, u32[]{:S(2)}) collective-permute-start(f32[64,2048]{1,0:T(8,128)S(1)} %get-tuple-element.89), channel_id=1, source_target_pairs={{0,4},{1,5},{2,6},{3,7},{4,8},{5,9},{6,10},{7,11},{8,12},{9,13},{1... | collective-permute-start | bytes 1572872 | tf_op jit(solution)/shard_map/ppermute | solution.py:96
  46.7 14.5 %collective-permute-start.12 = (bf16[64,2048]{1,0:T(8,128)(2,1)S(1)}, bf16[64,2048]{1,0:T(8,128)(2,1)S(1)}, u32[]{:S(2)}, u32[]{:S(2)}) collective-permute-start(bf16[64,2048]{1,0:T(8,128)(2,1)S(1)} %get-tuple-element.90), channel_id=1, source_target_pairs={{0,5},{1,4},{2,7},{3,6},{4,9},{5,8},{6,11},{7,10},{8,13},{9,12},{1... | collective-permute-start | bytes 786440 | tf_op jit(solution)/shard_map/ppermute | solution.py:96
  52.6 10.2 %collective-permute-start.21 = (bf16[64,2048]{1,0:T(8,128)(2,1)S(1)}, bf16[64,2048]{1,0:T(8,128)(2,1)S(1)}, u32[]{:S(2)}, u32[]{:S(2)}) collective-permute-start(bf16[64,2048]{1,0:T(8,128)(2,1)S(1)} %get-tuple-element.102.refs_1_), channel_id=1, source_target_pairs={{0,2},{1,3},{2,0},{3,1},{4,6},{5,7},{6,4},{7,5},{8,10},{9,11},{10,... | collective-permute-start | bytes 786440 | tf_op jit(solution)/shard_map/ppermute | solution.py:88
  53.3 13.5 %collective-permute-start.13 = (bf16[64,2048]{1,0:T(8,128)(2,1)S(1)}, bf16[64,2048]{1,0:T(8,128)(2,1)S(1)}, u32[]{:S(2)}, u32[]{:S(2)}) collective-permute-start(bf16[64,2048]{1,0:T(8,128)(2,1)S(1)} %get-tuple-element.90), channel_id=1, source_target_pairs={{0,6},{1,7},{2,4},{3,5},{4,10},{5,11},{6,8},{7,9},{8,14},{9,15},{1... | collective-permute-start | bytes 786440 | tf_op jit(solution)/shard_map/ppermute | solution.py:96
  61.2 10.7 %collective-permute-start.14 = (bf16[64,2048]{1,0:T(8,128)(2,1)S(1)}, bf16[64,2048]{1,0:T(8,128)(2,1)S(1)}, u32[]{:S(2)}, u32[]{:S(2)}) collective-permute-start(bf16[64,2048]{1,0:T(8,128)(2,1)S(1)} %collective-permute-done.12.refs_2_), channel_id=1, source_target_pairs={{0,2},{1,3},{2,0},{3,1},{4,6},{5,7},{6,4},{7,5},{8,10},{9,11},{10,... | collective-permute-start | bytes 786440 | tf_op jit(solution)/shard_map/ppermute | solution.py:88
  61.5 13.9 %collective-permute-start.20 = (bf16[64,2048]{1,0:T(8,128)(2,1)S(1)}, bf16[64,2048]{1,0:T(8,128)(2,1)S(1)}, u32[]{:S(2)}, u32[]{:S(2)}) collective-permute-start(bf16[64,2048]{1,0:T(8,128)(2,1)S(1)} %get-tuple-element.102.refs_1_), channel_id=1, source_target_pairs={{0,1},{1,0},{2,3},{3,2},{4,5},{5,4},{6,7},{7,6},{8,9},{9,8},{10,11... | collective-permute-start | bytes 786440 | tf_op jit(solution)/shard_map/ppermute | solution.py:88
  62.8 12.5 %collective-permute-start.22 = (bf16[64,2048]{1,0:T(8,128)(2,1)S(1)}, bf16[64,2048]{1,0:T(8,128)(2,1)S(1)}, u32[]{:S(2)}, u32[]{:S(2)}) collective-permute-start(bf16[64,2048]{1,0:T(8,128)(2,1)S(1)} %collective-permute-done.21.refs_3_), channel_id=1, source_target_pairs={{0,1},{1,0},{2,3},{3,2},{4,5},{5,4},{6,7},{7,6},{8,9},{9,8},{10,11... | collective-permute-start | bytes 786440 | tf_op jit(solution)/shard_map/ppermute | solution.py:88
  80.5 16.8 %collective-permute-start.29 = (f32[64,2048]{1,0:T(8,128)S(1)}, f32[64,2048]{1,0:T(8,128)S(1)}, u32[]{:S(2)}, u32[]{:S(2)}) collective-permute-start(f32[64,2048]{1,0:T(8,128)S(1)} %get-tuple-element.113), channel_id=1, source_target_pairs={{0,4},{1,5},{2,6},{3,7},{4,8},{5,9},{6,10},{7,11},{8,12},{9,13},{1... | collective-permute-start | bytes 1572872 | tf_op jit(solution)/shard_map/ppermute | solution.py:96
  84.3 11.3 %collective-permute-start.30 = (bf16[64,2048]{1,0:T(8,128)(2,1)S(1)}, bf16[64,2048]{1,0:T(8,128)(2,1)S(1)}, u32[]{:S(2)}, u32[]{:S(2)}) collective-permute-start(bf16[64,2048]{1,0:T(8,128)(2,1)S(1)} %get-tuple-element.114), channel_id=1, source_target_pairs={{0,6},{1,7},{2,4},{3,5},{4,10},{5,11},{6,8},{7,9},{8,14},{9,15},{1... | collective-permute-start | bytes 786440 | tf_op jit(solution)/shard_map/ppermute | solution.py:96
  84.6 12.7 %collective-permute-start.31 = (bf16[64,2048]{1,0:T(8,128)(2,1)S(1)}, bf16[64,2048]{1,0:T(8,128)(2,1)S(1)}, u32[]{:S(2)}, u32[]{:S(2)}) collective-permute-start(bf16[64,2048]{1,0:T(8,128)(2,1)S(1)} %get-tuple-element.115), channel_id=1, source_target_pairs={{0,5},{1,4},{2,7},{3,6},{4,9},{5,8},{6,11},{7,10},{8,13},{9,12},{1... | collective-permute-start | bytes 786440 | tf_op jit(solution)/shard_map/ppermute | solution.py:96
  90.5 9.6 %collective-permute-start.26 = (bf16[64,2048]{1,0:T(8,128)(2,1)S(1)}, bf16[64,2048]{1,0:T(8,128)(2,1)S(1)}, u32[]{:S(2)}, u32[]{:S(2)}) collective-permute-start(bf16[64,2048]{1,0:T(8,128)(2,1)S(1)} %get-tuple-element.112), channel_id=1, source_target_pairs={{0,5},{1,4},{2,7},{3,6},{4,9},{5,8},{6,11},{7,10},{8,13},{9,12},{1... | collective-permute-start | bytes 786440 | tf_op jit(solution)/shard_map/ppermute | solution.py:96
  90.5 25.2 %collective-permute-start.25 = (f32[64,2048]{1,0:T(8,128)S(1)}, f32[64,2048]{1,0:T(8,128)S(1)}, u32[]{:S(2)}, u32[]{:S(2)}) collective-permute-start(f32[64,2048]{1,0:T(8,128)S(1)} %get-tuple-element.111), channel_id=1, source_target_pairs={{0,4},{1,5},{2,6},{3,7},{4,8},{5,9},{6,10},{7,11},{8,12},{9,13},{1... | collective-permute-start | bytes 1572872 | tf_op jit(solution)/shard_map/ppermute | solution.py:96
  98.1 13.7 %collective-permute-start.27 = (bf16[64,2048]{1,0:T(8,128)(2,1)S(1)}, bf16[64,2048]{1,0:T(8,128)(2,1)S(1)}, u32[]{:S(2)}, u32[]{:S(2)}) collective-permute-start(bf16[64,2048]{1,0:T(8,128)(2,1)S(1)} %get-tuple-element.112), channel_id=1, source_target_pairs={{0,6},{1,7},{2,4},{3,5},{4,10},{5,11},{6,8},{7,9},{8,14},{9,15},{1... | collective-permute-start | bytes 786440 | tf_op jit(solution)/shard_map/ppermute | solution.py:96
  100.1 15.6 %collective-permute-start.28 = (bf16[64,2048]{1,0:T(8,128)(2,1)S(1)}, bf16[64,2048]{1,0:T(8,128)(2,1)S(1)}, u32[]{:S(2)}, u32[]{:S(2)}) collective-permute-start(bf16[64,2048]{1,0:T(8,128)(2,1)S(1)} %collective-permute-done.26.refs_2_), channel_id=1, source_target_pairs={{0,2},{1,3},{2,0},{3,1},{4,6},{5,7},{6,4},{7,5},{8,10},{9,11},{10,... | collective-permute-start | bytes 786440 | tf_op jit(solution)/shard_map/ppermute | solution.py:88
  101.4 18.4 %collective-permute-start.34 = (bf16[64,2048]{1,0:T(8,128)(2,1)S(1)}, bf16[64,2048]{1,0:T(8,128)(2,1)S(1)}, u32[]{:S(2)}, u32[]{:S(2)}) collective-permute-start(bf16[64,2048]{1,0:T(8,128)(2,1)S(1)} %get-tuple-element.123.refs_1_), channel_id=1, source_target_pairs={{0,1},{1,0},{2,3},{3,2},{4,5},{5,4},{6,7},{7,6},{8,9},{9,8},{10,11... | collective-permute-start | bytes 786440 | tf_op jit(solution)/shard_map/ppermute | solution.py:88
  104.5 15.3 %collective-permute-start.36 = (bf16[64,2048]{1,0:T(8,128)(2,1)S(1)}, bf16[64,2048]{1,0:T(8,128)(2,1)S(1)}, u32[]{:S(2)}, u32[]{:S(2)}) collective-permute-start(bf16[64,2048]{1,0:T(8,128)(2,1)S(1)} %collective-permute-done.35.refs_3_), channel_id=1, source_target_pairs={{0,1},{1,0},{2,3},{3,2},{4,5},{5,4},{6,7},{7,6},{8,9},{9,8},{10,11... | collective-permute-start | bytes 786440 | tf_op jit(solution)/shard_map/ppermute | solution.py:88
  118.5 8.5 %collective-permute-start.33 = (bf16[64,2048]{1,0:T(8,128)(2,1)S(1)}, bf16[64,2048]{1,0:T(8,128)(2,1)S(1)}, u32[]{:S(2)}, u32[]{:S(2)}) collective-permute-start(bf16[64,2048]{1,0:T(8,128)(2,1)S(1)} %get-tuple-element.121), channel_id=1, source_target_pairs={{0,1},{1,0},{2,3},{3,2},{4,5},{5,4},{6,7},{7,6},{8,9},{9,8},{10,11... | collective-permute-start | bytes 786440 | tf_op jit(solution)/shard_map/ppermute | solution.py:88
  128.9 22.0 %collective-permute-start.40 = (f32[64,2048]{1,0:T(8,128)S(1)}, f32[64,2048]{1,0:T(8,128)S(1)}, u32[]{:S(2)}, u32[]{:S(2)}) collective-permute-start(f32[64,2048]{1,0:T(8,128)S(1)} %get-tuple-element.132), channel_id=1, source_target_pairs={{0,4},{1,5},{2,6},{3,7},{4,8},{5,9},{6,10},{7,11},{8,12},{9,13},{1... | collective-permute-start | bytes 1572872 | tf_op jit(solution)/shard_map/ppermute | solution.py:96
  134.1 16.8 %collective-permute-start.39 = (f32[64,2048]{1,0:T(8,128)S(1)}, f32[64,2048]{1,0:T(8,128)S(1)}, u32[]{:S(2)}, u32[]{:S(2)}) collective-permute-start(f32[64,2048]{1,0:T(8,128)S(1)} %get-tuple-element.131), channel_id=1, source_target_pairs={{0,4},{1,5},{2,6},{3,7},{4,8},{5,9},{6,10},{7,11},{8,12},{9,13},{1... | collective-permute-start | bytes 1572872 | tf_op jit(solution)/shard_map/ppermute | solution.py:96
  134.1 14.4 %collective-permute-start.41 = (bf16[64,2048]{1,0:T(8,128)(2,1)S(1)}, bf16[64,2048]{1,0:T(8,128)(2,1)S(1)}, u32[]{:S(2)}, u32[]{:S(2)}) collective-permute-start(bf16[64,2048]{1,0:T(8,128)(2,1)S(1)} %get-tuple-element.133), channel_id=1, source_target_pairs={{0,6},{1,7},{2,4},{3,5},{4,10},{5,11},{6,8},{7,9},{8,14},{9,15},{1... | collective-permute-start | bytes 786440 | tf_op jit(solution)/shard_map/ppermute | solution.py:96
  136.3 14.6 %collective-permute-start.42 = (bf16[64,2048]{1,0:T(8,128)(2,1)S(1)}, bf16[64,2048]{1,0:T(8,128)(2,1)S(1)}, u32[]{:S(2)}, u32[]{:S(2)}) collective-permute-start(bf16[64,2048]{1,0:T(8,128)(2,1)S(1)} %get-tuple-element.134), channel_id=1, source_target_pairs={{0,5},{1,4},{2,7},{3,6},{4,9},{5,8},{6,11},{7,10},{8,13},{9,12},{1... | collective-permute-start | bytes 786440 | tf_op jit(solution)/shard_map/ppermute | solution.py:96
  (12 other events, 98.0 us)

commit v4 on v3

--- a/solution.py
+++ b/solution.py
@@ -13,7 +13,7 @@
 FIRST = (1, 2)
 BACK = (1, 2)
 MODE = ("rows", "sums")
-LAST = ("rows", "sums")
+LAST = ("sums", "sums")
 LIMIT = 16 * 1024 * 1024
 
 
@@ -369,7 +369,8 @@
 
     def pass_sum(step, c):
         kept, got, mine, part = sums[c]
-        both, state["mark"] = add_rows(mine, part, state["mark"], ())
+        after = (kept,) if way(step, c) == "sums" and step == STEPS - 1 else ()
+        both, state["mark"] = add_rows(mine, part, state["mark"], after)
         go = onward if way(step, c) == "sums" else across
         sums[c] = (kept, got, go(both, 3 - BACK[c]))
 

time: 152 us -> 149 us (0.980)
  starting transfers between devices: 49.6 us -> 38.2 us
  waiting for transfers between devices: 78.8 us -> 86.7 us
    ppermute x16 -> x18, starting transfers between devices: 15.6 us -> 7.35 us  [onward(): return lax.ppermute(x, ('section', 'expert'), pairs)]
    ppermute x26 -> x24, waiting for transfers between devices: 42.1 us -> 49.5 us  [across(): return lax.ppermute(x, 'expert', [(e, e ^ bits) for e in range(4)])]
    ppermute x26 -> x24, starting transfers between devices: 32.6 us -> 29.5 us  [across(): return lax.ppermute(x, 'expert', [(e, e ^ bits) for e in range(4)])]
    ppermute x16 -> x18, waiting for transfers between devices: 35.2 us -> 35.6 us  [onward(): return lax.ppermute(x, ('section', 'expert'), pairs)]
    pallas_call x19 -> x18, Pallas kernels: 23.4 us -> 23.4 us  [call(): pl.pallas_call(lambda *refs: kernel(*refs[len(after):]), in_specs=specs,...]
  transfers between devices with their start and end apart: 43 -> 43, of which waited for: 24 -> 27; matrix products, arithmetic and copies ran while one was open for 0% -> 0% of each run, Pallas kernels for 14% -> 14%
where the time goes in v4:
time: 149 us; the launch traced here: 148 us
  waiting for transfers between devices  86.7 us (58%)
  starting transfers between devices  38.2 us (26%)
  Pallas kernels  23.4 us (16%)
    ppermute x24, waiting for transfers between devices, across(): return lax.ppermute(x, 'expert', [(e, e ^ bits) for e in range(4)])  49.5 us
    ppermute x18, waiting for transfers between devices, onward(): return lax.ppermute(x, ('section', 'expert'), pairs)  35.6 us
    ppermute x24, starting transfers between devices, across(): return lax.ppermute(x, 'expert', [(e, e ^ bits) for e in range(4)])  29.5 us
    pallas_call x18, Pallas kernels, call(): pl.pallas_call(lambda *refs: kernel(*refs[len(after):]), in_specs=specs,...  23.4 us
    ppermute x18, starting transfers between devices, onward(): return lax.ppermute(x, ('section', 'expert'), pairs)  7.35 us
  transfers between devices with their start and end apart: 43, of which 27 were waited for; matrix products, arithmetic and copies ran while one was open for 0% of the time, Pallas kernels for 14%

profile of v4, /device:TPU:0, one launch (start us, length us, event | category | flops | bytes accessed | tf_op | source)
XLA Modules:
  0.0 148.5 jit_solution(1990258537084818465)
XLA Ops:
  1.5 3.0 %collective-permute-start = (bf16[64,2176]{1,0:T(8,128)(2,1)S(1)}, bf16[64,2176]{1,0:T(8,128)(2,1)S(1)}, u32[]{:S(2)}, u32[]{:S(2)}) collective-permute-start(bf16[64,2176]{1,0:T(8,128)(2,1)S(1)} %get-tuple-element.69.refs_2_), channel_id=1, source_target_pairs={{0,1},{1,0},{2,3},{3,2},{4,5},{5,4},{6,7},{7,6},{8,9},{9,8},{10,11... | collective-permute-start | bytes 835592 | tf_op jit(solution)/shard_map/ppermute | solution.py:88
  6.5 4.6 %collective-permute-done.refs_3_ = bf16[64,2176]{1,0:T(8,128)(2,1)S(1)} collective-permute-done((bf16[64,2176]{1,0:T(8,128)(2,1)S(1)}, bf16[64,2176]{1,0:T(8,128)(2,1)S(1)}, u32[]{:S(2)}, u32[]{:S(2)}) %collective-permute-start) | collective-permute-done | bytes 278560 | tf_op jit(solution)/shard_map/ppermute | solution.py:88
  11.2 1.8 %collective-permute-start.2 = (bf16[64,2176]{1,0:T(8,128)(2,1)S(1)}, bf16[64,2176]{1,0:T(8,128)(2,1)S(1)}, u32[]{:S(2)}, u32[]{:S(2)}) collective-permute-start(bf16[64,2176]{1,0:T(8,128)(2,1)S(1)} %collective-permute-done.refs_3_), channel_id=1, source_target_pairs={{0,2},{1,3},{2,0},{3,1},{4,6},{5,7},{6,4},{7,5},{8,10},{9,11},{10,... | collective-permute-start | bytes 835592 | tf_op jit(solution)/shard_map/ppermute | solution.py:88
  17.9 2.2 %collective-permute-done.1.refs_4_ = bf16[64,2176]{1,0:T(8,128)(2,1)S(1)} collective-permute-done((bf16[64,2176]{1,0:T(8,128)(2,1)S(1)}, bf16[64,2176]{1,0:T(8,128)(2,1)S(1)}, u32[]{:S(2)}, u32[]{:S(2)}) %collective-permute-start.1) | collective-permute-done | bytes 278560 | tf_op jit(solution)/shard_map/ppermute | solution.py:88
  20.1 4.5 %collective-permute-done.2.refs_5_ = bf16[64,2176]{1,0:T(8,128)(2,1)S(1)} collective-permute-done((bf16[64,2176]{1,0:T(8,128)(2,1)S(1)}, bf16[64,2176]{1,0:T(8,128)(2,1)S(1)}, u32[]{:S(2)}, u32[]{:S(2)}) %collective-permute-start.2) | collective-permute-done | bytes 278560 | tf_op jit(solution)/shard_map/ppermute | solution.py:88
  24.6 5.4 %shard_map.74 = (f32[64,2048]{1,0:T(8,128)S(1)}, bf16[64,2048]{1,0:T(8,128)(2,1)S(1)}, bf16[64,2048]{1,0:T(8,128)(2,1)S(1)}, bf16[64,2048]{1,0:T(8,128)(2,1)S(1)...) custom-call(s32[1]{0:T(128)} %bitcast.refs_0_, ...), custom_call_target="tpu_custom_call" | custom-call | flops 2415919104 | bytes 2097152 | tf_op jit(solution)/shard_map/pallas_call | solution.py:112
  30.4 2.7 %shard_map.75 = (f32[64,2048]{1,0:T(8,128)S(1)}, bf16[64,2048]{1,0:T(8,128)(2,1)S(1)}, bf16[64,2048]{1,0:T(8,128)(2,1)S(1)}, bf16[64,2048]{1,0:T(8,128)(2,1)S(1)...) custom-call(s32[1]{0:T(128)} %bitcast.refs_0_, f32[64,2048]{1,0:T(8,128)S(1)} %get-tuple-element.75.refs_1_, ...), custom_call_target="tpu_custom_call" | custom-call | flops 2415919104 | bytes 2097152 | tf_op jit(solution)/shard_map/pallas_call | solution.py:112
  33.1 1.8 %collective-permute-start.10 = (bf16[64,2048]{1,0:T(8,128)(2,1)S(1)}, bf16[64,2048]{1,0:T(8,128)(2,1)S(1)}, u32[]{:S(2)}, u32[]{:S(2)}) collective-permute-start(bf16[64,2048]{1,0:T(8,128)(2,1)S(1)} %get-tuple-element.84), channel_id=1, source_target_pairs={{0,2},{1,3},{2,0},{3,1},{4,6},{5,7},{6,4},{7,5},{8,10},{9,11},{10,... | collective-permute-start | bytes 786440 | tf_op jit(solution)/shard_map/ppermute | solution.py:88
  37.0 1.6 %collective-permute-start.9 = (bf16[64,2048]{1,0:T(8,128)(2,1)S(1)}, bf16[64,2048]{1,0:T(8,128)(2,1)S(1)}, u32[]{:S(2)}, u32[]{:S(2)}) collective-permute-start(bf16[64,2048]{1,0:T(8,128)(2,1)S(1)} %get-tuple-element.82), channel_id=1, source_target_pairs={{0,2},{1,3},{2,0},{3,1},{4,6},{5,7},{6,4},{7,5},{8,10},{9,11},{10,... | collective-permute-start | bytes 786440 | tf_op jit(solution)/shard_map/ppermute | solution.py:88
  40.5 2.9 %collective-permute-done.4.refs_1_ = bf16[64,2048]{1,0:T(8,128)(2,1)S(1)} collective-permute-done((bf16[64,2048]{1,0:T(8,128)(2,1)S(1)}, bf16[64,2048]{1,0:T(8,128)(2,1)S(1)}, u32[]{:S(2)}, u32[]{:S(2)}) %collective-permute-start.4) | collective-permute-done | bytes 262176 | tf_op jit(solution)/shard_map/ppermute | solution.py:88
  43.4 5.6 %collective-permute-done.9.refs_2_ = bf16[64,2048]{1,0:T(8,128)(2,1)S(1)} collective-permute-done((bf16[64,2048]{1,0:T(8,128)(2,1)S(1)}, bf16[64,2048]{1,0:T(8,128)(2,1)S(1)}, u32[]{:S(2)}, u32[]{:S(2)}) %collective-permute-start.9) | collective-permute-done | bytes 262176 | tf_op jit(solution)/shard_map/ppermute | solution.py:88
  49.2 2.2 %collective-permute-start.12 = (bf16[64,2048]{1,0:T(8,128)(2,1)S(1)}, bf16[64,2048]{1,0:T(8,128)(2,1)S(1)}, u32[]{:S(2)}, u32[]{:S(2)}) collective-permute-start(bf16[64,2048]{1,0:T(8,128)(2,1)S(1)} %get-tuple-element.88), channel_id=1, source_target_pairs={{0,5},{1,4},{2,7},{3,6},{4,9},{5,8},{6,11},{7,10},{8,13},{9,12},{1... | collective-permute-start | bytes 786440 | tf_op jit(solution)/shard_map/ppermute | solution.py:96
  53.5 9.3 %collective-permute-done.12.refs_2_ = bf16[64,2048]{1,0:T(8,128)(2,1)S(1)} collective-permute-done((bf16[64,2048]{1,0:T(8,128)(2,1)S(1)}, bf16[64,2048]{1,0:T(8,128)(2,1)S(1)}, u32[]{:S(2)}, u32[]{:S(2)}) %collective-permute-start.12) | collective-permute-done | bytes 262176 | tf_op jit(solution)/shard_map/ppermute | solution.py:96
  66.3 5.3 %collective-permute-done.14.refs_4_ = bf16[64,2048]{1,0:T(8,128)(2,1)S(1)} collective-permute-done((bf16[64,2048]{1,0:T(8,128)(2,1)S(1)}, bf16[64,2048]{1,0:T(8,128)(2,1)S(1)}, u32[]{:S(2)}, u32[]{:S(2)}) %collective-permute-start.14) | collective-permute-done | bytes 262176 | tf_op jit(solution)/shard_map/ppermute | solution.py:88
  71.6 2.8 %shard_map.80 = (f32[64,2048]{1,0:T(8,128)S(1)}, bf16[64,2048]{1,0:T(8,128)(2,1)S(1)}, bf16[64,2048]{1,0:T(8,128)(2,1)S(1)}, bf16[64,2048]{1,0:T(8,128)(2,1)S(1)}, f32[8,128]{1,0:T(8,128)S(1)}) custom-call(f32[64,2048]{1,0:T(8,128)S(1)} %collective-permute-done.11.refs_0_, f32[1,2048]{1,0:T(1,128)S(1)} %copy-done, ...), custom_call_target="tpu_custom_call" | custom-call | flops 2415919104 | bytes 2097152 | tf_op jit(solution)/shard_map/pallas_call | solution.py:112
  75.1 2.7 %shard_map.81 = (f32[64,2048]{1,0:T(8,128)S(1)}, bf16[64,2048]{1,0:T(8,128)(2,1)S(1)}, bf16[64,2048]{1,0:T(8,128)(2,1)S(1)}, bf16[64,2048]{1,0:T(8,128)(2,1)S(1)}, f32[8,128]{1,0:T(8,128)S(1)}) custom-call(f32[64,2048]{1,0:T(8,128)S(1)} %get-tuple-element.99.refs_0_, bf16[64,2048]{1,0:T(8,128)(2,1)S(1)} %get-tuple-element.100.refs_1_, ...), custom_call_target="tpu_custom_call" | custom-call | flops 2415919104 | bytes 2097152 | tf_op jit(solution)/shard_map/pallas_call | solution.py:112
  80.2 1.9 %collective-permute-done.19.refs_1_ = bf16[64,2048]{1,0:T(8,128)(2,1)S(1)} collective-permute-done((bf16[64,2048]{1,0:T(8,128)(2,1)S(1)}, bf16[64,2048]{1,0:T(8,128)(2,1)S(1)}, u32[]{:S(2)}, u32[]{:S(2)}) %collective-permute-start.19) | collective-permute-done | bytes 262176 | tf_op jit(solution)/shard_map/ppermute | solution.py:88
  83.1 3.0 %collective-permute-done.24.refs_1_ = bf16[64,2048]{1,0:T(8,128)(2,1)S(1)} collective-permute-done((bf16[64,2048]{1,0:T(8,128)(2,1)S(1)}, bf16[64,2048]{1,0:T(8,128)(2,1)S(1)}, u32[]{:S(2)}, u32[]{:S(2)}) %collective-permute-start.24) | collective-permute-done | bytes 262176 | tf_op jit(solution)/shard_map/ppermute | solution.py:88
  86.2 1.6 %collective-permute-done.18.refs_1_ = bf16[64,2048]{1,0:T(8,128)(2,1)S(1)} collective-permute-done((bf16[64,2048]{1,0:T(8,128)(2,1)S(1)}, bf16[64,2048]{1,0:T(8,128)(2,1)S(1)}, u32[]{:S(2)}, u32[]{:S(2)}) %collective-permute-start.18) | collective-permute-done | bytes 262176 | tf_op jit(solution)/shard_map/ppermute | solution.py:88
  87.8 5.8 %collective-permute-done.23.refs_2_ = bf16[64,2048]{1,0:T(8,128)(2,1)S(1)} collective-permute-done((bf16[64,2048]{1,0:T(8,128)(2,1)S(1)}, bf16[64,2048]{1,0:T(8,128)(2,1)S(1)}, u32[]{:S(2)}, u32[]{:S(2)}) %collective-permute-start.23) | collective-permute-done | bytes 262176 | tf_op jit(solution)/shard_map/ppermute | solution.py:88
  98.0 4.4 %collective-permute-done.26.refs_2_ = bf16[64,2048]{1,0:T(8,128)(2,1)S(1)} collective-permute-done((bf16[64,2048]{1,0:T(8,128)(2,1)S(1)}, bf16[64,2048]{1,0:T(8,128)(2,1)S(1)}, u32[]{:S(2)}, u32[]{:S(2)}) %collective-permute-start.26) | collective-permute-done | bytes 262176 | tf_op jit(solution)/shard_map/ppermute | solution.py:96
  102.4 1.7 %collective-permute-start.28 = (bf16[64,2048]{1,0:T(8,128)(2,1)S(1)}, bf16[64,2048]{1,0:T(8,128)(2,1)S(1)}, u32[]{:S(2)}, u32[]{:S(2)}) collective-permute-start(bf16[64,2048]{1,0:T(8,128)(2,1)S(1)} %collective-permute-done.26.refs_2_), channel_id=1, source_target_pairs={{0,2},{1,3},{2,0},{3,1},{4,6},{5,7},{6,4},{7,5},{8,10},{9,11},{10,... | collective-permute-start | bytes 786440 | tf_op jit(solution)/shard_map/ppermute | solution.py:88
  106.3 6.2 %collective-permute-done.27.refs_3_ = bf16[64,2048]{1,0:T(8,128)(2,1)S(1)} collective-permute-done((bf16[64,2048]{1,0:T(8,128)(2,1)S(1)}, bf16[64,2048]{1,0:T(8,128)(2,1)S(1)}, u32[]{:S(2)}, u32[]{:S(2)}) %collective-permute-start.27) | collective-permute-done | bytes 262176 | tf_op jit(solution)/shard_map/ppermute | solution.py:96
  112.5 3.5 %collective-permute-done.28.refs_4_ = bf16[64,2048]{1,0:T(8,128)(2,1)S(1)} collective-permute-done((bf16[64,2048]{1,0:T(8,128)(2,1)S(1)}, bf16[64,2048]{1,0:T(8,128)(2,1)S(1)}, u32[]{:S(2)}, u32[]{:S(2)}) %collective-permute-start.28) | collective-permute-done | bytes 262176 | tf_op jit(solution)/shard_map/ppermute | solution.py:88
  116.0 2.8 %shard_map.86 = (f32[64,2048]{1,0:T(8,128)S(1)}, bf16[64,2048]{1,0:T(8,128)(2,1)S(1)}, bf16[64,2048]{1,0:T(8,128)(2,1)S(1)}, bf16[64,2048]{1,0:T(8,128)(2,1)S(1)}, f32[8,128]{1,0:T(8,128)S(1)}) custom-call(f32[64,2048]{1,0:T(8,128)S(1)} %collective-permute-done.25.refs_0_, f32[1,2048]{1,0:T(1,128)S(1)} %copy-done, ...), custom_call_target="tpu_custom_call" | custom-call | flops 2415919104 | bytes 2097152 | tf_op jit(solution)/shard_map/pallas_call | solution.py:112
  118.9 2.7 %shard_map.87 = (f32[64,2048]{1,0:T(8,128)S(1)}, bf16[64,2048]{1,0:T(8,128)(2,1)S(1)}, bf16[64,2048]{1,0:T(8,128)(2,1)S(1)}, bf16[64,2048]{1,0:T(8,128)(2,1)S(1)}, f32[8,128]{1,0:T(8,128)S(1)}) custom-call(f32[64,2048]{1,0:T(8,128)S(1)} %get-tuple-element.120.refs_0_, bf16[64,2048]{1,0:T(8,128)(2,1)S(1)} %get-tuple-element.121.refs_1_, ...), custom_call_target="tpu_custom_call" | custom-call | flops 2415919104 | bytes 2097152 | tf_op jit(solution)/shard_map/pallas_call | solution.py:112
  124.7 6.3 %collective-permute-done.34.refs_2_ = bf16[64,2048]{1,0:T(8,128)(2,1)S(1)} collective-permute-done((bf16[64,2048]{1,0:T(8,128)(2,1)S(1)}, bf16[64,2048]{1,0:T(8,128)(2,1)S(1)}, u32[]{:S(2)}, u32[]{:S(2)}) %collective-permute-start.34) | collective-permute-done | bytes 262176 | tf_op jit(solution)/shard_map/ppermute | solution.py:88
  131.6 3.3 %collective-permute-done.39.refs_0_.refs_3_ = f32[64,2048]{1,0:T(8,128)S(1)} collective-permute-done((f32[64,2048]{1,0:T(8,128)S(1)}, f32[64,2048]{1,0:T(8,128)S(1)}, u32[]{:S(2)}, u32[]{:S(2)}) %collective-permute-start.39) | collective-permute-done | bytes 524320 | tf_op jit(solution)/shard_map/ppermute | solution.py:96
  135.8 3.1 %collective-permute-done.40.refs_4_ = bf16[64,2048]{1,0:T(8,128)(2,1)S(1)} collective-permute-done((bf16[64,2048]{1,0:T(8,128)(2,1)S(1)}, bf16[64,2048]{1,0:T(8,128)(2,1)S(1)}, u32[]{:S(2)}, u32[]{:S(2)}) %collective-permute-start.40) | collective-permute-done | bytes 262176 | tf_op jit(solution)/shard_map/ppermute | solution.py:96
  138.9 2.5 %collective-permute-done.33.refs_1_ = bf16[64,2048]{1,0:T(8,128)(2,1)S(1)} collective-permute-done((bf16[64,2048]{1,0:T(8,128)(2,1)S(1)}, bf16[64,2048]{1,0:T(8,128)(2,1)S(1)}, u32[]{:S(2)}, u32[]{:S(2)}) %collective-permute-start.33) | collective-permute-done | bytes 262176 | tf_op jit(solution)/shard_map/ppermute | solution.py:96
  141.4 3.6 %collective-permute-done.42.refs_5_ = bf16[64,2048]{1,0:T(8,128)(2,1)S(1)} collective-permute-done((bf16[64,2048]{1,0:T(8,128)(2,1)S(1)}, bf16[64,2048]{1,0:T(8,128)(2,1)S(1)}, u32[]{:S(2)}, u32[]{:S(2)}) %collective-permute-start.42) | collective-permute-done | bytes 262176 | tf_op jit(solution)/shard_map/ppermute | solution.py:96
  145.0 2.3 %collective-permute-done.38.refs_2_ = bf16[64,2048]{1,0:T(8,128)(2,1)S(1)} collective-permute-done((bf16[64,2048]{1,0:T(8,128)(2,1)S(1)}, bf16[64,2048]{1,0:T(8,128)(2,1)S(1)}, u32[]{:S(2)}, u32[]{:S(2)}) %collective-permute-start.38) | collective-permute-done | bytes 262176 | tf_op jit(solution)/shard_map/ppermute | solution.py:96
  (74 shorter events, 35.3 us)
Async XLA Ops:
  1.5 9.7 %collective-permute-start = (bf16[64,2176]{1,0:T(8,128)(2,1)S(1)}, bf16[64,2176]{1,0:T(8,128)(2,1)S(1)}, u32[]{:S(2)}, u32[]{:S(2)}) collective-permute-start(bf16[64,2176]{1,0:T(8,128)(2,1)S(1)} %get-tuple-element.69.refs_2_), channel_id=1, source_target_pairs={{0,1},{1,0},{2,3},{3,2},{4,5},{5,4},{6,7},{7,6},{8,9},{9,8},{10,11... | collective-permute-start | bytes 835592 | tf_op jit(solution)/shard_map/ppermute | solution.py:88
  4.5 9.9 %collective-permute-start.7 = (bf16[64,2176]{1,0:T(8,128)(2,1)S(1)}, bf16[64,2176]{1,0:T(8,128)(2,1)S(1)}, u32[]{:S(2)}, u32[]{:S(2)}) collective-permute-start(bf16[64,2176]{1,0:T(8,128)(2,1)S(1)} %get-tuple-element.76.refs_2_), channel_id=1, source_target_pairs={{0,2},{1,3},{2,0},{3,1},{4,6},{5,7},{6,4},{7,5},{8,10},{9,11},{10,... | collective-permute-start | bytes 835592 | tf_op jit(solution)/shard_map/ppermute | solution.py:88
  6.0 14.0 %collective-permute-start.1 = (bf16[64,2176]{1,0:T(8,128)(2,1)S(1)}, bf16[64,2176]{1,0:T(8,128)(2,1)S(1)}, u32[]{:S(2)}, u32[]{:S(2)}) collective-permute-start(bf16[64,2176]{1,0:T(8,128)(2,1)S(1)} %get-tuple-element.69.refs_2_), channel_id=1, source_target_pairs={{0,2},{1,3},{2,0},{3,1},{4,6},{5,7},{6,4},{7,5},{8,10},{9,11},{10,... | collective-permute-start | bytes 835592 | tf_op jit(solution)/shard_map/ppermute | solution.py:88
  11.2 13.4 %collective-permute-start.2 = (bf16[64,2176]{1,0:T(8,128)(2,1)S(1)}, bf16[64,2176]{1,0:T(8,128)(2,1)S(1)}, u32[]{:S(2)}, u32[]{:S(2)}) collective-permute-start(bf16[64,2176]{1,0:T(8,128)(2,1)S(1)} %collective-permute-done.refs_3_), channel_id=1, source_target_pairs={{0,2},{1,3},{2,0},{3,1},{4,6},{5,7},{6,4},{7,5},{8,10},{9,11},{10,... | collective-permute-start | bytes 835592 | tf_op jit(solution)/shard_map/ppermute | solution.py:88
  12.9 17.5 %collective-permute-start.6 = (bf16[64,2176]{1,0:T(8,128)(2,1)S(1)}, bf16[64,2176]{1,0:T(8,128)(2,1)S(1)}, u32[]{:S(2)}, u32[]{:S(2)}) collective-permute-start(bf16[64,2176]{1,0:T(8,128)(2,1)S(1)} %get-tuple-element.76.refs_2_), channel_id=1, source_target_pairs={{0,1},{1,0},{2,3},{3,2},{4,5},{5,4},{6,7},{7,6},{8,9},{9,8},{10,11... | collective-permute-start | bytes 835592 | tf_op jit(solution)/shard_map/ppermute | solution.py:88
  14.4 16.0 %collective-permute-start.8 = (bf16[64,2176]{1,0:T(8,128)(2,1)S(1)}, bf16[64,2176]{1,0:T(8,128)(2,1)S(1)}, u32[]{:S(2)}, u32[]{:S(2)}) collective-permute-start(bf16[64,2176]{1,0:T(8,128)(2,1)S(1)} %collective-permute-done.7.refs_4_), channel_id=1, source_target_pairs={{0,1},{1,0},{2,3},{3,2},{4,5},{5,4},{6,7},{7,6},{8,9},{9,8},{10,11... | collective-permute-start | bytes 835592 | tf_op jit(solution)/shard_map/ppermute | solution.py:88
  34.9 17.0 %collective-permute-start.15 = (f32[64,2048]{1,0:T(8,128)S(1)}, f32[64,2048]{1,0:T(8,128)S(1)}, u32[]{:S(2)}, u32[]{:S(2)}) collective-permute-start(f32[64,2048]{1,0:T(8,128)S(1)} %get-tuple-element.90), channel_id=1, source_target_pairs={{0,4},{1,5},{2,6},{3,7},{4,8},{5,9},{6,10},{7,11},{8,12},{9,13},{1... | collective-permute-start | bytes 1572872 | tf_op jit(solution)/shard_map/ppermute | solution.py:96
  37.0 11.9 %collective-permute-start.9 = (bf16[64,2048]{1,0:T(8,128)(2,1)S(1)}, bf16[64,2048]{1,0:T(8,128)(2,1)S(1)}, u32[]{:S(2)}, u32[]{:S(2)}) collective-permute-start(bf16[64,2048]{1,0:T(8,128)(2,1)S(1)} %get-tuple-element.82), channel_id=1, source_target_pairs={{0,2},{1,3},{2,0},{3,1},{4,6},{5,7},{6,4},{7,5},{8,10},{9,11},{10,... | collective-permute-start | bytes 786440 | tf_op jit(solution)/shard_map/ppermute | solution.py:88
  38.6 12.9 %collective-permute-start.16 = (bf16[64,2048]{1,0:T(8,128)(2,1)S(1)}, bf16[64,2048]{1,0:T(8,128)(2,1)S(1)}, u32[]{:S(2)}, u32[]{:S(2)}) collective-permute-start(bf16[64,2048]{1,0:T(8,128)(2,1)S(1)} %get-tuple-element.91), channel_id=1, source_target_pairs={{0,6},{1,7},{2,4},{3,5},{4,10},{5,11},{6,8},{7,9},{8,14},{9,15},{1... | collective-permute-start | bytes 786440 | tf_op jit(solution)/shard_map/ppermute | solution.py:96
  40.1 11.7 %collective-permute-start.17 = (bf16[64,2048]{1,0:T(8,128)(2,1)S(1)}, bf16[64,2048]{1,0:T(8,128)(2,1)S(1)}, u32[]{:S(2)}, u32[]{:S(2)}) collective-permute-start(bf16[64,2048]{1,0:T(8,128)(2,1)S(1)} %get-tuple-element.92), channel_id=1, source_target_pairs={{0,5},{1,4},{2,7},{3,6},{4,9},{5,8},{6,11},{7,10},{8,13},{9,12},{1... | collective-permute-start | bytes 786440 | tf_op jit(solution)/shard_map/ppermute | solution.py:96
  49.2 17.2 %collective-permute-start.11 = (f32[64,2048]{1,0:T(8,128)S(1)}, f32[64,2048]{1,0:T(8,128)S(1)}, u32[]{:S(2)}, u32[]{:S(2)}) collective-permute-start(f32[64,2048]{1,0:T(8,128)S(1)} %get-tuple-element.87), channel_id=1, source_target_pairs={{0,4},{1,5},{2,6},{3,7},{4,8},{5,9},{6,10},{7,11},{8,12},{9,13},{1... | collective-permute-start | bytes 1572872 | tf_op jit(solution)/shard_map/ppermute | solution.py:96
  49.2 13.6 %collective-permute-start.12 = (bf16[64,2048]{1,0:T(8,128)(2,1)S(1)}, bf16[64,2048]{1,0:T(8,128)(2,1)S(1)}, u32[]{:S(2)}, u32[]{:S(2)}) collective-permute-start(bf16[64,2048]{1,0:T(8,128)(2,1)S(1)} %get-tuple-element.88), channel_id=1, source_target_pairs={{0,5},{1,4},{2,7},{3,6},{4,9},{5,8},{6,11},{7,10},{8,13},{9,12},{1... | collective-permute-start | bytes 786440 | tf_op jit(solution)/shard_map/ppermute | solution.py:96
  52.1 12.7 %collective-permute-start.21 = (bf16[64,2048]{1,0:T(8,128)(2,1)S(1)}, bf16[64,2048]{1,0:T(8,128)(2,1)S(1)}, u32[]{:S(2)}, u32[]{:S(2)}) collective-permute-start(bf16[64,2048]{1,0:T(8,128)(2,1)S(1)} %get-tuple-element.100.refs_1_), channel_id=1, source_target_pairs={{0,2},{1,3},{2,0},{3,1},{4,6},{5,7},{6,4},{7,5},{8,10},{9,11},{10,... | collective-permute-start | bytes 786440 | tf_op jit(solution)/shard_map/ppermute | solution.py:88
  53.3 13.1 %collective-permute-start.13 = (bf16[64,2048]{1,0:T(8,128)(2,1)S(1)}, bf16[64,2048]{1,0:T(8,128)(2,1)S(1)}, u32[]{:S(2)}, u32[]{:S(2)}) collective-permute-start(bf16[64,2048]{1,0:T(8,128)(2,1)S(1)} %get-tuple-element.88), channel_id=1, source_target_pairs={{0,6},{1,7},{2,4},{3,5},{4,10},{5,11},{6,8},{7,9},{8,14},{9,15},{1... | collective-permute-start | bytes 786440 | tf_op jit(solution)/shard_map/ppermute | solution.py:96
  64.3 10.8 %collective-permute-start.20 = (bf16[64,2048]{1,0:T(8,128)(2,1)S(1)}, bf16[64,2048]{1,0:T(8,128)(2,1)S(1)}, u32[]{:S(2)}, u32[]{:S(2)}) collective-permute-start(bf16[64,2048]{1,0:T(8,128)(2,1)S(1)} %get-tuple-element.100.refs_1_), channel_id=1, source_target_pairs={{0,1},{1,0},{2,3},{3,2},{4,5},{5,4},{6,7},{7,6},{8,9},{9,8},{10,11... | collective-permute-start | bytes 786440 | tf_op jit(solution)/shard_map/ppermute | solution.py:88
  64.8 10.2 %collective-permute-start.22 = (bf16[64,2048]{1,0:T(8,128)(2,1)S(1)}, bf16[64,2048]{1,0:T(8,128)(2,1)S(1)}, u32[]{:S(2)}, u32[]{:S(2)}) collective-permute-start(bf16[64,2048]{1,0:T(8,128)(2,1)S(1)} %collective-permute-done.21.refs_3_), channel_id=1, source_target_pairs={{0,1},{1,0},{2,3},{3,2},{4,5},{5,4},{6,7},{7,6},{8,9},{9,8},{10,11... | collective-permute-start | bytes 786440 | tf_op jit(solution)/shard_map/ppermute | solution.py:88
  79.3 16.4 %collective-permute-start.29 = (f32[64,2048]{1,0:T(8,128)S(1)}, f32[64,2048]{1,0:T(8,128)S(1)}, u32[]{:S(2)}, u32[]{:S(2)}) collective-permute-start(f32[64,2048]{1,0:T(8,128)S(1)} %get-tuple-element.111), channel_id=1, source_target_pairs={{0,4},{1,5},{2,6},{3,7},{4,8},{5,9},{6,10},{7,11},{8,12},{9,13},{1... | collective-permute-start | bytes 1572872 | tf_op jit(solution)/shard_map/ppermute | solution.py:96
  82.1 11.5 %collective-permute-start.23 = (bf16[64,2048]{1,0:T(8,128)(2,1)S(1)}, bf16[64,2048]{1,0:T(8,128)(2,1)S(1)}, u32[]{:S(2)}, u32[]{:S(2)}) collective-permute-start(bf16[64,2048]{1,0:T(8,128)(2,1)S(1)} %get-tuple-element.104), channel_id=1, source_target_pairs={{0,2},{1,3},{2,0},{3,1},{4,6},{5,7},{6,4},{7,5},{8,10},{9,11},{10,... | collective-permute-start | bytes 786440 | tf_op jit(solution)/shard_map/ppermute | solution.py:88
  82.9 12.8 %collective-permute-start.30 = (bf16[64,2048]{1,0:T(8,128)(2,1)S(1)}, bf16[64,2048]{1,0:T(8,128)(2,1)S(1)}, u32[]{:S(2)}, u32[]{:S(2)}) collective-permute-start(bf16[64,2048]{1,0:T(8,128)(2,1)S(1)} %get-tuple-element.112), channel_id=1, source_target_pairs={{0,6},{1,7},{2,4},{3,5},{4,10},{5,11},{6,8},{7,9},{8,14},{9,15},{1... | collective-permute-start | bytes 786440 | tf_op jit(solution)/shard_map/ppermute | solution.py:96
  86.2 9.6 %collective-permute-start.31 = (bf16[64,2048]{1,0:T(8,128)(2,1)S(1)}, bf16[64,2048]{1,0:T(8,128)(2,1)S(1)}, u32[]{:S(2)}, u32[]{:S(2)}) collective-permute-start(bf16[64,2048]{1,0:T(8,128)(2,1)S(1)} %get-tuple-element.113), channel_id=1, source_target_pairs={{0,5},{1,4},{2,7},{3,6},{4,9},{5,8},{6,11},{7,10},{8,13},{9,12},{1... | collective-permute-start | bytes 786440 | tf_op jit(solution)/shard_map/ppermute | solution.py:96
  94.0 22.1 %collective-permute-start.25 = (f32[64,2048]{1,0:T(8,128)S(1)}, f32[64,2048]{1,0:T(8,128)S(1)}, u32[]{:S(2)}, u32[]{:S(2)}) collective-permute-start(f32[64,2048]{1,0:T(8,128)S(1)} %get-tuple-element.109), channel_id=1, source_target_pairs={{0,4},{1,5},{2,6},{3,7},{4,8},{5,9},{6,10},{7,11},{8,12},{9,13},{1... | collective-permute-start | bytes 1572872 | tf_op jit(solution)/shard_map/ppermute | solution.py:96
  96.0 9.2 %collective-permute-start.36 = (bf16[64,2048]{1,0:T(8,128)(2,1)S(1)}, bf16[64,2048]{1,0:T(8,128)(2,1)S(1)}, u32[]{:S(2)}, u32[]{:S(2)}) collective-permute-start(bf16[64,2048]{1,0:T(8,128)(2,1)S(1)} %get-tuple-element.121.refs_1_), channel_id=1, source_target_pairs={{0,2},{1,3},{2,0},{3,1},{4,6},{5,7},{6,4},{7,5},{8,10},{9,11},{10,... | collective-permute-start | bytes 786440 | tf_op jit(solution)/shard_map/ppermute | solution.py:88
  97.5 15.0 %collective-permute-start.27 = (bf16[64,2048]{1,0:T(8,128)(2,1)S(1)}, bf16[64,2048]{1,0:T(8,128)(2,1)S(1)}, u32[]{:S(2)}, u32[]{:S(2)}) collective-permute-start(bf16[64,2048]{1,0:T(8,128)(2,1)S(1)} %get-tuple-element.110), channel_id=1, source_target_pairs={{0,6},{1,7},{2,4},{3,5},{4,10},{5,11},{6,8},{7,9},{8,14},{9,15},{1... | collective-permute-start | bytes 786440 | tf_op jit(solution)/shard_map/ppermute | solution.py:96
  102.4 13.6 %collective-permute-start.28 = (bf16[64,2048]{1,0:T(8,128)(2,1)S(1)}, bf16[64,2048]{1,0:T(8,128)(2,1)S(1)}, u32[]{:S(2)}, u32[]{:S(2)}) collective-permute-start(bf16[64,2048]{1,0:T(8,128)(2,1)S(1)} %collective-permute-done.26.refs_2_), channel_id=1, source_target_pairs={{0,2},{1,3},{2,0},{3,1},{4,6},{5,7},{6,4},{7,5},{8,10},{9,11},{10,... | collective-permute-start | bytes 786440 | tf_op jit(solution)/shard_map/ppermute | solution.py:88
  104.2 14.7 %collective-permute-start.35 = (bf16[64,2048]{1,0:T(8,128)(2,1)S(1)}, bf16[64,2048]{1,0:T(8,128)(2,1)S(1)}, u32[]{:S(2)}, u32[]{:S(2)}) collective-permute-start(bf16[64,2048]{1,0:T(8,128)(2,1)S(1)} %get-tuple-element.121.refs_1_), channel_id=1, source_target_pairs={{0,1},{1,0},{2,3},{3,2},{4,5},{5,4},{6,7},{7,6},{8,9},{9,8},{10,11... | collective-permute-start | bytes 786440 | tf_op jit(solution)/shard_map/ppermute | solution.py:88
  105.1 13.8 %collective-permute-start.37 = (bf16[64,2048]{1,0:T(8,128)(2,1)S(1)}, bf16[64,2048]{1,0:T(8,128)(2,1)S(1)}, u32[]{:S(2)}, u32[]{:S(2)}) collective-permute-start(bf16[64,2048]{1,0:T(8,128)(2,1)S(1)} %collective-permute-done.36.refs_3_), channel_id=1, source_target_pairs={{0,1},{1,0},{2,3},{3,2},{4,5},{5,4},{6,7},{7,6},{8,9},{9,8},{10,11... | collective-permute-start | bytes 786440 | tf_op jit(solution)/shard_map/ppermute | solution.py:88
  118.8 12.3 %collective-permute-start.32 = (f32[64,2048]{1,0:T(8,128)S(1)}, f32[64,2048]{1,0:T(8,128)S(1)}, u32[]{:S(2)}, u32[]{:S(2)}) collective-permute-start(f32[64,2048]{1,0:T(8,128)S(1)} %get-tuple-element.116), channel_id=1, source_target_pairs={{0,4},{1,5},{2,6},{3,7},{4,8},{5,9},{6,10},{7,11},{8,12},{9,13},{1... | collective-permute-start | bytes 1572872 | tf_op jit(solution)/shard_map/ppermute | solution.py:96
  121.6 13.3 %collective-permute-start.39 = (f32[64,2048]{1,0:T(8,128)S(1)}, f32[64,2048]{1,0:T(8,128)S(1)}, u32[]{:S(2)}, u32[]{:S(2)}) collective-permute-start(f32[64,2048]{1,0:T(8,128)S(1)} %get-tuple-element.125), channel_id=1, source_target_pairs={{0,4},{1,5},{2,6},{3,7},{4,8},{5,9},{6,10},{7,11},{8,12},{9,13},{1... | collective-permute-start | bytes 1572872 | tf_op jit(solution)/shard_map/ppermute | solution.py:96
  124.6 14.2 %collective-permute-start.40 = (bf16[64,2048]{1,0:T(8,128)(2,1)S(1)}, bf16[64,2048]{1,0:T(8,128)(2,1)S(1)}, u32[]{:S(2)}, u32[]{:S(2)}) collective-permute-start(bf16[64,2048]{1,0:T(8,128)(2,1)S(1)} %get-tuple-element.126), channel_id=1, source_target_pairs={{0,6},{1,7},{2,4},{3,5},{4,10},{5,11},{6,8},{7,9},{8,14},{9,15},{1... | collective-permute-start | bytes 786440 | tf_op jit(solution)/shard_map/ppermute | solution.py:96
  131.1 10.3 %collective-permute-start.33 = (bf16[64,2048]{1,0:T(8,128)(2,1)S(1)}, bf16[64,2048]{1,0:T(8,128)(2,1)S(1)}, u32[]{:S(2)}, u32[]{:S(2)}) collective-permute-start(bf16[64,2048]{1,0:T(8,128)(2,1)S(1)} %get-tuple-element.117), channel_id=1, source_target_pairs={{0,5},{1,4},{2,7},{3,6},{4,9},{5,8},{6,11},{7,10},{8,13},{9,12},{1... | collective-permute-start | bytes 786440 | tf_op jit(solution)/shard_map/ppermute | solution.py:96
  135.5 9.5 %collective-permute-start.42 = (bf16[64,2048]{1,0:T(8,128)(2,1)S(1)}, bf16[64,2048]{1,0:T(8,128)(2,1)S(1)}, u32[]{:S(2)}, u32[]{:S(2)}) collective-permute-start(bf16[64,2048]{1,0:T(8,128)(2,1)S(1)} %get-tuple-element.130), channel_id=1, source_target_pairs={{0,5},{1,4},{2,7},{3,6},{4,9},{5,8},{6,11},{7,10},{8,13},{9,12},{1... | collective-permute-start | bytes 786440 | tf_op jit(solution)/shard_map/ppermute | solution.py:96
  135.5 11.8 %collective-permute-start.38 = (bf16[64,2048]{1,0:T(8,128)(2,1)S(1)}, bf16[64,2048]{1,0:T(8,128)(2,1)S(1)}, u32[]{:S(2)}, u32[]{:S(2)}) collective-permute-start(bf16[64,2048]{1,0:T(8,128)(2,1)S(1)} %get-tuple-element.124), channel_id=1, source_target_pairs={{0,6},{1,7},{2,4},{3,5},{4,10},{5,11},{6,8},{7,9},{8,14},{9,15},{1... | collective-permute-start | bytes 786440 | tf_op jit(solution)/shard_map/ppermute | solution.py:96
  (12 other events, 105.0 us)

commit v5 on v4

--- a/solution.py
+++ b/solution.py
@@ -369,7 +369,7 @@
 
     def pass_sum(step, c):
         kept, got, mine, part = sums[c]
-        after = (kept,) if way(step, c) == "sums" and step == STEPS - 1 else ()
+        after = (kept,) if way(step, c) == "sums" and step == STEPS - 1 and c == 0 else ()
         both, state["mark"] = add_rows(mine, part, state["mark"], after)
         go = onward if way(step, c) == "sums" else across
         sums[c] = (kept, got, go(both, 3 - BACK[c]))

time: 149 us -> 148 us (level)
  waiting for transfers between devices: 86.7 us -> 74.7 us
  starting transfers between devices: 38.2 us -> 49.5 us
    ppermute x18, starting transfers between devices: 7.35 us -> 18.6 us  [onward(): return lax.ppermute(x, ('section', 'expert'), pairs)]
    ppermute x24, waiting for transfers between devices: 49.5 us -> 39.9 us  [across(): return lax.ppermute(x, 'expert', [(e, e ^ bits) for e in range(4)])]
    ppermute x18, waiting for transfers between devices: 35.6 us -> 33.2 us  [onward(): return lax.ppermute(x, ('section', 'expert'), pairs)]
  transfers between devices with their start and end apart: 43 -> 43, of which waited for: 27 -> 26; matrix products, arithmetic and copies ran while one was open for 0% -> 0% of each run, Pallas kernels for 14% -> 14%
where the time goes in v5:
time: 148 us
  waiting for transfers between devices  74.7 us (50%)
  starting transfers between devices  49.5 us (33%)
  Pallas kernels  23.4 us (16%)
    ppermute x24, waiting for transfers between devices, across(): return lax.ppermute(x, 'expert', [(e, e ^ bits) for e in range(4)])  39.9 us
    ppermute x18, waiting for transfers between devices, onward(): return lax.ppermute(x, ('section', 'expert'), pairs)  33.2 us
    ppermute x24, starting transfers between devices, across(): return lax.ppermute(x, 'expert', [(e, e ^ bits) for e in range(4)])  29.6 us
    pallas_call x18, Pallas kernels, call(): pl.pallas_call(lambda *refs: kernel(*refs[len(after):]), in_specs=specs,...  23.4 us
    ppermute x18, starting transfers between devices, onward(): return lax.ppermute(x, ('section', 'expert'), pairs)  18.6 us
  transfers between devices with their start and end apart: 43, of which 26 were waited for; matrix products, arithmetic and copies ran while one was open for 0% of the time, Pallas kernels for 14%

profile of v5, /device:TPU:0, one launch (start us, length us, event | category | flops | bytes accessed | tf_op | source)
XLA Modules:
  0.0 147.7 jit_solution(14003753886453121225)
XLA Ops:
  1.5 3.0 %collective-permute-start = (bf16[64,2176]{1,0:T(8,128)(2,1)S(1)}, bf16[64,2176]{1,0:T(8,128)(2,1)S(1)}, u32[]{:S(2)}, u32[]{:S(2)}) collective-permute-start(bf16[64,2176]{1,0:T(8,128)(2,1)S(1)} %get-tuple-element.69.refs_2_), channel_id=1, source_target_pairs={{0,1},{1,0},{2,3},{3,2},{4,5},{5,4},{6,7},{7,6},{8,9},{9,8},{10,11... | collective-permute-start | bytes 835592 | tf_op jit(solution)/shard_map/ppermute | solution.py:88
  6.5 4.6 %collective-permute-done.refs_3_ = bf16[64,2176]{1,0:T(8,128)(2,1)S(1)} collective-permute-done((bf16[64,2176]{1,0:T(8,128)(2,1)S(1)}, bf16[64,2176]{1,0:T(8,128)(2,1)S(1)}, u32[]{:S(2)}, u32[]{:S(2)}) %collective-permute-start) | collective-permute-done | bytes 278560 | tf_op jit(solution)/shard_map/ppermute | solution.py:88
  11.2 1.8 %collective-permute-start.2 = (bf16[64,2176]{1,0:T(8,128)(2,1)S(1)}, bf16[64,2176]{1,0:T(8,128)(2,1)S(1)}, u32[]{:S(2)}, u32[]{:S(2)}) collective-permute-start(bf16[64,2176]{1,0:T(8,128)(2,1)S(1)} %collective-permute-done.refs_3_), channel_id=1, source_target_pairs={{0,2},{1,3},{2,0},{3,1},{4,6},{5,7},{6,4},{7,5},{8,10},{9,11},{10,... | collective-permute-start | bytes 835592 | tf_op jit(solution)/shard_map/ppermute | solution.py:88
  17.9 2.2 %collective-permute-done.1.refs_4_ = bf16[64,2176]{1,0:T(8,128)(2,1)S(1)} collective-permute-done((bf16[64,2176]{1,0:T(8,128)(2,1)S(1)}, bf16[64,2176]{1,0:T(8,128)(2,1)S(1)}, u32[]{:S(2)}, u32[]{:S(2)}) %collective-permute-start.1) | collective-permute-done | bytes 278560 | tf_op jit(solution)/shard_map/ppermute | solution.py:88
  20.1 4.5 %collective-permute-done.2.refs_5_ = bf16[64,2176]{1,0:T(8,128)(2,1)S(1)} collective-permute-done((bf16[64,2176]{1,0:T(8,128)(2,1)S(1)}, bf16[64,2176]{1,0:T(8,128)(2,1)S(1)}, u32[]{:S(2)}, u32[]{:S(2)}) %collective-permute-start.2) | collective-permute-done | bytes 278560 | tf_op jit(solution)/shard_map/ppermute | solution.py:88
  24.6 5.4 %shard_map.74 = (f32[64,2048]{1,0:T(8,128)S(1)}, bf16[64,2048]{1,0:T(8,128)(2,1)S(1)}, bf16[64,2048]{1,0:T(8,128)(2,1)S(1)}, bf16[64,2048]{1,0:T(8,128)(2,1)S(1)...) custom-call(s32[1]{0:T(128)} %bitcast.refs_0_, ...), custom_call_target="tpu_custom_call" | custom-call | flops 2415919104 | bytes 2097152 | tf_op jit(solution)/shard_map/pallas_call | solution.py:112
  30.4 2.7 %shard_map.75 = (f32[64,2048]{1,0:T(8,128)S(1)}, bf16[64,2048]{1,0:T(8,128)(2,1)S(1)}, bf16[64,2048]{1,0:T(8,128)(2,1)S(1)}, bf16[64,2048]{1,0:T(8,128)(2,1)S(1)...) custom-call(s32[1]{0:T(128)} %bitcast.refs_0_, f32[64,2048]{1,0:T(8,128)S(1)} %get-tuple-element.75.refs_1_, ...), custom_call_target="tpu_custom_call" | custom-call | flops 2415919104 | bytes 2097152 | tf_op jit(solution)/shard_map/pallas_call | solution.py:112
  36.4 1.8 %collective-permute-done.5.refs_1_ = bf16[64,2048]{1,0:T(8,128)(2,1)S(1)} collective-permute-done((bf16[64,2048]{1,0:T(8,128)(2,1)S(1)}, bf16[64,2048]{1,0:T(8,128)(2,1)S(1)}, u32[]{:S(2)}, u32[]{:S(2)}) %collective-permute-start.5) | collective-permute-done | bytes 262176 | tf_op jit(solution)/shard_map/ppermute | solution.py:88
  38.3 2.5 %collective-permute-start.9 = (bf16[64,2048]{1,0:T(8,128)(2,1)S(1)}, bf16[64,2048]{1,0:T(8,128)(2,1)S(1)}, u32[]{:S(2)}, u32[]{:S(2)}) collective-permute-start(bf16[64,2048]{1,0:T(8,128)(2,1)S(1)} %get-tuple-element.82), channel_id=1, source_target_pairs={{0,2},{1,3},{2,0},{3,1},{4,6},{5,7},{6,4},{7,5},{8,10},{9,11},{10,... | collective-permute-start | bytes 786440 | tf_op jit(solution)/shard_map/ppermute | solution.py:88
  42.5 3.9 %collective-permute-done.9.refs_2_ = bf16[64,2048]{1,0:T(8,128)(2,1)S(1)} collective-permute-done((bf16[64,2048]{1,0:T(8,128)(2,1)S(1)}, bf16[64,2048]{1,0:T(8,128)(2,1)S(1)}, u32[]{:S(2)}, u32[]{:S(2)}) %collective-permute-start.9) | collective-permute-done | bytes 262176 | tf_op jit(solution)/shard_map/ppermute | solution.py:88
  46.7 4.7 %collective-permute-start.12 = (bf16[64,2048]{1,0:T(8,128)(2,1)S(1)}, bf16[64,2048]{1,0:T(8,128)(2,1)S(1)}, u32[]{:S(2)}, u32[]{:S(2)}) collective-permute-start(bf16[64,2048]{1,0:T(8,128)(2,1)S(1)} %get-tuple-element.88), channel_id=1, source_target_pairs={{0,5},{1,4},{2,7},{3,6},{4,9},{5,8},{6,11},{7,10},{8,13},{9,12},{1... | collective-permute-start | bytes 786440 | tf_op jit(solution)/shard_map/ppermute | solution.py:96
  53.8 7.4 %collective-permute-done.12.refs_2_ = bf16[64,2048]{1,0:T(8,128)(2,1)S(1)} collective-permute-done((bf16[64,2048]{1,0:T(8,128)(2,1)S(1)}, bf16[64,2048]{1,0:T(8,128)(2,1)S(1)}, u32[]{:S(2)}, u32[]{:S(2)}) %collective-permute-start.12) | collective-permute-done | bytes 262176 | tf_op jit(solution)/shard_map/ppermute | solution.py:96
  63.5 3.2 %collective-permute-done.13.refs_3_ = bf16[64,2048]{1,0:T(8,128)(2,1)S(1)} collective-permute-done((bf16[64,2048]{1,0:T(8,128)(2,1)S(1)}, bf16[64,2048]{1,0:T(8,128)(2,1)S(1)}, u32[]{:S(2)}, u32[]{:S(2)}) %collective-permute-start.13) | collective-permute-done | bytes 262176 | tf_op jit(solution)/shard_map/ppermute | solution.py:96
  66.7 5.2 %collective-permute-done.14.refs_4_ = bf16[64,2048]{1,0:T(8,128)(2,1)S(1)} collective-permute-done((bf16[64,2048]{1,0:T(8,128)(2,1)S(1)}, bf16[64,2048]{1,0:T(8,128)(2,1)S(1)}, u32[]{:S(2)}, u32[]{:S(2)}) %collective-permute-start.14) | collective-permute-done | bytes 262176 | tf_op jit(solution)/shard_map/ppermute | solution.py:88
  71.9 2.8 %shard_map.80 = (f32[64,2048]{1,0:T(8,128)S(1)}, bf16[64,2048]{1,0:T(8,128)(2,1)S(1)}, bf16[64,2048]{1,0:T(8,128)(2,1)S(1)}, bf16[64,2048]{1,0:T(8,128)(2,1)S(1)}, f32[8,128]{1,0:T(8,128)S(1)}) custom-call(f32[64,2048]{1,0:T(8,128)S(1)} %collective-permute-done.11.refs_0_, f32[1,2048]{1,0:T(1,128)S(1)} %copy-done, ...), custom_call_target="tpu_custom_call" | custom-call | flops 2415919104 | bytes 2097152 | tf_op jit(solution)/shard_map/pallas_call | solution.py:112
  75.4 2.7 %shard_map.81 = (f32[64,2048]{1,0:T(8,128)S(1)}, bf16[64,2048]{1,0:T(8,128)(2,1)S(1)}, bf16[64,2048]{1,0:T(8,128)(2,1)S(1)}, bf16[64,2048]{1,0:T(8,128)(2,1)S(1)}, f32[8,128]{1,0:T(8,128)S(1)}) custom-call(f32[64,2048]{1,0:T(8,128)S(1)} %get-tuple-element.99.refs_0_, bf16[64,2048]{1,0:T(8,128)(2,1)S(1)} %get-tuple-element.100.refs_1_, ...), custom_call_target="tpu_custom_call" | custom-call | flops 2415919104 | bytes 2097152 | tf_op jit(solution)/shard_map/pallas_call | solution.py:112
  80.5 2.1 %collective-permute-done.19.refs_1_ = bf16[64,2048]{1,0:T(8,128)(2,1)S(1)} collective-permute-done((bf16[64,2048]{1,0:T(8,128)(2,1)S(1)}, bf16[64,2048]{1,0:T(8,128)(2,1)S(1)}, u32[]{:S(2)}, u32[]{:S(2)}) %collective-permute-start.19) | collective-permute-done | bytes 262176 | tf_op jit(solution)/shard_map/ppermute | solution.py:88
  84.6 2.2 %collective-permute-start.31 = (bf16[64,2048]{1,0:T(8,128)(2,1)S(1)}, bf16[64,2048]{1,0:T(8,128)(2,1)S(1)}, u32[]{:S(2)}, u32[]{:S(2)}) collective-permute-start(bf16[64,2048]{1,0:T(8,128)(2,1)S(1)} %get-tuple-element.113), channel_id=1, source_target_pairs={{0,5},{1,4},{2,7},{3,6},{4,9},{5,8},{6,11},{7,10},{8,13},{9,12},{1... | collective-permute-start | bytes 786440 | tf_op jit(solution)/shard_map/ppermute | solution.py:96
  86.7 3.5 %collective-permute-done.23.refs_2_ = bf16[64,2048]{1,0:T(8,128)(2,1)S(1)} collective-permute-done((bf16[64,2048]{1,0:T(8,128)(2,1)S(1)}, bf16[64,2048]{1,0:T(8,128)(2,1)S(1)}, u32[]{:S(2)}, u32[]{:S(2)}) %collective-permute-start.23) | collective-permute-done | bytes 262176 | tf_op jit(solution)/shard_map/ppermute | solution.py:88
  90.5 5.1 %collective-permute-start.25 = (f32[64,2048]{1,0:T(8,128)S(1)}, f32[64,2048]{1,0:T(8,128)S(1)}, u32[]{:S(2)}, u32[]{:S(2)}) collective-permute-start(f32[64,2048]{1,0:T(8,128)S(1)} %get-tuple-element.109), channel_id=1, source_target_pairs={{0,4},{1,5},{2,6},{3,7},{4,8},{5,9},{6,10},{7,11},{8,12},{9,13},{1... | collective-permute-start | bytes 1572872 | tf_op jit(solution)/shard_map/ppermute | solution.py:96
  98.1 2.0 %collective-permute-done.26.refs_2_ = bf16[64,2048]{1,0:T(8,128)(2,1)S(1)} collective-permute-done((bf16[64,2048]{1,0:T(8,128)(2,1)S(1)}, bf16[64,2048]{1,0:T(8,128)(2,1)S(1)}, u32[]{:S(2)}, u32[]{:S(2)}) %collective-permute-start.26) | collective-permute-done | bytes 262176 | tf_op jit(solution)/shard_map/ppermute | solution.py:96
  102.3 2.2 %collective-permute-done.36.refs_3_ = bf16[64,2048]{1,0:T(8,128)(2,1)S(1)} collective-permute-done((bf16[64,2048]{1,0:T(8,128)(2,1)S(1)}, bf16[64,2048]{1,0:T(8,128)(2,1)S(1)}, u32[]{:S(2)}, u32[]{:S(2)}) %collective-permute-start.36) | collective-permute-done | bytes 262176 | tf_op jit(solution)/shard_map/ppermute | solution.py:88
  106.2 5.6 %collective-permute-done.27.refs_3_ = bf16[64,2048]{1,0:T(8,128)(2,1)S(1)} collective-permute-done((bf16[64,2048]{1,0:T(8,128)(2,1)S(1)}, bf16[64,2048]{1,0:T(8,128)(2,1)S(1)}, u32[]{:S(2)}, u32[]{:S(2)}) %collective-permute-start.27) | collective-permute-done | bytes 262176 | tf_op jit(solution)/shard_map/ppermute | solution.py:96
  111.8 3.9 %collective-permute-done.28.refs_4_ = bf16[64,2048]{1,0:T(8,128)(2,1)S(1)} collective-permute-done((bf16[64,2048]{1,0:T(8,128)(2,1)S(1)}, bf16[64,2048]{1,0:T(8,128)(2,1)S(1)}, u32[]{:S(2)}, u32[]{:S(2)}) %collective-permute-start.28) | collective-permute-done | bytes 262176 | tf_op jit(solution)/shard_map/ppermute | solution.py:88
  115.7 2.8 %shard_map.86 = (f32[64,2048]{1,0:T(8,128)S(1)}, bf16[64,2048]{1,0:T(8,128)(2,1)S(1)}, bf16[64,2048]{1,0:T(8,128)(2,1)S(1)}, bf16[64,2048]{1,0:T(8,128)(2,1)S(1)}, f32[8,128]{1,0:T(8,128)S(1)}) custom-call(f32[64,2048]{1,0:T(8,128)S(1)} %collective-permute-done.25.refs_0_, f32[1,2048]{1,0:T(1,128)S(1)} %copy-done, ...), custom_call_target="tpu_custom_call" | custom-call | flops 2415919104 | bytes 2097152 | tf_op jit(solution)/shard_map/pallas_call | solution.py:112
  119.9 2.7 %shard_map.87 = (f32[64,2048]{1,0:T(8,128)S(1)}, bf16[64,2048]{1,0:T(8,128)(2,1)S(1)}, bf16[64,2048]{1,0:T(8,128)(2,1)S(1)}, bf16[64,2048]{1,0:T(8,128)(2,1)S(1)}, f32[8,128]{1,0:T(8,128)S(1)}) custom-call(f32[64,2048]{1,0:T(8,128)S(1)} %get-tuple-element.120.refs_0_, bf16[64,2048]{1,0:T(8,128)(2,1)S(1)} %get-tuple-element.121.refs_1_, ...), custom_call_target="tpu_custom_call" | custom-call | flops 2415919104 | bytes 2097152 | tf_op jit(solution)/shard_map/pallas_call | solution.py:112
  125.6 1.9 %collective-permute-done.34.refs_2_ = bf16[64,2048]{1,0:T(8,128)(2,1)S(1)} collective-permute-done((bf16[64,2048]{1,0:T(8,128)(2,1)S(1)}, bf16[64,2048]{1,0:T(8,128)(2,1)S(1)}, u32[]{:S(2)}, u32[]{:S(2)}) %collective-permute-start.34) | collective-permute-done | bytes 262176 | tf_op jit(solution)/shard_map/ppermute | solution.py:88
  129.0 2.8 %collective-permute-done.41.refs_1_ = bf16[64,2048]{1,0:T(8,128)(2,1)S(1)} collective-permute-done((bf16[64,2048]{1,0:T(8,128)(2,1)S(1)}, bf16[64,2048]{1,0:T(8,128)(2,1)S(1)}, u32[]{:S(2)}, u32[]{:S(2)}) %collective-permute-start.41) | collective-permute-done | bytes 262176 | tf_op jit(solution)/shard_map/ppermute | solution.py:88
  134.5 3.8 %collective-permute-done.40.refs_4_ = bf16[64,2048]{1,0:T(8,128)(2,1)S(1)} collective-permute-done((bf16[64,2048]{1,0:T(8,128)(2,1)S(1)}, bf16[64,2048]{1,0:T(8,128)(2,1)S(1)}, u32[]{:S(2)}, u32[]{:S(2)}) %collective-permute-start.40) | collective-permute-done | bytes 262176 | tf_op jit(solution)/shard_map/ppermute | solution.py:96
  138.3 2.7 %collective-permute-done.33.refs_1_ = bf16[64,2048]{1,0:T(8,128)(2,1)S(1)} collective-permute-done((bf16[64,2048]{1,0:T(8,128)(2,1)S(1)}, bf16[64,2048]{1,0:T(8,128)(2,1)S(1)}, u32[]{:S(2)}, u32[]{:S(2)}) %collective-permute-start.33) | collective-permute-done | bytes 262176 | tf_op jit(solution)/shard_map/ppermute | solution.py:96
  141.0 2.8 %collective-permute-done.42.refs_5_ = bf16[64,2048]{1,0:T(8,128)(2,1)S(1)} collective-permute-done((bf16[64,2048]{1,0:T(8,128)(2,1)S(1)}, bf16[64,2048]{1,0:T(8,128)(2,1)S(1)}, u32[]{:S(2)}, u32[]{:S(2)}) %collective-permute-start.42) | collective-permute-done | bytes 262176 | tf_op jit(solution)/shard_map/ppermute | solution.py:96
  143.8 2.8 %collective-permute-done.38.refs_2_ = bf16[64,2048]{1,0:T(8,128)(2,1)S(1)} collective-permute-done((bf16[64,2048]{1,0:T(8,128)(2,1)S(1)}, bf16[64,2048]{1,0:T(8,128)(2,1)S(1)}, u32[]{:S(2)}, u32[]{:S(2)}) %collective-permute-start.38) | collective-permute-done | bytes 262176 | tf_op jit(solution)/shard_map/ppermute | solution.py:96
  (74 shorter events, 40.4 us)
Async XLA Ops:
  1.5 9.7 %collective-permute-start = (bf16[64,2176]{1,0:T(8,128)(2,1)S(1)}, bf16[64,2176]{1,0:T(8,128)(2,1)S(1)}, u32[]{:S(2)}, u32[]{:S(2)}) collective-permute-start(bf16[64,2176]{1,0:T(8,128)(2,1)S(1)} %get-tuple-element.69.refs_2_), channel_id=1, source_target_pairs={{0,1},{1,0},{2,3},{3,2},{4,5},{5,4},{6,7},{7,6},{8,9},{9,8},{10,11... | collective-permute-start | bytes 835592 | tf_op jit(solution)/shard_map/ppermute | solution.py:88
  4.5 9.9 %collective-permute-start.7 = (bf16[64,2176]{1,0:T(8,128)(2,1)S(1)}, bf16[64,2176]{1,0:T(8,128)(2,1)S(1)}, u32[]{:S(2)}, u32[]{:S(2)}) collective-permute-start(bf16[64,2176]{1,0:T(8,128)(2,1)S(1)} %get-tuple-element.76.refs_2_), channel_id=1, source_target_pairs={{0,2},{1,3},{2,0},{3,1},{4,6},{5,7},{6,4},{7,5},{8,10},{9,11},{10,... | collective-permute-start | bytes 835592 | tf_op jit(solution)/shard_map/ppermute | solution.py:88
  6.0 14.0 %collective-permute-start.1 = (bf16[64,2176]{1,0:T(8,128)(2,1)S(1)}, bf16[64,2176]{1,0:T(8,128)(2,1)S(1)}, u32[]{:S(2)}, u32[]{:S(2)}) collective-permute-start(bf16[64,2176]{1,0:T(8,128)(2,1)S(1)} %get-tuple-element.69.refs_2_), channel_id=1, source_target_pairs={{0,2},{1,3},{2,0},{3,1},{4,6},{5,7},{6,4},{7,5},{8,10},{9,11},{10,... | collective-permute-start | bytes 835592 | tf_op jit(solution)/shard_map/ppermute | solution.py:88
  11.2 13.4 %collective-permute-start.2 = (bf16[64,2176]{1,0:T(8,128)(2,1)S(1)}, bf16[64,2176]{1,0:T(8,128)(2,1)S(1)}, u32[]{:S(2)}, u32[]{:S(2)}) collective-permute-start(bf16[64,2176]{1,0:T(8,128)(2,1)S(1)} %collective-permute-done.refs_3_), channel_id=1, source_target_pairs={{0,2},{1,3},{2,0},{3,1},{4,6},{5,7},{6,4},{7,5},{8,10},{9,11},{10,... | collective-permute-start | bytes 835592 | tf_op jit(solution)/shard_map/ppermute | solution.py:88
  12.9 17.5 %collective-permute-start.6 = (bf16[64,2176]{1,0:T(8,128)(2,1)S(1)}, bf16[64,2176]{1,0:T(8,128)(2,1)S(1)}, u32[]{:S(2)}, u32[]{:S(2)}) collective-permute-start(bf16[64,2176]{1,0:T(8,128)(2,1)S(1)} %get-tuple-element.76.refs_2_), channel_id=1, source_target_pairs={{0,1},{1,0},{2,3},{3,2},{4,5},{5,4},{6,7},{7,6},{8,9},{9,8},{10,11... | collective-permute-start | bytes 835592 | tf_op jit(solution)/shard_map/ppermute | solution.py:88
  14.4 16.0 %collective-permute-start.8 = (bf16[64,2176]{1,0:T(8,128)(2,1)S(1)}, bf16[64,2176]{1,0:T(8,128)(2,1)S(1)}, u32[]{:S(2)}, u32[]{:S(2)}) collective-permute-start(bf16[64,2176]{1,0:T(8,128)(2,1)S(1)} %collective-permute-done.7.refs_4_), channel_id=1, source_target_pairs={{0,1},{1,0},{2,3},{3,2},{4,5},{5,4},{6,7},{7,6},{8,9},{9,8},{10,11... | collective-permute-start | bytes 835592 | tf_op jit(solution)/shard_map/ppermute | solution.py:88
  36.4 16.0 %collective-permute-start.15 = (f32[64,2048]{1,0:T(8,128)S(1)}, f32[64,2048]{1,0:T(8,128)S(1)}, u32[]{:S(2)}, u32[]{:S(2)}) collective-permute-start(f32[64,2048]{1,0:T(8,128)S(1)} %get-tuple-element.90), channel_id=1, source_target_pairs={{0,4},{1,5},{2,6},{3,7},{4,8},{5,9},{6,10},{7,11},{8,12},{9,13},{1... | collective-permute-start | bytes 1572872 | tf_op jit(solution)/shard_map/ppermute | solution.py:96
  40.8 10.6 %collective-permute-start.16 = (bf16[64,2048]{1,0:T(8,128)(2,1)S(1)}, bf16[64,2048]{1,0:T(8,128)(2,1)S(1)}, u32[]{:S(2)}, u32[]{:S(2)}) collective-permute-start(bf16[64,2048]{1,0:T(8,128)(2,1)S(1)} %get-tuple-element.91), channel_id=1, source_target_pairs={{0,6},{1,7},{2,4},{3,5},{4,10},{5,11},{6,8},{7,9},{8,14},{9,15},{1... | collective-permute-start | bytes 786440 | tf_op jit(solution)/shard_map/ppermute | solution.py:96
  40.9 11.5 %collective-permute-start.17 = (bf16[64,2048]{1,0:T(8,128)(2,1)S(1)}, bf16[64,2048]{1,0:T(8,128)(2,1)S(1)}, u32[]{:S(2)}, u32[]{:S(2)}) collective-permute-start(bf16[64,2048]{1,0:T(8,128)(2,1)S(1)} %get-tuple-element.92), channel_id=1, source_target_pairs={{0,5},{1,4},{2,7},{3,6},{4,9},{5,8},{6,11},{7,10},{8,13},{9,12},{1... | collective-permute-start | bytes 786440 | tf_op jit(solution)/shard_map/ppermute | solution.py:96
  46.6 20.1 %collective-permute-start.11 = (f32[64,2048]{1,0:T(8,128)S(1)}, f32[64,2048]{1,0:T(8,128)S(1)}, u32[]{:S(2)}, u32[]{:S(2)}) collective-permute-start(f32[64,2048]{1,0:T(8,128)S(1)} %get-tuple-element.87), channel_id=1, source_target_pairs={{0,4},{1,5},{2,6},{3,7},{4,8},{5,9},{6,10},{7,11},{8,12},{9,13},{1... | collective-permute-start | bytes 1572872 | tf_op jit(solution)/shard_map/ppermute | solution.py:96
  46.7 14.5 %collective-permute-start.12 = (bf16[64,2048]{1,0:T(8,128)(2,1)S(1)}, bf16[64,2048]{1,0:T(8,128)(2,1)S(1)}, u32[]{:S(2)}, u32[]{:S(2)}) collective-permute-start(bf16[64,2048]{1,0:T(8,128)(2,1)S(1)} %get-tuple-element.88), channel_id=1, source_target_pairs={{0,5},{1,4},{2,7},{3,6},{4,9},{5,8},{6,11},{7,10},{8,13},{9,12},{1... | collective-permute-start | bytes 786440 | tf_op jit(solution)/shard_map/ppermute | solution.py:96
  52.6 10.2 %collective-permute-start.21 = (bf16[64,2048]{1,0:T(8,128)(2,1)S(1)}, bf16[64,2048]{1,0:T(8,128)(2,1)S(1)}, u32[]{:S(2)}, u32[]{:S(2)}) collective-permute-start(bf16[64,2048]{1,0:T(8,128)(2,1)S(1)} %get-tuple-element.100.refs_1_), channel_id=1, source_target_pairs={{0,2},{1,3},{2,0},{3,1},{4,6},{5,7},{6,4},{7,5},{8,10},{9,11},{10,... | collective-permute-start | bytes 786440 | tf_op jit(solution)/shard_map/ppermute | solution.py:88
  53.3 13.5 %collective-permute-start.13 = (bf16[64,2048]{1,0:T(8,128)(2,1)S(1)}, bf16[64,2048]{1,0:T(8,128)(2,1)S(1)}, u32[]{:S(2)}, u32[]{:S(2)}) collective-permute-start(bf16[64,2048]{1,0:T(8,128)(2,1)S(1)} %get-tuple-element.88), channel_id=1, source_target_pairs={{0,6},{1,7},{2,4},{3,5},{4,10},{5,11},{6,8},{7,9},{8,14},{9,15},{1... | collective-permute-start | bytes 786440 | tf_op jit(solution)/shard_map/ppermute | solution.py:96
  61.2 10.7 %collective-permute-start.14 = (bf16[64,2048]{1,0:T(8,128)(2,1)S(1)}, bf16[64,2048]{1,0:T(8,128)(2,1)S(1)}, u32[]{:S(2)}, u32[]{:S(2)}) collective-permute-start(bf16[64,2048]{1,0:T(8,128)(2,1)S(1)} %collective-permute-done.12.refs_2_), channel_id=1, source_target_pairs={{0,2},{1,3},{2,0},{3,1},{4,6},{5,7},{6,4},{7,5},{8,10},{9,11},{10,... | collective-permute-start | bytes 786440 | tf_op jit(solution)/shard_map/ppermute | solution.py:88
  61.5 13.9 %collective-permute-start.20 = (bf16[64,2048]{1,0:T(8,128)(2,1)S(1)}, bf16[64,2048]{1,0:T(8,128)(2,1)S(1)}, u32[]{:S(2)}, u32[]{:S(2)}) collective-permute-start(bf16[64,2048]{1,0:T(8,128)(2,1)S(1)} %get-tuple-element.100.refs_1_), channel_id=1, source_target_pairs={{0,1},{1,0},{2,3},{3,2},{4,5},{5,4},{6,7},{7,6},{8,9},{9,8},{10,11... | collective-permute-start | bytes 786440 | tf_op jit(solution)/shard_map/ppermute | solution.py:88
  62.8 12.5 %collective-permute-start.22 = (bf16[64,2048]{1,0:T(8,128)(2,1)S(1)}, bf16[64,2048]{1,0:T(8,128)(2,1)S(1)}, u32[]{:S(2)}, u32[]{:S(2)}) collective-permute-start(bf16[64,2048]{1,0:T(8,128)(2,1)S(1)} %collective-permute-done.21.refs_3_), channel_id=1, source_target_pairs={{0,1},{1,0},{2,3},{3,2},{4,5},{5,4},{6,7},{7,6},{8,9},{9,8},{10,11... | collective-permute-start | bytes 786440 | tf_op jit(solution)/shard_map/ppermute | solution.py:88
  80.5 16.8 %collective-permute-start.29 = (f32[64,2048]{1,0:T(8,128)S(1)}, f32[64,2048]{1,0:T(8,128)S(1)}, u32[]{:S(2)}, u32[]{:S(2)}) collective-permute-start(f32[64,2048]{1,0:T(8,128)S(1)} %get-tuple-element.111), channel_id=1, source_target_pairs={{0,4},{1,5},{2,6},{3,7},{4,8},{5,9},{6,10},{7,11},{8,12},{9,13},{1... | collective-permute-start | bytes 1572872 | tf_op jit(solution)/shard_map/ppermute | solution.py:96
  84.3 11.3 %collective-permute-start.30 = (bf16[64,2048]{1,0:T(8,128)(2,1)S(1)}, bf16[64,2048]{1,0:T(8,128)(2,1)S(1)}, u32[]{:S(2)}, u32[]{:S(2)}) collective-permute-start(bf16[64,2048]{1,0:T(8,128)(2,1)S(1)} %get-tuple-element.112), channel_id=1, source_target_pairs={{0,6},{1,7},{2,4},{3,5},{4,10},{5,11},{6,8},{7,9},{8,14},{9,15},{1... | collective-permute-start | bytes 786440 | tf_op jit(solution)/shard_map/ppermute | solution.py:96
  84.6 12.7 %collective-permute-start.31 = (bf16[64,2048]{1,0:T(8,128)(2,1)S(1)}, bf16[64,2048]{1,0:T(8,128)(2,1)S(1)}, u32[]{:S(2)}, u32[]{:S(2)}) collective-permute-start(bf16[64,2048]{1,0:T(8,128)(2,1)S(1)} %get-tuple-element.113), channel_id=1, source_target_pairs={{0,5},{1,4},{2,7},{3,6},{4,9},{5,8},{6,11},{7,10},{8,13},{9,12},{1... | collective-permute-start | bytes 786440 | tf_op jit(solution)/shard_map/ppermute | solution.py:96
  90.5 9.6 %collective-permute-start.26 = (bf16[64,2048]{1,0:T(8,128)(2,1)S(1)}, bf16[64,2048]{1,0:T(8,128)(2,1)S(1)}, u32[]{:S(2)}, u32[]{:S(2)}) collective-permute-start(bf16[64,2048]{1,0:T(8,128)(2,1)S(1)} %get-tuple-element.110), channel_id=1, source_target_pairs={{0,5},{1,4},{2,7},{3,6},{4,9},{5,8},{6,11},{7,10},{8,13},{9,12},{1... | collective-permute-start | bytes 786440 | tf_op jit(solution)/shard_map/ppermute | solution.py:96
  90.5 25.2 %collective-permute-start.25 = (f32[64,2048]{1,0:T(8,128)S(1)}, f32[64,2048]{1,0:T(8,128)S(1)}, u32[]{:S(2)}, u32[]{:S(2)}) collective-permute-start(f32[64,2048]{1,0:T(8,128)S(1)} %get-tuple-element.109), channel_id=1, source_target_pairs={{0,4},{1,5},{2,6},{3,7},{4,8},{5,9},{6,10},{7,11},{8,12},{9,13},{1... | collective-permute-start | bytes 1572872 | tf_op jit(solution)/shard_map/ppermute | solution.py:96
  98.1 13.7 %collective-permute-start.27 = (bf16[64,2048]{1,0:T(8,128)(2,1)S(1)}, bf16[64,2048]{1,0:T(8,128)(2,1)S(1)}, u32[]{:S(2)}, u32[]{:S(2)}) collective-permute-start(bf16[64,2048]{1,0:T(8,128)(2,1)S(1)} %get-tuple-element.110), channel_id=1, source_target_pairs={{0,6},{1,7},{2,4},{3,5},{4,10},{5,11},{6,8},{7,9},{8,14},{9,15},{1... | collective-permute-start | bytes 786440 | tf_op jit(solution)/shard_map/ppermute | solution.py:96
  100.1 15.6 %collective-permute-start.28 = (bf16[64,2048]{1,0:T(8,128)(2,1)S(1)}, bf16[64,2048]{1,0:T(8,128)(2,1)S(1)}, u32[]{:S(2)}, u32[]{:S(2)}) collective-permute-start(bf16[64,2048]{1,0:T(8,128)(2,1)S(1)} %collective-permute-done.26.refs_2_), channel_id=1, source_target_pairs={{0,2},{1,3},{2,0},{3,1},{4,6},{5,7},{6,4},{7,5},{8,10},{9,11},{10,... | collective-permute-start | bytes 786440 | tf_op jit(solution)/shard_map/ppermute | solution.py:88
  101.4 18.5 %collective-permute-start.35 = (bf16[64,2048]{1,0:T(8,128)(2,1)S(1)}, bf16[64,2048]{1,0:T(8,128)(2,1)S(1)}, u32[]{:S(2)}, u32[]{:S(2)}) collective-permute-start(bf16[64,2048]{1,0:T(8,128)(2,1)S(1)} %get-tuple-element.121.refs_1_), channel_id=1, source_target_pairs={{0,1},{1,0},{2,3},{3,2},{4,5},{5,4},{6,7},{7,6},{8,9},{9,8},{10,11... | collective-permute-start | bytes 786440 | tf_op jit(solution)/shard_map/ppermute | solution.py:88
  104.5 15.4 %collective-permute-start.37 = (bf16[64,2048]{1,0:T(8,128)(2,1)S(1)}, bf16[64,2048]{1,0:T(8,128)(2,1)S(1)}, u32[]{:S(2)}, u32[]{:S(2)}) collective-permute-start(bf16[64,2048]{1,0:T(8,128)(2,1)S(1)} %collective-permute-done.36.refs_3_), channel_id=1, source_target_pairs={{0,1},{1,0},{2,3},{3,2},{4,5},{5,4},{6,7},{7,6},{8,9},{9,8},{10,11... | collective-permute-start | bytes 786440 | tf_op jit(solution)/shard_map/ppermute | solution.py:88
  118.5 10.5 %collective-permute-start.32 = (f32[64,2048]{1,0:T(8,128)S(1)}, f32[64,2048]{1,0:T(8,128)S(1)}, u32[]{:S(2)}, u32[]{:S(2)}) collective-permute-start(f32[64,2048]{1,0:T(8,128)S(1)} %get-tuple-element.116), channel_id=1, source_target_pairs={{0,4},{1,5},{2,6},{3,7},{4,8},{5,9},{6,10},{7,11},{8,12},{9,13},{1... | collective-permute-start | bytes 1572872 | tf_op jit(solution)/shard_map/ppermute | solution.py:96
  122.6 9.2 %collective-permute-start.41 = (bf16[64,2048]{1,0:T(8,128)(2,1)S(1)}, bf16[64,2048]{1,0:T(8,128)(2,1)S(1)}, u32[]{:S(2)}, u32[]{:S(2)}) collective-permute-start(bf16[64,2048]{1,0:T(8,128)(2,1)S(1)} %get-tuple-element.128), channel_id=1, source_target_pairs={{0,2},{1,3},{2,0},{3,1},{4,6},{5,7},{6,4},{7,5},{8,10},{9,11},{10,... | collective-permute-start | bytes 786440 | tf_op jit(solution)/shard_map/ppermute | solution.py:88
  123.6 17.3 %collective-permute-start.39 = (f32[64,2048]{1,0:T(8,128)S(1)}, f32[64,2048]{1,0:T(8,128)S(1)}, u32[]{:S(2)}, u32[]{:S(2)}) collective-permute-start(f32[64,2048]{1,0:T(8,128)S(1)} %get-tuple-element.125), channel_id=1, source_target_pairs={{0,4},{1,5},{2,6},{3,7},{4,8},{5,9},{6,10},{7,11},{8,12},{9,13},{1... | collective-permute-start | bytes 1572872 | tf_op jit(solution)/shard_map/ppermute | solution.py:96
  124.1 14.2 %collective-permute-start.40 = (bf16[64,2048]{1,0:T(8,128)(2,1)S(1)}, bf16[64,2048]{1,0:T(8,128)(2,1)S(1)}, u32[]{:S(2)}, u32[]{:S(2)}) collective-permute-start(bf16[64,2048]{1,0:T(8,128)(2,1)S(1)} %get-tuple-element.126), channel_id=1, source_target_pairs={{0,6},{1,7},{2,4},{3,5},{4,10},{5,11},{6,8},{7,9},{8,14},{9,15},{1... | collective-permute-start | bytes 786440 | tf_op jit(solution)/shard_map/ppermute | solution.py:96
  127.4 13.5 %collective-permute-start.33 = (bf16[64,2048]{1,0:T(8,128)(2,1)S(1)}, bf16[64,2048]{1,0:T(8,128)(2,1)S(1)}, u32[]{:S(2)}, u32[]{:S(2)}) collective-permute-start(bf16[64,2048]{1,0:T(8,128)(2,1)S(1)} %get-tuple-element.117), channel_id=1, source_target_pairs={{0,5},{1,4},{2,7},{3,6},{4,9},{5,8},{6,11},{7,10},{8,13},{9,12},{1... | collective-permute-start | bytes 786440 | tf_op jit(solution)/shard_map/ppermute | solution.py:96
  132.4 11.4 %collective-permute-start.42 = (bf16[64,2048]{1,0:T(8,128)(2,1)S(1)}, bf16[64,2048]{1,0:T(8,128)(2,1)S(1)}, u32[]{:S(2)}, u32[]{:S(2)}) collective-permute-start(bf16[64,2048]{1,0:T(8,128)(2,1)S(1)} %get-tuple-element.130), channel_id=1, source_target_pairs={{0,5},{1,4},{2,7},{3,6},{4,9},{5,8},{6,11},{7,10},{8,13},{9,12},{1... | collective-permute-start | bytes 786440 | tf_op jit(solution)/shard_map/ppermute | solution.py:96
  133.1 13.5 %collective-permute-start.38 = (bf16[64,2048]{1,0:T(8,128)(2,1)S(1)}, bf16[64,2048]{1,0:T(8,128)(2,1)S(1)}, u32[]{:S(2)}, u32[]{:S(2)}) collective-permute-start(bf16[64,2048]{1,0:T(8,128)(2,1)S(1)} %get-tuple-element.124), channel_id=1, source_target_pairs={{0,6},{1,7},{2,4},{3,5},{4,10},{5,11},{6,8},{7,9},{8,14},{9,15},{1... | collective-permute-start | bytes 786440 | tf_op jit(solution)/shard_map/ppermute | solution.py:96
  (12 other events, 101.5 us)
